TPU v7x, 32 devices: a whole 2x2x4 slice. The times are simulated.
32 devices in a mesh: section: 8 (over z, y), dp: 4 (over x, core).
Axes of the slice: x: 2, y: 2, z: 4, core: 2. Of those that a mesh axis runs over, the one named last changes fastest.
Arguments:
- checkpoints: bfloat16 [8, 3, 64, 1024], P('section', None, None, 'dp'), may hold values from -6 to 6
- gain: float32 [8, 1024], P('section'), may hold values from 0.25 to 1.75
- w_in: bfloat16 [8, 1024, 8192], P('section', None, 'dp'), may hold values from -0.09375 to 0.09375
- w_out: bfloat16 [8, 8192, 1024], P('section', 'dp'), may hold values from -0.0625 to 0.0625
- cotangent: bfloat16 [3, 64, 4096], P(None, None, 'dp'), may hold values from -6 to 6
Outputs:
- grad_in: bfloat16 [8, 1024, 8192], P('section', None, 'dp')
- grad_out: bfloat16 [8, 8192, 1024], P('section', 'dp')
- grad_gain: float32 [8, 1024], P('section', 'dp')
- section_grads: bfloat16 [8, 3, 64, 1024], P('section', None, None, 'dp')
All inputs are finite; a program needn't handle non-finite values.
Results may differ from a plain program's by a relative error of at most 0.04.
Values may be sent and summed in bfloat16 or wider, within the bound.
No kernel may reach another device: no remote copies, remote signals or barrier semaphores. Data moves between devices by JAX's collectives and lax.ppermute only.
A program may use at most 64 MiB of HBM per device.

v0:
```python
import functools

import jax
import jax.numpy as jnp
from jax import lax
from jax.experimental import pallas as pl
from jax.experimental.pallas import tpu as pltpu
from jax.sharding import PartitionSpec as P

F32 = jnp.float32
BF16 = jnp.bfloat16


def flip(block, axis, bits):
    count = lax.axis_size(axis)
    return lax.ppermute(block, axis, [(i, i ^ bits) for i in range(count)])


def side_rows(values, width):
    lead = values.astype(BF16)
    trail = (values - lead.astype(F32)).astype(BF16)
    flat = jnp.concatenate([lead, trail])
    return jnp.pad(flat, (0, 16 * width - flat.shape[0])).reshape(16, width)


def side_values(rows, count):
    flat = rows.reshape(-1)
    return flat[:count].astype(F32) + flat[count:2 * count].astype(F32)


def gelu_tanh(value):
    return jax.nn.gelu(value, approximate=True)


def shards_of_any(checkpoints, gain, w_in, w_out, cotangent):
    sections = lax.axis_size("section")
    n_dp = lax.axis_size("dp")
    here = lax.axis_index("section")
    lane = lax.axis_index("dp")
    layers = sections // 4
    mine = here % 4
    last = here // 4 == layers - 1
    _, micro, tok, share = checkpoints.shape
    rows = micro * tok
    quarter = share * n_dp
    width = 4 * quarter
    gain_row = gain[0]
    weight_in = w_in[0]
    weight_out = w_out[0]
    hidden = weight_in.shape[1]
    piece = hidden // 4
    core = lane % 2

    def gather_dp(block):
        bit = n_dp // 2
        parts = {0: block}
        while bit >= 1:
            other = flip(jnp.concatenate([parts[j] for j in parts], axis=1), "dp", bit)
            for at, j in enumerate(list(parts)):
                parts[j ^ bit] = other[:, at * block.shape[1]:(at + 1) * block.shape[1]]
            bit //= 2
        full = jnp.zeros((rows, quarter), block.dtype)
        for j, part in parts.items():
            full = lax.dynamic_update_slice(full, part, (0, (lane ^ j) * block.shape[1]))
        return full

    def cot_quarter(block):
        if n_dp < 4:
            whole = lax.all_gather(block, "dp", axis=1, tiled=True)
            return lax.dynamic_slice_in_dim(whole, mine * quarter, quarter, 1)
        per = n_dp // 4
        top = [s * n_dp + d for s in range(sections) for d in range(n_dp) if s // 4 == layers - 1]
        held = block
        far = lambda i, b: (i % n_dp // per ^ i // n_dp % 4) & b
        got = lax.ppermute(held, ("section", "dp"), [(i, i ^ 2 * per) for i in top if far(i, 3) == 0])
        held = jnp.where((lane // per ^ mine) & 2 == 0, held, got)
        got = lax.ppermute(held, ("section", "dp"), [(i, i ^ per) for i in top if far(i, 1) == 0])
        held = jnp.where((lane // per ^ mine) & 1 == 0, held, got)
        if per == 1:
            return held
        parts = {0: held}
        bit = per // 2
        while bit >= 1:
            for j in list(parts):
                parts[j ^ bit] = flip(parts[j], "dp", bit)
            bit //= 2
        full = jnp.zeros((rows, quarter), block.dtype)
        for j, part in parts.items():
            full = lax.dynamic_update_slice(full, part, (0, (lane % per ^ j) * block.shape[1]))
        return full

    def cut(values, j):
        return lax.dynamic_slice_in_dim(values, (mine ^ j) * piece, piece, 1)

    def fill(parts):
        full = jnp.zeros((rows, hidden), parts[0].dtype)
        for j, part in enumerate(parts):
            full = lax.dynamic_update_slice(full, part, (0, (mine ^ j) * piece))
        return full

    x_full = gather_dp(checkpoints[0].reshape(rows, share))
    cot = cot_quarter(cotangent.reshape(rows, cotangent.shape[2]))
    x_wide = x_full.astype(F32)
    scaled_raw = (x_wide * gain_row).astype(BF16)
    squares = jnp.sum(x_wide * x_wide, axis=1)

    act_raw = jnp.dot(scaled_raw, weight_in, preferred_element_type=F32)
    extra = side_rows(squares, piece)
    act = cut(act_raw, 0)
    for j in (3, 1, 2):
        got = flip(jnp.concatenate([cut(act_raw, j).astype(BF16), extra], axis=0), "section", j)
        act = act + got[:rows].astype(F32)
        squares = squares + side_values(got[rows:], rows)
    scale = lax.rsqrt(squares / width + 1e-06)[:, None]
    act = act * scale
    hid, pull = jax.vjp(gelu_tanh, act)
    hid = hid.astype(BF16)
    hid_full = fill([hid] + [flip(hid, "section", j) for j in (1, 2, 3)])
    normed = x_wide * scale
    scaled = (normed * gain_row).astype(BF16)

    def halves(values, side):
        pairs = values.reshape(rows, n_dp // 2, 2, share)
        return jnp.where(side == 0, pairs[:, :, 0], pairs[:, :, 1]).reshape(rows, quarter // 2)

    def own(values):
        return lax.dynamic_slice_in_dim(values, lane // 2 * share, share, 1)

    incoming = jnp.zeros((rows, quarter), BF16)
    normed_half = halves(normed, core)
    gain_half = halves(jnp.broadcast_to(gain_row, (rows, quarter)), core)
    for phase in range(layers):
        final = phase == layers - 1
        dy = jnp.where(last, cot, incoming) if phase > 0 else cot
        dhid_raw = jnp.dot(dy, weight_out.T, preferred_element_type=F32)
        dhid = cut(dhid_raw, 0)
        for j in (3, 1, 2):
            dhid = dhid + flip(cut(dhid_raw, j).astype(BF16), "section", j).astype(F32)
        dact = pull(dhid)[0].astype(BF16)
        inner = jnp.sum(dact.astype(F32) * act, axis=1)
        payload = jnp.concatenate([dact, side_rows(inner, piece)], axis=0)
        others = [flip(payload, "section", j) for j in (1, 2, 3)]
        for got in others:
            inner = inner + side_values(got[rows:], rows)
        dact_full = fill([dact] + [got[:rows] for got in others])
        part = jnp.dot(dact_full, weight_in.T, preferred_element_type=F32).astype(BF16)

        send = jnp.concatenate([halves(part, 1 - core), side_rows(inner, quarter // 2)], axis=0)
        got = flip(send, "dp", 1)
        dscaled = halves(part, core).astype(F32) + got[:rows].astype(F32)
        inner = inner + side_values(got[rows:], rows)
        bit = 2
        while bit < n_dp:
            send = jnp.concatenate([dscaled.astype(BF16), side_rows(inner, quarter // 2)], axis=0)
            got = flip(send, "dp", bit)
            dscaled = dscaled + got[:rows].astype(F32)
            inner = inner + side_values(got[rows:], rows)
            bit *= 2
        dnorm = dscaled * gain_half
        dy_half = halves(dy, core).astype(F32)
        grad_x = (dy_half + scale * (dnorm - normed_half * (inner / width)[:, None])).astype(BF16)
        if not final:
            down = lax.ppermute(grad_x, "section", [(i, i - 4) for i in range(4, sections)])
            other = flip(down, "dp", 1)
            pairs = jnp.where(
                core == 0,
                jnp.stack([down.reshape(rows, n_dp // 2, share), other.reshape(rows, n_dp // 2, share)], axis=2),
                jnp.stack([other.reshape(rows, n_dp // 2, share), down.reshape(rows, n_dp // 2, share)], axis=2),
            )
            incoming = pairs.reshape(rows, quarter)

    grad_out = jnp.dot(hid_full.T, dy, preferred_element_type=F32).astype(BF16)
    grad_in = jnp.dot(scaled.T, dact_full, preferred_element_type=F32).astype(BF16)
    grad_gain = jnp.sum(own(dscaled) * own(normed_half), axis=0)
    return (
        grad_in[None],
        grad_out[None],
        grad_gain[None],
        own(grad_x).reshape(1, micro, tok, share),
    )


SIDE = 16
GELU_IN = 0.7978845608028654
GELU_CUBE = 0.044715


def resident(shape, dtype):
    return pltpu.VMEM(shape, dtype)


def local(body, outs, *args, scratch=(), flops=0):
    spec = pl.BlockSpec(memory_space=pltpu.VMEM)
    moved = sum(a.size * a.dtype.itemsize for a in args)
    return pl.pallas_call(
        body,
        out_shape=tuple(outs),
        in_specs=[spec] * len(args),
        out_specs=tuple(spec for _ in outs),
        scratch_shapes=list(scratch),
        compiler_params=pltpu.CompilerParams(vmem_limit_bytes=16 * 1024 * 1024),
        cost_estimate=pl.CostEstimate(flops=flops, bytes_accessed=moved, transcendentals=0),
    )(*args)


def diagonal(rows, width):
    return lax.broadcasted_iota(jnp.int32, (rows, width), 0) == lax.broadcasted_iota(jnp.int32, (rows, width), 1)


def as_row(column, width):
    rows = column.shape[0]
    return jnp.sum(jnp.where(diagonal(rows, width), column, 0.0), axis=0, keepdims=True)


def as_column(row, rows):
    return jnp.sum(jnp.where(diagonal(rows, row.shape[1]), row, 0.0), axis=1, keepdims=True)


def side_block(row):
    lead = row.astype(BF16).astype(F32)
    at = lax.broadcasted_iota(jnp.int32, (SIDE, row.shape[1]), 0)
    return jnp.where(at == 0, lead, jnp.where(at == 1, row - lead, 0.0)).astype(BF16)


def side_row(block):
    wide = block.astype(F32)
    return wide[0:1] + wide[1:2]


def load_kernel(*refs):
    count = len(refs) // 2
    copies = [pltpu.make_async_copy(refs[i], refs[count + i], refs[-1].at[i]) for i in range(count)]
    for copy in copies:
        copy.start()
    for copy in copies:
        copy.wait()


def load(*arrays):
    return pl.pallas_call(
        load_kernel,
        out_shape=tuple(resident(a.shape, a.dtype) for a in arrays),
        in_specs=[pl.BlockSpec(memory_space=pl.ANY)] * len(arrays),
        out_specs=tuple(pl.BlockSpec(memory_space=pltpu.VMEM) for _ in arrays),
        scratch_shapes=[pltpu.SemaphoreType.DMA((len(arrays),))],
        compiler_params=pltpu.CompilerParams(vmem_limit_bytes=1024 * 1024),
        cost_estimate=pl.CostEstimate(flops=0, bytes_accessed=sum(2 * a.size * a.dtype.itemsize for a in arrays), transcendentals=0),
    )(*(pltpu.with_memory_space_constraint(a, pltpu.HBM) for a in arrays))


def place():
    return lax.axis_index("section") % 4, lax.axis_index("dp")


def dot_nt(left, right):
    return lax.dot_general(left, right, (((1,), (1,)), ((), ())), preferred_element_type=F32)


def dot_tn(left, right):
    return lax.dot_general(left, right, (((0,), (0,)), ((), ())), preferred_element_type=F32)


def slot(index, size):
    return pl.ds(pl.multiple_of(index * size, size), size)


def spread_in_part(part, at, gain, weight, mine, total, begin):
    share = part.shape[1]
    piece = weight.shape[1] // 4
    scaled = (part[...].astype(F32) * gain[:, slot(at, share)]).astype(BF16)
    for d in (3, 2, 1, 0):
        block = jnp.dot(scaled, weight[slot(at, share), slot(mine ^ d, piece)], preferred_element_type=F32)
        columns = slice(d * piece, (d + 1) * piece)
        total[:, columns] = block if begin else total[:, columns] + block


def square_sum(part):
    wide = part[...].astype(F32)
    return jnp.sum(wide * wide, axis=1, keepdims=True)


def spread_in_first_kernel(x0, x1, gain, weight, total):
    mine, lane = place()
    spread_in_part(x0, lane, gain, weight, mine, total, True)
    spread_in_part(x1, lane ^ 1, gain, weight, mine, total, False)


def spread_in_last_kernel(x0, x1, x2, x3, gain, weight, before, own, s1, s2, s3, x_full, total):
    mine, lane = place()
    rows, share = x0.shape
    piece = own.shape[1]
    total[...] = before[...]
    spread_in_part(x2, lane ^ 2, gain, weight, mine, total, False)
    spread_in_part(x3, lane ^ 3, gain, weight, mine, total, False)
    row = as_row(square_sum(x0) + square_sum(x1) + square_sum(x2) + square_sum(x3), piece)
    block = side_block(row)
    for d, out in ((3, s3), (2, s2), (1, s1)):
        out[:rows] = total[:, d * piece:(d + 1) * piece].astype(BF16)
        out[rows:] = block
    own[:rows] = total[:, :piece]
    own[rows:] = jnp.broadcast_to(row, (SIDE, piece))
    for d, part in enumerate((x0, x1, x2, x3)):
        x_full[:, slot(lane ^ d, share)] = part[...]


def spread_dy(dy, weight, mine, own, s1, s2, s3):
    piece = own.shape[1]
    for d, out in ((3, s3), (2, s2), (1, s1)):
        out[...] = dot_nt(dy[...], weight[slot(mine ^ d, piece), :]).astype(BF16)
    own[...] = dot_nt(dy[...], weight[slot(mine, piece), :])


def spread_first_kernel(cot, sent, weight, own, s1, s2, s3, dy):
    mine, lane = place()

    @pl.when(lane == mine)
    def _():
        dy[...] = cot[...]

    @pl.when(lane != mine)
    def _():
        dy[...] = sent[...]

    spread_dy(dy, weight, mine, own, s1, s2, s3)


def spread_next_kernel(layers, ds, begin, end, *refs):
    parts, refs = refs[:len(ds)], refs[len(ds):]
    before, weight = refs[:2]
    refs = refs[2:]
    mine, lane = place()
    rows, share = parts[0].shape
    piece = weight.shape[0] // 4
    last = lax.axis_index("section") // 4 == layers - 1
    if begin:
        (total,) = refs
    elif end:
        earlier, *others, own, s1, s2, s3, dy, total = refs
        total[...] = earlier[...]
    else:
        earlier, total = refs
        total[...] = earlier[...]
    for i, (d, part) in enumerate(zip(ds, parts)):
        at = slot(lane ^ d, share)
        value = jnp.where(last, before[:, at], part[...])
        for j in (3, 2, 1, 0):
            block = dot_nt(value, weight[slot(mine ^ j, piece), at])
            columns = slice(j * piece, (j + 1) * piece)
            total[:, columns] = block if begin and i == 0 else total[:, columns] + block
    if end:
        for j, out in ((3, s3), (2, s2), (1, s1)):
            out[...] = total[:, j * piece:(j + 1) * piece].astype(BF16)
        own[...] = total[:, :piece]
        done = [d for d in range(4) if d not in ds]

        @pl.when(last)
        def _():
            dy[...] = before[...]

        @pl.when(jnp.logical_not(last))
        def _():
            for d, part in zip((*done, *ds), (*others, *parts)):
                dy[:, slot(lane ^ d, share)] = part[...]


def act_kernel(width, own, g1, g2, g3, act, slope, hid, scale):
    rows = act.shape[0]
    row = own[rows:rows + 1] + side_row(g1[rows:]) + side_row(g2[rows:]) + side_row(g3[rows:])
    r = lax.rsqrt(as_column(row, rows) / width + 1e-06)
    scale[...] = r
    a = (own[:rows] + g1[:rows].astype(F32) + g2[:rows].astype(F32) + g3[:rows].astype(F32)) * r
    act[...] = a
    square = a * a
    t = jnp.tanh(GELU_IN * (a + GELU_CUBE * (square * a)))
    half = 0.5 * (1.0 + t)
    hid[...] = (a * half).astype(BF16)
    slope[...] = half + 0.5 * a * (1.0 - t * t) * (GELU_IN * (1.0 + 3.0 * GELU_CUBE * square))


def dact_kernel(own, g1, g2, g3, act, slope, pay):
    rows, piece = own.shape
    dhid = own[...] + g1[...].astype(F32) + g2[...].astype(F32) + g3[...].astype(F32)
    da = (dhid * slope[...]).astype(BF16)
    pay[:rows] = da
    pay[rows:] = side_block(as_row(jnp.sum(da.astype(F32) * act[...], axis=1, keepdims=True), piece))


def back_part(part, j, weight, mine, lane, total, begin):
    rows = total.shape[0]
    piece = part.shape[1]
    share = weight.shape[0] // 4
    for d in (1, 3, 0, 2):
        block = dot_nt(part[:rows], weight[slot(lane ^ d, share), slot(mine ^ j, piece)])
        columns = slice(d * share, (d + 1) * share)
        total[:, columns] = block if begin else total[:, columns] + block


def back_kernel(js, begin, *refs):
    *parts, weight = refs[:len(js) + 1]
    *earlier, total = refs[len(js) + 1:]
    mine, lane = place()
    if not begin:
        total[...] = earlier[0][...]
    for i, (j, part) in enumerate(zip(js, parts)):
        back_part(part, j, weight, mine, lane, total, begin and i == 0)


def back_last_kernel(p0, p1, p2, p3, weight, earlier, keep, send, total):
    mine, lane = place()
    rows = total.shape[0]
    share = weight.shape[0] // 4
    total[...] = earlier[...]
    back_part(p1, 1, weight, mine, lane, total, False)
    row = side_row(p0[rows:]) + side_row(p1[rows:]) + side_row(p2[rows:]) + side_row(p3[rows:])
    for at, d in ((0, 1), (1, 3)):
        send[:rows, at * share:(at + 1) * share] = total[:, d * share:(d + 1) * share].astype(BF16)
    send[rows:] = side_block(row)
    for at, d in ((0, 0), (1, 2)):
        keep[:rows, at * share:(at + 1) * share] = total[:, d * share:(d + 1) * share]
    keep[rows:] = jnp.broadcast_to(row, (SIDE, keep.shape[1]))


def middle_kernel(keep, got, rest, send):
    rows = keep.shape[0] - SIDE
    share = rest.shape[1]
    row = (keep[rows:rows + 1] + side_row(got[rows:]))[:, :share]
    send[:rows] = (keep[:rows, share:] + got[:rows, share:].astype(F32)).astype(BF16)
    send[rows:] = side_block(row)
    rest[:rows] = keep[:rows, :share] + got[:rows, :share].astype(F32)
    rest[rows:] = jnp.broadcast_to(row, (SIDE, share))


def finish_kernel(width, rest, got, x_own, dy, gain, scale, grad_x, *grad_gain):
    _, lane = place()
    rows, share = x_own.shape
    at = slot(lane, share)
    r = scale[...]
    du = rest[:rows] + got[:rows].astype(F32)
    normed = x_own[...].astype(F32) * r
    inner = as_column(rest[rows:rows + 1] + side_row(got[rows:]), rows) / width
    dnorm = du * gain[:, at]
    grad_x[...] = (dy[:, at].astype(F32) + r * (dnorm - normed * inner)).astype(BF16)
    if grad_gain:
        grad_gain[0][...] = jnp.sum(du * normed, axis=0, keepdims=True)


def grad_out_kernel(h0, h1, h2, h3, dy, out, held, sems):
    mine, _ = place()
    piece = h0.shape[1]
    copies = []
    for d, part in enumerate((h0, h1, h2, h3)):
        held[d] = dot_tn(part[...], dy[...]).astype(BF16)
        copies.append(pltpu.make_async_copy(held.at[d], out.at[slot(mine ^ d, piece), :], sems.at[d]))
        copies[-1].start()
    for copy in copies:
        copy.wait()


def grad_in_kernel(p0, p1, p2, p3, x_full, gain, scale, out, scaled, held, sems):
    mine, _ = place()
    rows = x_full.shape[0]
    piece = p0.shape[1]
    scaled[...] = (x_full[...].astype(F32) * scale[...] * gain[...]).astype(BF16)
    copies = []
    for d, part in enumerate((p0, p1, p2, p3)):
        held[d] = dot_tn(scaled[...], part[:rows]).astype(BF16)
        copies.append(pltpu.make_async_copy(held.at[d], out.at[:, slot(mine ^ d, piece)], sems.at[d]))
        copies[-1].start()
    for copy in copies:
        copy.wait()


def gradient(body, shape, block, *args, scratch=(), flops=0):
    return pl.pallas_call(
        body,
        out_shape=jax.ShapeDtypeStruct(shape, BF16),
        in_specs=[pl.BlockSpec(memory_space=pltpu.VMEM)] * len(args),
        out_specs=pl.BlockSpec(memory_space=pl.ANY),
        scratch_shapes=[*scratch, pltpu.VMEM((4,) + block, BF16), pltpu.SemaphoreType.DMA((4,))],
        compiler_params=pltpu.CompilerParams(vmem_limit_bytes=16 * 1024 * 1024),
        cost_estimate=pl.CostEstimate(flops=flops, bytes_accessed=2 * shape[0] * shape[1], transcendentals=0),
    )(*args)


def shards_of_four(checkpoints, gain, w_in, w_out, cotangent):
    sections = lax.axis_size("section")
    here = lax.axis_index("section")
    lane = lax.axis_index("dp")
    layers = sections // 4
    mine = here % 4
    _, micro, tok, share = checkpoints.shape
    rows = micro * tok
    quarter = share * 4
    width = 4 * quarter
    hidden = w_in.shape[2]
    piece = hidden // 4
    work = 2 * rows * quarter * hidden

    x0 = checkpoints[0].reshape(rows, share)
    cot = cotangent.reshape(rows, quarter)
    top = [s * 4 + d for s in range(sections) for d in range(4) if s // 4 == layers - 1]
    x2 = flip(x0, "dp", 2)
    x1 = flip(x0, "dp", 1)
    weight_in, x0, gain = load(w_in[0], x0, gain)
    x2, x1, weight_in = lax.optimization_barrier((x2, x1, weight_in))
    sent = lax.ppermute(cot, ("section", "dp"), [((i // 4 ^ near) * 4 + i // 4 % 4, i) for i in top for near in (1, 0, 2) if i // 4 % 4 ^ i % 4 == (2, 1, 3)[near]])
    x3 = flip(x2, "dp", 1)

    wide = (rows + SIDE, piece)
    (begun,) = local(spread_in_first_kernel, [resident((rows, hidden), F32)], x0, x1, gain, weight_in, flops=work)
    own, s1, s2, s3, x_full = local(
        spread_in_last_kernel,
        [resident(wide, F32)] + [resident(wide, BF16)] * 3 + [resident((rows, quarter), BF16)],
        x0, x1, x2, x3, gain, weight_in, begun,
        scratch=[pltpu.VMEM((rows, hidden), F32)], flops=work,
    )
    s1, s2, s3, cot, w_out = lax.optimization_barrier((s1, s2, s3, cot, w_out))
    g3 = flip(s3, "section", 3)
    g2 = flip(s2, "section", 2)
    g1 = flip(s1, "section", 1)
    weight_out, cot = load(w_out[0], cot)
    act, slope, hid, scale = local(
        functools.partial(act_kernel, width),
        [resident((rows, piece), F32), resident((rows, piece), F32), resident((rows, piece), BF16), resident((rows, 1), F32)],
        own, g3, g2, g1,
    )

    spread_outs = [resident((rows, piece), F32)] + [resident((rows, piece), BF16)] * 3 + [resident((rows, quarter), BF16)]

    def gather_hidden(block):
        return [block] + [flip(block, "section", j) for j in (1, 2, 3)]

    if layers == 1:
        hids = gather_hidden(hid)
    for phase in range(layers):
        final = phase == layers - 1
        if phase == 0:
            own, s1, s2, s3, dy = local(spread_first_kernel, spread_outs, cot, sent, weight_out, flops=work)
        else:
            d0, d1, d2, d3 = down
            first, hids = lax.optimization_barrier((d0, hids))
            total = [resident((rows, hidden), F32)]
            step = functools.partial(spread_next_kernel, layers)
            begun = local(functools.partial(step, (0,), True, False), total, first, dy, weight_out, flops=work // 4)
            begun = local(functools.partial(step, (1, 2), False, False), total, d1, d2, dy, weight_out, *begun, flops=work // 2)
            own, s1, s2, s3, dy = local(
                functools.partial(step, (3,), False, True), spread_outs, d3, dy, weight_out, *begun, d0, d1, d2,
                scratch=[pltpu.VMEM((rows, hidden), F32)], flops=work // 4,
            )
        g3 = flip(s3, "section", 3)
        g2 = flip(s2, "section", 2)
        g1 = flip(s1, "section", 1)
        if final:
            grad_out = gradient(grad_out_kernel, (hidden, quarter), (piece, quarter), *hids, dy, flops=work)
            own, grad_out = lax.optimization_barrier((own, grad_out))
        (pay,) = local(dact_kernel, [resident(wide, BF16)], own, g3, g2, g1, act, slope)
        p3 = flip(pay, "section", 3)
        p2 = flip(pay, "section", 2)
        p1 = flip(pay, "section", 1)
        total = [resident((rows, quarter), F32)]
        begun = local(functools.partial(back_kernel, (0,), True), total, pay, weight_in, flops=work // 4)
        begun = local(functools.partial(back_kernel, (3, 2), False), total, p3, p2, weight_in, *begun, flops=work // 2)
        keep, send = local(
            back_last_kernel,
            [resident((rows + SIDE, 2 * share), F32), resident((rows + SIDE, 2 * share), BF16)],
            pay, p1, p2, p3, weight_in, *begun,
            scratch=[pltpu.VMEM((rows, quarter), F32)], flops=work // 4,
        )
        got = flip(send, "dp", 1)
        rest, send = local(
            middle_kernel,
            [resident((rows + SIDE, share), F32), resident((rows + SIDE, share), BF16)],
            keep, got,
        )
        if phase == 0 and not final:
            send, hid = lax.optimization_barrier((send, hid))
            hids = gather_hidden(hid)
        got = flip(send, "dp", 2)
        if final:
            grad_in = gradient(
                grad_in_kernel, (quarter, hidden), (quarter, piece), pay, p1, p2, p3, x_full, gain, scale,
                scratch=[pltpu.VMEM((rows, quarter), BF16)], flops=work,
            )
            got, grad_in = lax.optimization_barrier((got, grad_in))
        outs = [resident((rows, share), BF16)]
        if final:
            outs = [jax.ShapeDtypeStruct((rows, share), BF16), jax.ShapeDtypeStruct((1, share), F32)]
        finished = local(functools.partial(finish_kernel, width), outs, rest, got, x0, dy, gain, scale)
        if not final:
            d0 = lax.ppermute(finished[0], "section", [(i, i - 4) for i in range(4, sections)])
            d2 = flip(d0, "dp", 2)
            d1 = flip(d0, "dp", 1)
            d3 = flip(d2, "dp", 1)
            down = (d0, d1, d2, d3)

    grad_x, grad_gain = finished
    return grad_in[None], grad_out[None], grad_gain, grad_x.reshape(1, micro, tok, share)


def shards(checkpoints, gain, w_in, w_out, cotangent):
    rows = checkpoints.shape[1] * checkpoints.shape[2]
    share = checkpoints.shape[3]
    piece = w_in.shape[2] // 4
    if lax.axis_size("dp") == 4 and rows % 16 == 0 and share % 128 == 0 and piece % 128 == 0 and rows <= min(share, piece):
        return shards_of_four(checkpoints, gain, w_in, w_out, cotangent)
    return shards_of_any(checkpoints, gain, w_in, w_out, cotangent)


def solution(mesh):
    in_specs = (
        P("section", None, None, "dp"),
        P("section", None),
        P("section", None, "dp"),
        P("section", "dp", None),
        P(None, None, "dp"),
    )
    out_specs = (
        P("section", None, "dp"),
        P("section", "dp", None),
        P("section", "dp"),
        P("section", None, None, "dp"),
    )
    return jax.shard_map(shards, mesh=mesh, in_specs=in_specs, out_specs=out_specs, check_vma=False)
```

profile of v0, /device:TPU:0, one launch (start us, length us, event | category | flops | bytes accessed | tf_op | source)
XLA Modules:
  0.0 102.3 jit_solution(12111940299961589227)
XLA Ops:
  0.6 0.5 collective-permute-start.1
  1.1 2.6 %collective-permute-start = (bf16[192,256]{1,0:T(8,128)(2,1)}, bf16[192,256]{1,0:T(8,128)(2,1)S(1)}, u32[]{:S(2)}, u32[]{:S(2)}) collective-permute-start(bf16[192,256]{1,0:T(8,128)(2,1)} %bitcast.14), channel_id=1, source_target_pairs={{0,2},{1,3},{2,0},{3,1},{4,6},{5,7},{6,4},{7,5},{8,10},{9,11},{10,... | collective-permute-start | bytes 294920 | tf_op jit(solution)/shard_map/ppermute | solution.py:16
  3.7 0.7 collective-permute-start.3
  4.4 2.2 %shard_map.84 = (bf16[1024,2048]{1,0:T(8,128)(2,1)S(1)}, bf16[192,256]{1,0:T(8,128)(2,1)S(1)}, f32[1,1024]{1,0:T(1,128)S(1)}) custom-call(bf16[1024,2048]{1,0:T(8,128)(2,1)} %bitcast.7, bf16[192,256]{1,0:T(8,128)(2,1)} %bitcast.15, f32[1,1024]{1,0:T(1,128)} %refs_2_.1), custom_call_target="tpu_custom_call" | custom-call | bytes 8593408 | tf_op jit(solution)/shard_map/pallas_call | solution.py:240
  6.6 0.7 collective-permute-done.x2
  7.3 0.6 shard_map.85.before
  7.9 0.7 collective-permute-done.2.x3
  8.6 0.6 shard_map.86
  9.2 2.9 %collective-permute-start.7 = (bf16[208,512]{1,0:T(8,128)(2,1)S(1)}, bf16[208,512]{1,0:T(8,128)(2,1)S(1)}, u32[]{:S(2)}, u32[]{:S(2)}) collective-permute-start(bf16[208,512]{1,0:T(8,128)(2,1)S(1)} %get-tuple-element.75), channel_id=1, source_target_pairs={{0,12},{4,8},{8,4},{12,0},{16,28},{20,24},{24,20},{28,16},{1,13},{... | collective-permute-start | bytes 638984 | tf_op jit(solution)/shard_map/ppermute | solution.py:16
  12.1 0.4 collective-permute-start.8
  12.6 0.2 collective-permute-start.9
  12.8 2.3 %shard_map.87 = (bf16[2048,1024]{1,0:T(8,128)(2,1)S(1)}, bf16[192,1024]{1,0:T(8,128)(2,1)S(1)}) custom-call(bf16[2048,1024]{1,0:T(8,128)(2,1)} %bitcast.9, bf16[192,1024]{1,0:T(8,128)(2,1)} %bitcast.12), custom_call_target="tpu_custom_call" | custom-call | bytes 9175040 | tf_op jit(solution)/shard_map/pallas_call | solution.py:240
  15.1 1.6 %shard_map.88 = (f32[192,512]{1,0:T(8,128)S(1)}, bf16[192,512]{1,0:T(8,128)(2,1)S(1)}, bf16[192,512]{1,0:T(8,128)(2,1)S(1)}, bf16[192,512]{1,0:T(8,128)(2,1)S(1)}, bf16[192,1024]{1,0:T(8,128)(2,1)S(1)}) custom-call(bf16[192,1024]{1,0:T(8,128)(2,1)S(1)} %get-tuple-element.68.cot, bf16[192,1024]{1,0:T(8,128)(2,1)S(1)} %collective-permute-done.3.sent, ...), custom_call_target="tpu_custom_call" | custom-call | flops 805306368 | bytes 4980736 | tf_op jit(solution)/shard_map/pallas_call | solution.py:195
  16.7 2.9 %collective-permute-start.4 = (bf16[192,512]{1,0:T(8,128)(2,1)S(1)}, bf16[192,512]{1,0:T(8,128)(2,1)S(1)}, u32[]{:S(2)}, u32[]{:S(2)}) collective-permute-start(bf16[192,512]{1,0:T(8,128)(2,1)S(1)} %get-tuple-element.71), channel_id=1, source_target_pairs={{0,12},{4,8},{8,4},{12,0},{16,28},{20,24},{24,20},{28,16},{1,13},{... | collective-permute-start | bytes 589832 | tf_op jit(solution)/shard_map/ppermute | solution.py:16
  19.5 0.4 collective-permute-start.5
  20.0 0.2 collective-permute-start.6
  20.2 3.0 %collective-permute-done.8.g2 = bf16[208,512]{1,0:T(8,128)(2,1)S(1)} collective-permute-done((bf16[208,512]{1,0:T(8,128)(2,1)S(1)}, bf16[208,512]{1,0:T(8,128)(2,1)S(1)}, u32[]{:S(2)}, u32[]{:S(2)}) %collective-permute-start.8) | collective-permute-done | bytes 213024 | tf_op jit(solution)/shard_map/ppermute | solution.py:16
  23.2 0.6 shard_map.89
  23.8 3.3 %collective-permute-done.4.g1 = bf16[192,512]{1,0:T(8,128)(2,1)S(1)} collective-permute-done((bf16[192,512]{1,0:T(8,128)(2,1)S(1)}, bf16[192,512]{1,0:T(8,128)(2,1)S(1)}, u32[]{:S(2)}, u32[]{:S(2)}) %collective-permute-start.4) | collective-permute-done | bytes 196640 | tf_op jit(solution)/shard_map/ppermute | solution.py:16
  27.1 3.8 %collective-permute-done.5.g2 = bf16[192,512]{1,0:T(8,128)(2,1)S(1)} collective-permute-done((bf16[192,512]{1,0:T(8,128)(2,1)S(1)}, bf16[192,512]{1,0:T(8,128)(2,1)S(1)}, u32[]{:S(2)}, u32[]{:S(2)}) %collective-permute-start.5) | collective-permute-done | bytes 196640 | tf_op jit(solution)/shard_map/ppermute | solution.py:16
  30.9 0.2 shard_map.90.refs_0_.p0
  31.2 2.4 %collective-permute-start.12 = (bf16[208,512]{1,0:T(8,128)(2,1)S(1)}, bf16[208,512]{1,0:T(8,128)(2,1)S(1)}, u32[]{:S(2)}, u32[]{:S(2)}) collective-permute-start(bf16[208,512]{1,0:T(8,128)(2,1)S(1)} %shard_map.90.refs_0_.p0), channel_id=1, source_target_pairs={{0,12},{4,8},{8,4},{12,0},{16,28},{20,24},{24,20},{28,16},{1,13},{... | collective-permute-start | bytes 638984 | tf_op jit(solution)/shard_map/ppermute | solution.py:16
  33.6 0.5 collective-permute-start.11
  34.1 0.7 collective-permute-start.10
  34.7 0.5 shard_map.91.refs_3_
  35.2 5.1 %collective-permute-done.12.refs_0_.p3 = bf16[208,512]{1,0:T(8,128)(2,1)S(1)} collective-permute-done((bf16[208,512]{1,0:T(8,128)(2,1)S(1)}, bf16[208,512]{1,0:T(8,128)(2,1)S(1)}, u32[]{:S(2)}, u32[]{:S(2)}) %collective-permute-start.12) | collective-permute-done | bytes 213024 | tf_op jit(solution)/shard_map/ppermute | solution.py:16
  40.3 3.5 %collective-permute-done.11.refs_1_.p2 = bf16[208,512]{1,0:T(8,128)(2,1)S(1)} collective-permute-done((bf16[208,512]{1,0:T(8,128)(2,1)S(1)}, bf16[208,512]{1,0:T(8,128)(2,1)S(1)}, u32[]{:S(2)}, u32[]{:S(2)}) %collective-permute-start.11) | collective-permute-done | bytes 213024 | tf_op jit(solution)/shard_map/ppermute | solution.py:16
  43.8 0.8 shard_map.92.earlier
  44.7 0.5 shard_map.93
  45.3 1.5 %collective-permute-done.13.got = bf16[208,512]{1,0:T(8,128)(2,1)S(1)} collective-permute-done((bf16[208,512]{1,0:T(8,128)(2,1)S(1)}, bf16[208,512]{1,0:T(8,128)(2,1)S(1)}, u32[]{:S(2)}, u32[]{:S(2)}) %collective-permute-start.13) | collective-permute-done | bytes 213024 | tf_op jit(solution)/shard_map/ppermute | solution.py:16
  46.8 1.6 %collective-permute-start.14 = (bf16[208,256]{1,0:T(8,128)(2,1)S(1)}, bf16[208,256]{1,0:T(8,128)(2,1)S(1)}, u32[]{:S(2)}, u32[]{:S(2)}) collective-permute-start(bf16[208,256]{1,0:T(8,128)(2,1)S(1)} %get-tuple-element.85), channel_id=1, source_target_pairs={{0,2},{1,3},{2,0},{3,1},{4,6},{5,7},{6,4},{7,5},{8,10},{9,11},{10,... | collective-permute-start | bytes 319496 | tf_op jit(solution)/shard_map/ppermute | solution.py:16
  48.3 3.5 %collective-permute-done.14.got = bf16[208,256]{1,0:T(8,128)(2,1)S(1)} collective-permute-done((bf16[208,256]{1,0:T(8,128)(2,1)S(1)}, bf16[208,256]{1,0:T(8,128)(2,1)S(1)}, u32[]{:S(2)}, u32[]{:S(2)}) %collective-permute-start.14) | collective-permute-done | bytes 106528 | tf_op jit(solution)/shard_map/ppermute | solution.py:16
  51.9 0.2 shard_map.95
  52.1 1.3 %collective-permute-start.15 = (bf16[192,256]{1,0:T(8,128)(2,1)S(1)}, bf16[192,256]{1,0:T(8,128)(2,1)S(1)}, u32[]{:S(2)}, u32[]{:S(2)}) collective-permute-start(bf16[192,256]{1,0:T(8,128)(2,1)S(1)} %shard_map.95), channel_id=1, source_target_pairs={{16,0},{20,4},{24,8},{28,12},{17,1},{21,5},{25,9},{29,13},{18,2},{... | collective-permute-start | bytes 294920 | tf_op jit(solution)/shard_map/ppermute | solution.py:590
  53.4 1.6 %collective-permute-start.21 = (bf16[192,512]{1,0:T(8,128)(2,1)S(1)}, bf16[192,512]{1,0:T(8,128)(2,1)S(1)}, u32[]{:S(2)}, u32[]{:S(2)}) collective-permute-start(bf16[192,512]{1,0:T(8,128)(2,1)S(1)} %get-tuple-element.91.h0), channel_id=1, source_target_pairs={{0,12},{4,8},{8,4},{12,0},{16,28},{20,24},{24,20},{28,16},{1,13},{... | collective-permute-start | bytes 589832 | tf_op jit(solution)/shard_map/ppermute | solution.py:16
  55.0 0.4 collective-permute-start.20
  55.4 1.5 %collective-permute-start.19 = (bf16[192,512]{1,0:T(8,128)(2,1)S(1)}, bf16[192,512]{1,0:T(8,128)(2,1)S(1)}, u32[]{:S(2)}, u32[]{:S(2)}) collective-permute-start(bf16[192,512]{1,0:T(8,128)(2,1)S(1)} %get-tuple-element.91.h0), channel_id=1, source_target_pairs={{0,4},{4,0},{8,12},{12,8},{16,20},{20,16},{24,28},{28,24},{1,5},{5... | collective-permute-start | bytes 589832 | tf_op jit(solution)/shard_map/ppermute | solution.py:16
  56.9 5.1 %collective-permute-done.15.refs_0_.refs_4_ = bf16[192,256]{1,0:T(8,128)(2,1)S(1)} collective-permute-done((bf16[192,256]{1,0:T(8,128)(2,1)S(1)}, bf16[192,256]{1,0:T(8,128)(2,1)S(1)}, u32[]{:S(2)}, u32[]{:S(2)}) %collective-permute-start.15) | collective-permute-done | bytes 98336 | tf_op jit(solution)/shard_map/ppermute | solution.py:590
  62.0 1.5 %collective-permute-start.16 = (bf16[192,256]{1,0:T(8,128)(2,1)S(1)}, bf16[192,256]{1,0:T(8,128)(2,1)S(1)}, u32[]{:S(2)}, u32[]{:S(2)}) collective-permute-start(bf16[192,256]{1,0:T(8,128)(2,1)S(1)} %collective-permute-done.15.refs_0_.refs_4_), channel_id=1, source_target_pairs={{0,2},{1,3},{2,0},{3,1},{4,6},{5,7},{6,4},{7,5},{8,10},{9,11},{10,... | collective-permute-start | bytes 294920 | tf_op jit(solution)/shard_map/ppermute | solution.py:16
  63.5 3.1 %collective-permute-done.16.refs_1_.refs_6_ = bf16[192,256]{1,0:T(8,128)(2,1)S(1)} collective-permute-done((bf16[192,256]{1,0:T(8,128)(2,1)S(1)}, bf16[192,256]{1,0:T(8,128)(2,1)S(1)}, u32[]{:S(2)}, u32[]{:S(2)}) %collective-permute-start.16) | collective-permute-done | bytes 98336 | tf_op jit(solution)/shard_map/ppermute | solution.py:16
  66.6 0.5 shard_map.96.refs_4_
  67.1 0.9 shard_map.97.refs_3_
  68.0 0.8 shard_map.98
  68.8 0.1 collective-permute-start.22
  68.9 2.2 %collective-permute-start.23 = (bf16[192,512]{1,0:T(8,128)(2,1)S(1)}, bf16[192,512]{1,0:T(8,128)(2,1)S(1)}, u32[]{:S(2)}, u32[]{:S(2)}) collective-permute-start(bf16[192,512]{1,0:T(8,128)(2,1)S(1)} %get-tuple-element.98), channel_id=1, source_target_pairs={{0,8},{4,12},{8,0},{12,4},{16,24},{20,28},{24,16},{28,20},{1,9},{5... | collective-permute-start | bytes 589832 | tf_op jit(solution)/shard_map/ppermute | solution.py:16
  71.0 1.3 %collective-permute-start.24 = (bf16[192,512]{1,0:T(8,128)(2,1)S(1)}, bf16[192,512]{1,0:T(8,128)(2,1)S(1)}, u32[]{:S(2)}, u32[]{:S(2)}) collective-permute-start(bf16[192,512]{1,0:T(8,128)(2,1)S(1)} %get-tuple-element.99), channel_id=1, source_target_pairs={{0,4},{4,0},{8,12},{12,8},{16,20},{20,16},{24,28},{28,24},{1,5},{5... | collective-permute-start | bytes 589832 | tf_op jit(solution)/shard_map/ppermute | solution.py:16
  72.3 2.5 %shard_map.99 = bf16[2048,1024]{1,0:T(8,128)(2,1)} custom-call(bf16[192,512]{1,0:T(8,128)(2,1)S(1)} %get-tuple-element.91.h0, bf16[192,512]{1,0:T(8,128)(2,1)S(1)} %collective-permute-done.19.h1, bf16[192,512]{1,0:T(8,128)(2,1)S(1)} %collective-permute-done.20.h2, bf16[192,512]{1,0:T(8,128)(2,1)S(1)} %collective-permute-done.21.h3, ...), custom_call_target="tpu_custom_call" | custom-call | flops 805306368 | bytes 4194304 | tf_op jit(solution)/shard_map/pallas_call | solution.py:474
  74.9 2.6 %collective-permute-done.22.g1 = bf16[192,512]{1,0:T(8,128)(2,1)S(1)} collective-permute-done((bf16[192,512]{1,0:T(8,128)(2,1)S(1)}, bf16[192,512]{1,0:T(8,128)(2,1)S(1)}, u32[]{:S(2)}, u32[]{:S(2)}) %collective-permute-start.22) | collective-permute-done | bytes 196640 | tf_op jit(solution)/shard_map/ppermute | solution.py:16
  77.5 3.0 %collective-permute-done.23.g2 = bf16[192,512]{1,0:T(8,128)(2,1)S(1)} collective-permute-done((bf16[192,512]{1,0:T(8,128)(2,1)S(1)}, bf16[192,512]{1,0:T(8,128)(2,1)S(1)}, u32[]{:S(2)}, u32[]{:S(2)}) %collective-permute-start.23) | collective-permute-done | bytes 196640 | tf_op jit(solution)/shard_map/ppermute | solution.py:16
  80.5 0.8 collective-permute-done.24.g3
  81.3 0.2 shard_map.100.refs_0_.p0
  81.5 0.4 collective-permute-start.27
  81.9 1.8 %collective-permute-start.26 = (bf16[208,512]{1,0:T(8,128)(2,1)S(1)}, bf16[208,512]{1,0:T(8,128)(2,1)S(1)}, u32[]{:S(2)}, u32[]{:S(2)}) collective-permute-start(bf16[208,512]{1,0:T(8,128)(2,1)S(1)} %shard_map.100.refs_0_.p0), channel_id=1, source_target_pairs={{0,8},{4,12},{8,0},{12,4},{16,24},{20,28},{24,16},{28,20},{1,9},{5... | collective-permute-start | bytes 638984 | tf_op jit(solution)/shard_map/ppermute | solution.py:16
  83.7 1.4 %collective-permute-start.25 = (bf16[208,512]{1,0:T(8,128)(2,1)S(1)}, bf16[208,512]{1,0:T(8,128)(2,1)S(1)}, u32[]{:S(2)}, u32[]{:S(2)}) collective-permute-start(bf16[208,512]{1,0:T(8,128)(2,1)S(1)} %shard_map.100.refs_0_.p0), channel_id=1, source_target_pairs={{0,4},{4,0},{8,12},{12,8},{16,20},{20,16},{24,28},{28,24},{1,5},{5... | collective-permute-start | bytes 638984 | tf_op jit(solution)/shard_map/ppermute | solution.py:16
  85.1 0.5 shard_map.101.refs_3_
  85.6 5.1 %collective-permute-done.27.refs_0_.p3 = bf16[208,512]{1,0:T(8,128)(2,1)S(1)} collective-permute-done((bf16[208,512]{1,0:T(8,128)(2,1)S(1)}, bf16[208,512]{1,0:T(8,128)(2,1)S(1)}, u32[]{:S(2)}, u32[]{:S(2)}) %collective-permute-start.27) | collective-permute-done | bytes 213024 | tf_op jit(solution)/shard_map/ppermute | solution.py:16
  90.6 2.8 %collective-permute-done.26.refs_1_.p2 = bf16[208,512]{1,0:T(8,128)(2,1)S(1)} collective-permute-done((bf16[208,512]{1,0:T(8,128)(2,1)S(1)}, bf16[208,512]{1,0:T(8,128)(2,1)S(1)}, u32[]{:S(2)}, u32[]{:S(2)}) %collective-permute-start.26) | collective-permute-done | bytes 213024 | tf_op jit(solution)/shard_map/ppermute | solution.py:16
  93.4 0.8 shard_map.102.earlier
  94.3 0.5 shard_map.103
  94.9 1.5 %collective-permute-done.28.got = bf16[208,512]{1,0:T(8,128)(2,1)S(1)} collective-permute-done((bf16[208,512]{1,0:T(8,128)(2,1)S(1)}, bf16[208,512]{1,0:T(8,128)(2,1)S(1)}, u32[]{:S(2)}, u32[]{:S(2)}) %collective-permute-start.28) | collective-permute-done | bytes 213024 | tf_op jit(solution)/shard_map/ppermute | solution.py:16
  96.4 1.6 %collective-permute-start.29 = (bf16[208,256]{1,0:T(8,128)(2,1)S(1)}, bf16[208,256]{1,0:T(8,128)(2,1)S(1)}, u32[]{:S(2)}, u32[]{:S(2)}) collective-permute-start(bf16[208,256]{1,0:T(8,128)(2,1)S(1)} %get-tuple-element.102), channel_id=1, source_target_pairs={{0,2},{1,3},{2,0},{3,1},{4,6},{5,7},{6,4},{7,5},{8,10},{9,11},{10,... | collective-permute-start | bytes 319496 | tf_op jit(solution)/shard_map/ppermute | solution.py:16
  98.0 2.6 %shard_map.105 = bf16[1024,2048]{1,0:T(8,128)(2,1)} custom-call(bf16[208,512]{1,0:T(8,128)(2,1)S(1)} %shard_map.100.refs_0_.p0, bf16[208,512]{1,0:T(8,128)(2,1)S(1)} %collective-permute-done.25.p1, bf16[208,512]{1,0:T(8,128)(2,1)S(1)} %collective-permute-done.26.refs_1_.p2, bf16[208,512]{1,0:T(8,128)(2,1)S(1)} %collective-permute-done.27.refs_0_.p3, ...), custom_call_target="tpu_custom_call" | custom-call | flops 805306368 | bytes 4194304 | tf_op jit(solution)/shard_map/pallas_call | solution.py:474
  100.6 0.8 collective-permute-done.29.got
  101.5 0.8 shard_map.106
  (19 shorter events, 0.3 us)
Async XLA Ops:
  0.6 6.0 %collective-permute-start.1 = (bf16[192,256]{1,0:T(8,128)(2,1)}, bf16[192,256]{1,0:T(8,128)(2,1)S(1)}, u32[]{:S(2)}, u32[]{:S(2)}) collective-permute-start(bf16[192,256]{1,0:T(8,128)(2,1)} %bitcast.13), channel_id=1, source_target_pairs={{0,1},{1,0},{2,3},{3,2},{4,5},{5,4},{6,7},{7,6},{8,9},{9,8},{10,11... | collective-permute-start | bytes 294920 | tf_op jit(solution)/shard_map/ppermute | solution.py:16
  1.1 6.2 %collective-permute-start = (bf16[192,256]{1,0:T(8,128)(2,1)}, bf16[192,256]{1,0:T(8,128)(2,1)S(1)}, u32[]{:S(2)}, u32[]{:S(2)}) collective-permute-start(bf16[192,256]{1,0:T(8,128)(2,1)} %bitcast.14), channel_id=1, source_target_pairs={{0,2},{1,3},{2,0},{3,1},{4,6},{5,7},{6,4},{7,5},{8,10},{9,11},{10,... | collective-permute-start | bytes 294920 | tf_op jit(solution)/shard_map/ppermute | solution.py:16
  3.7 11.4 %collective-permute-start.3 = (bf16[192,1024]{1,0:T(8,128)(2,1)}, bf16[192,1024]{1,0:T(8,128)(2,1)S(1)}, u32[]{:S(2)}, u32[]{:S(2)}) collective-permute-start(bf16[192,1024]{1,0:T(8,128)(2,1)} %bitcast.11), channel_id=1, source_target_pairs={{20,17},{16,18},{24,19},{17,20},{29,22},{21,23},{26,24},{18,25},{3... | collective-permute-start | bytes 1179656 | tf_op jit(solution)/shard_map/ppermute | solution.py:506
  7.3 1.3 %collective-permute-start.2 = (bf16[192,256]{1,0:T(8,128)(2,1)S(1)}, bf16[192,256]{1,0:T(8,128)(2,1)S(1)}, u32[]{:S(2)}, u32[]{:S(2)}) collective-permute-start(bf16[192,256]{1,0:T(8,128)(2,1)S(1)} %collective-permute-done.x2), channel_id=1, source_target_pairs={{0,1},{1,0},{2,3},{3,2},{4,5},{5,4},{6,7},{7,6},{8,9},{9,8},{10,11... | collective-permute-start | bytes 294920 | tf_op jit(solution)/shard_map/ppermute | solution.py:16
  9.2 10.7 %collective-permute-start.7 = (bf16[208,512]{1,0:T(8,128)(2,1)S(1)}, bf16[208,512]{1,0:T(8,128)(2,1)S(1)}, u32[]{:S(2)}, u32[]{:S(2)}) collective-permute-start(bf16[208,512]{1,0:T(8,128)(2,1)S(1)} %get-tuple-element.75), channel_id=1, source_target_pairs={{0,12},{4,8},{8,4},{12,0},{16,28},{20,24},{24,20},{28,16},{1,13},{... | collective-permute-start | bytes 638984 | tf_op jit(solution)/shard_map/ppermute | solution.py:16
  12.1 11.1 %collective-permute-start.8 = (bf16[208,512]{1,0:T(8,128)(2,1)S(1)}, bf16[208,512]{1,0:T(8,128)(2,1)S(1)}, u32[]{:S(2)}, u32[]{:S(2)}) collective-permute-start(bf16[208,512]{1,0:T(8,128)(2,1)S(1)} %get-tuple-element.76), channel_id=1, source_target_pairs={{0,8},{4,12},{8,0},{12,4},{16,24},{20,28},{24,16},{28,20},{1,9},{5... | collective-permute-start | bytes 638984 | tf_op jit(solution)/shard_map/ppermute | solution.py:16
  12.6 10.7 %collective-permute-start.9 = (bf16[208,512]{1,0:T(8,128)(2,1)S(1)}, bf16[208,512]{1,0:T(8,128)(2,1)S(1)}, u32[]{:S(2)}, u32[]{:S(2)}) collective-permute-start(bf16[208,512]{1,0:T(8,128)(2,1)S(1)} %get-tuple-element.77), channel_id=1, source_target_pairs={{0,4},{4,0},{8,12},{12,8},{16,20},{20,16},{24,28},{28,24},{1,5},{5... | collective-permute-start | bytes 638984 | tf_op jit(solution)/shard_map/ppermute | solution.py:16
  16.7 10.5 %collective-permute-start.4 = (bf16[192,512]{1,0:T(8,128)(2,1)S(1)}, bf16[192,512]{1,0:T(8,128)(2,1)S(1)}, u32[]{:S(2)}, u32[]{:S(2)}) collective-permute-start(bf16[192,512]{1,0:T(8,128)(2,1)S(1)} %get-tuple-element.71), channel_id=1, source_target_pairs={{0,12},{4,8},{8,4},{12,0},{16,28},{20,24},{24,20},{28,16},{1,13},{... | collective-permute-start | bytes 589832 | tf_op jit(solution)/shard_map/ppermute | solution.py:16
  19.5 11.4 %collective-permute-start.5 = (bf16[192,512]{1,0:T(8,128)(2,1)S(1)}, bf16[192,512]{1,0:T(8,128)(2,1)S(1)}, u32[]{:S(2)}, u32[]{:S(2)}) collective-permute-start(bf16[192,512]{1,0:T(8,128)(2,1)S(1)} %get-tuple-element.72), channel_id=1, source_target_pairs={{0,8},{4,12},{8,0},{12,4},{16,24},{20,28},{24,16},{28,20},{1,9},{5... | collective-permute-start | bytes 589832 | tf_op jit(solution)/shard_map/ppermute | solution.py:16
  20.0 11.0 %collective-permute-start.6 = (bf16[192,512]{1,0:T(8,128)(2,1)S(1)}, bf16[192,512]{1,0:T(8,128)(2,1)S(1)}, u32[]{:S(2)}, u32[]{:S(2)}) collective-permute-start(bf16[192,512]{1,0:T(8,128)(2,1)S(1)} %get-tuple-element.73), channel_id=1, source_target_pairs={{0,4},{4,0},{8,12},{12,8},{16,20},{20,16},{24,28},{28,24},{1,5},{5... | collective-permute-start | bytes 589832 | tf_op jit(solution)/shard_map/ppermute | solution.py:16
  31.2 9.1 %collective-permute-start.12 = (bf16[208,512]{1,0:T(8,128)(2,1)S(1)}, bf16[208,512]{1,0:T(8,128)(2,1)S(1)}, u32[]{:S(2)}, u32[]{:S(2)}) collective-permute-start(bf16[208,512]{1,0:T(8,128)(2,1)S(1)} %shard_map.90.refs_0_.p0), channel_id=1, source_target_pairs={{0,12},{4,8},{8,4},{12,0},{16,28},{20,24},{24,20},{28,16},{1,13},{... | collective-permute-start | bytes 638984 | tf_op jit(solution)/shard_map/ppermute | solution.py:16
  33.6 10.2 %collective-permute-start.11 = (bf16[208,512]{1,0:T(8,128)(2,1)S(1)}, bf16[208,512]{1,0:T(8,128)(2,1)S(1)}, u32[]{:S(2)}, u32[]{:S(2)}) collective-permute-start(bf16[208,512]{1,0:T(8,128)(2,1)S(1)} %shard_map.90.refs_0_.p0), channel_id=1, source_target_pairs={{0,8},{4,12},{8,0},{12,4},{16,24},{20,28},{24,16},{28,20},{1,9},{5... | collective-permute-start | bytes 638984 | tf_op jit(solution)/shard_map/ppermute | solution.py:16
  34.1 10.6 %collective-permute-start.10 = (bf16[208,512]{1,0:T(8,128)(2,1)S(1)}, bf16[208,512]{1,0:T(8,128)(2,1)S(1)}, u32[]{:S(2)}, u32[]{:S(2)}) collective-permute-start(bf16[208,512]{1,0:T(8,128)(2,1)S(1)} %shard_map.90.refs_0_.p0), channel_id=1, source_target_pairs={{0,4},{4,0},{8,12},{12,8},{16,20},{20,16},{24,28},{28,24},{1,5},{5... | collective-permute-start | bytes 638984 | tf_op jit(solution)/shard_map/ppermute | solution.py:16
  45.2 1.5 %collective-permute-start.13 = (bf16[208,512]{1,0:T(8,128)(2,1)S(1)}, bf16[208,512]{1,0:T(8,128)(2,1)S(1)}, u32[]{:S(2)}, u32[]{:S(2)}) collective-permute-start(bf16[208,512]{1,0:T(8,128)(2,1)S(1)} %get-tuple-element.81), channel_id=1, source_target_pairs={{0,1},{1,0},{2,3},{3,2},{4,5},{5,4},{6,7},{7,6},{8,9},{9,8},{10,11... | collective-permute-start | bytes 638984 | tf_op jit(solution)/shard_map/ppermute | solution.py:16
  46.8 5.1 %collective-permute-start.14 = (bf16[208,256]{1,0:T(8,128)(2,1)S(1)}, bf16[208,256]{1,0:T(8,128)(2,1)S(1)}, u32[]{:S(2)}, u32[]{:S(2)}) collective-permute-start(bf16[208,256]{1,0:T(8,128)(2,1)S(1)} %get-tuple-element.85), channel_id=1, source_target_pairs={{0,2},{1,3},{2,0},{3,1},{4,6},{5,7},{6,4},{7,5},{8,10},{9,11},{10,... | collective-permute-start | bytes 319496 | tf_op jit(solution)/shard_map/ppermute | solution.py:16
  52.1 9.9 %collective-permute-start.15 = (bf16[192,256]{1,0:T(8,128)(2,1)S(1)}, bf16[192,256]{1,0:T(8,128)(2,1)S(1)}, u32[]{:S(2)}, u32[]{:S(2)}) collective-permute-start(bf16[192,256]{1,0:T(8,128)(2,1)S(1)} %shard_map.95), channel_id=1, source_target_pairs={{16,0},{20,4},{24,8},{28,12},{17,1},{21,5},{25,9},{29,13},{18,2},{... | collective-permute-start | bytes 294920 | tf_op jit(solution)/shard_map/ppermute | solution.py:590
  53.4 13.2 %collective-permute-start.21 = (bf16[192,512]{1,0:T(8,128)(2,1)S(1)}, bf16[192,512]{1,0:T(8,128)(2,1)S(1)}, u32[]{:S(2)}, u32[]{:S(2)}) collective-permute-start(bf16[192,512]{1,0:T(8,128)(2,1)S(1)} %get-tuple-element.91.h0), channel_id=1, source_target_pairs={{0,12},{4,8},{8,4},{12,0},{16,28},{20,24},{24,20},{28,16},{1,13},{... | collective-permute-start | bytes 589832 | tf_op jit(solution)/shard_map/ppermute | solution.py:16
  55.0 11.6 %collective-permute-start.20 = (bf16[192,512]{1,0:T(8,128)(2,1)S(1)}, bf16[192,512]{1,0:T(8,128)(2,1)S(1)}, u32[]{:S(2)}, u32[]{:S(2)}) collective-permute-start(bf16[192,512]{1,0:T(8,128)(2,1)S(1)} %get-tuple-element.91.h0), channel_id=1, source_target_pairs={{0,8},{4,12},{8,0},{12,4},{16,24},{20,28},{24,16},{28,20},{1,9},{5... | collective-permute-start | bytes 589832 | tf_op jit(solution)/shard_map/ppermute | solution.py:16
  55.4 11.2 %collective-permute-start.19 = (bf16[192,512]{1,0:T(8,128)(2,1)S(1)}, bf16[192,512]{1,0:T(8,128)(2,1)S(1)}, u32[]{:S(2)}, u32[]{:S(2)}) collective-permute-start(bf16[192,512]{1,0:T(8,128)(2,1)S(1)} %get-tuple-element.91.h0), channel_id=1, source_target_pairs={{0,4},{4,0},{8,12},{12,8},{16,20},{20,16},{24,28},{28,24},{1,5},{5... | collective-permute-start | bytes 589832 | tf_op jit(solution)/shard_map/ppermute | solution.py:16
  62.0 4.6 %collective-permute-start.16 = (bf16[192,256]{1,0:T(8,128)(2,1)S(1)}, bf16[192,256]{1,0:T(8,128)(2,1)S(1)}, u32[]{:S(2)}, u32[]{:S(2)}) collective-permute-start(bf16[192,256]{1,0:T(8,128)(2,1)S(1)} %collective-permute-done.15.refs_0_.refs_4_), channel_id=1, source_target_pairs={{0,2},{1,3},{2,0},{3,1},{4,6},{5,7},{6,4},{7,5},{8,10},{9,11},{10,... | collective-permute-start | bytes 294920 | tf_op jit(solution)/shard_map/ppermute | solution.py:16
  63.5 3.7 %collective-permute-start.18 = (bf16[192,256]{1,0:T(8,128)(2,1)S(1)}, bf16[192,256]{1,0:T(8,128)(2,1)S(1)}, u32[]{:S(2)}, u32[]{:S(2)}) collective-permute-start(bf16[192,256]{1,0:T(8,128)(2,1)S(1)} %collective-permute-done.15.refs_0_.refs_4_), channel_id=1, source_target_pairs={{0,1},{1,0},{2,3},{3,2},{4,5},{5,4},{6,7},{7,6},{8,9},{9,8},{10,11... | collective-permute-start | bytes 294920 | tf_op jit(solution)/shard_map/ppermute | solution.py:16
  66.6 1.4 %collective-permute-start.17 = (bf16[192,256]{1,0:T(8,128)(2,1)S(1)}, bf16[192,256]{1,0:T(8,128)(2,1)S(1)}, u32[]{:S(2)}, u32[]{:S(2)}) collective-permute-start(bf16[192,256]{1,0:T(8,128)(2,1)S(1)} %collective-permute-done.16.refs_1_.refs_6_), channel_id=1, source_target_pairs={{0,1},{1,0},{2,3},{3,2},{4,5},{5,4},{6,7},{7,6},{8,9},{9,8},{10,11... | collective-permute-start | bytes 294920 | tf_op jit(solution)/shard_map/ppermute | solution.py:16
  68.8 8.7 %collective-permute-start.22 = (bf16[192,512]{1,0:T(8,128)(2,1)S(1)}, bf16[192,512]{1,0:T(8,128)(2,1)S(1)}, u32[]{:S(2)}, u32[]{:S(2)}) collective-permute-start(bf16[192,512]{1,0:T(8,128)(2,1)S(1)} %get-tuple-element.97), channel_id=1, source_target_pairs={{0,12},{4,8},{8,4},{12,0},{16,28},{20,24},{24,20},{28,16},{1,13},{... | collective-permute-start | bytes 589832 | tf_op jit(solution)/shard_map/ppermute | solution.py:16
  68.9 11.6 %collective-permute-start.23 = (bf16[192,512]{1,0:T(8,128)(2,1)S(1)}, bf16[192,512]{1,0:T(8,128)(2,1)S(1)}, u32[]{:S(2)}, u32[]{:S(2)}) collective-permute-start(bf16[192,512]{1,0:T(8,128)(2,1)S(1)} %get-tuple-element.98), channel_id=1, source_target_pairs={{0,8},{4,12},{8,0},{12,4},{16,24},{20,28},{24,16},{28,20},{1,9},{5... | collective-permute-start | bytes 589832 | tf_op jit(solution)/shard_map/ppermute | solution.py:16
  71.0 10.3 %collective-permute-start.24 = (bf16[192,512]{1,0:T(8,128)(2,1)S(1)}, bf16[192,512]{1,0:T(8,128)(2,1)S(1)}, u32[]{:S(2)}, u32[]{:S(2)}) collective-permute-start(bf16[192,512]{1,0:T(8,128)(2,1)S(1)} %get-tuple-element.99), channel_id=1, source_target_pairs={{0,4},{4,0},{8,12},{12,8},{16,20},{20,16},{24,28},{28,24},{1,5},{5... | collective-permute-start | bytes 589832 | tf_op jit(solution)/shard_map/ppermute | solution.py:16
  81.5 9.1 %collective-permute-start.27 = (bf16[208,512]{1,0:T(8,128)(2,1)S(1)}, bf16[208,512]{1,0:T(8,128)(2,1)S(1)}, u32[]{:S(2)}, u32[]{:S(2)}) collective-permute-start(bf16[208,512]{1,0:T(8,128)(2,1)S(1)} %shard_map.100.refs_0_.p0), channel_id=1, source_target_pairs={{0,12},{4,8},{8,4},{12,0},{16,28},{20,24},{24,20},{28,16},{1,13},{... | collective-permute-start | bytes 638984 | tf_op jit(solution)/shard_map/ppermute | solution.py:16
  81.9 11.6 %collective-permute-start.26 = (bf16[208,512]{1,0:T(8,128)(2,1)S(1)}, bf16[208,512]{1,0:T(8,128)(2,1)S(1)}, u32[]{:S(2)}, u32[]{:S(2)}) collective-permute-start(bf16[208,512]{1,0:T(8,128)(2,1)S(1)} %shard_map.100.refs_0_.p0), channel_id=1, source_target_pairs={{0,8},{4,12},{8,0},{12,4},{16,24},{20,28},{24,16},{28,20},{1,9},{5... | collective-permute-start | bytes 638984 | tf_op jit(solution)/shard_map/ppermute | solution.py:16
  83.7 10.6 %collective-permute-start.25 = (bf16[208,512]{1,0:T(8,128)(2,1)S(1)}, bf16[208,512]{1,0:T(8,128)(2,1)S(1)}, u32[]{:S(2)}, u32[]{:S(2)}) collective-permute-start(bf16[208,512]{1,0:T(8,128)(2,1)S(1)} %shard_map.100.refs_0_.p0), channel_id=1, source_target_pairs={{0,4},{4,0},{8,12},{12,8},{16,20},{20,16},{24,28},{28,24},{1,5},{5... | collective-permute-start | bytes 638984 | tf_op jit(solution)/shard_map/ppermute | solution.py:16
  94.8 1.5 %collective-permute-start.28 = (bf16[208,512]{1,0:T(8,128)(2,1)S(1)}, bf16[208,512]{1,0:T(8,128)(2,1)S(1)}, u32[]{:S(2)}, u32[]{:S(2)}) collective-permute-start(bf16[208,512]{1,0:T(8,128)(2,1)S(1)} %get-tuple-element.101), channel_id=1, source_target_pairs={{0,1},{1,0},{2,3},{3,2},{4,5},{5,4},{6,7},{7,6},{8,9},{9,8},{10,11... | collective-permute-start | bytes 638984 | tf_op jit(solution)/shard_map/ppermute | solution.py:16
  96.4 5.1 %collective-permute-start.29 = (bf16[208,256]{1,0:T(8,128)(2,1)S(1)}, bf16[208,256]{1,0:T(8,128)(2,1)S(1)}, u32[]{:S(2)}, u32[]{:S(2)}) collective-permute-start(bf16[208,256]{1,0:T(8,128)(2,1)S(1)} %get-tuple-element.102), channel_id=1, source_target_pairs={{0,2},{1,3},{2,0},{3,1},{4,6},{5,7},{6,4},{7,5},{8,10},{9,11},{10,... | collective-permute-start | bytes 319496 | tf_op jit(solution)/shard_map/ppermute | solution.py:16
where the time goes:
time: 102 us
  waiting for transfers between devices  49.9 us (49%)
  starting transfers between devices  31.2 us (31%)
  Pallas kernels  20.4 us (20%)
    ppermute x28, waiting for transfers between devices, flip(): return lax.ppermute(block, axis, [(i, i ^ bits) for i in range(count)])  44.8 us
    ppermute x28, starting transfers between devices, flip(): return lax.ppermute(block, axis, [(i, i ^ bits) for i in range(count)])  29.2 us
    pallas_call x19, Pallas kernels, local(): pl.pallas_call(body, out_shape=tuple(outs), in_specs=[spec] * len(args),...  10.7 us
    pallas_call x2, Pallas kernels, gradient(): pl.pallas_call(body, out_shape=jax.ShapeDtypeStruct(shape, BF16), in_spec...  5.13 us
    ppermute x1, waiting for transfers between devices, shards_of_four(): lax.ppermute(finished[0], 'section', [(i, i - 4) for i in range(4, sectio...  5.07 us
    pallas_call x2, Pallas kernels, load(): pl.pallas_call(load_kernel, out_shape=tuple((resident(a.shape, a.dtype) f...  4.49 us
  transfers between devices with their start and end apart: 30, of which 18 were waited for; matrix products, arithmetic and copies ran while one was open for 0% of the time, Pallas kernels for 17%

commit v1 on v0

--- a/solution.py
+++ b/solution.py
@@ -522,7 +522,7 @@
     act, slope, hid, scale = local(
         functools.partial(act_kernel, width),
         [resident((rows, piece), F32), resident((rows, piece), F32), resident((rows, piece), BF16), resident((rows, 1), F32)],
-        own, g3, g2, g1,
+        own, g1, g2, g3,
     )
 
     spread_outs = [resident((rows, piece), F32)] + [resident((rows, piece), BF16)] * 3 + [resident((rows, quarter), BF16)]
@@ -553,7 +553,7 @@
         if final:
             grad_out = gradient(grad_out_kernel, (hidden, quarter), (piece, quarter), *hids, dy, flops=work)
             own, grad_out = lax.optimization_barrier((own, grad_out))
-        (pay,) = local(dact_kernel, [resident(wide, BF16)], own, g3, g2, g1, act, slope)
+        (pay,) = local(dact_kernel, [resident(wide, BF16)], own, g1, g2, g3, act, slope)
         p3 = flip(pay, "section", 3)
         p2 = flip(pay, "section", 2)
         p1 = flip(pay, "section", 1)

time: 102 us -> 102 us (level)
  transfers between devices with their start and end apart: 30 -> 30, of which waited for: 18 -> 20; matrix products, arithmetic and copies ran while one was open for 0% -> 0% of each run, Pallas kernels for 17% -> 17%
where the time goes in v1:
time: 102 us
  waiting for transfers between devices  49.5 us (49%)
  starting transfers between devices  30.8 us (30%)
  Pallas kernels  20.3 us (20%)
    ppermute x28, waiting for transfers between devices, flip(): return lax.ppermute(block, axis, [(i, i ^ bits) for i in range(count)])  44.1 us
    ppermute x28, starting transfers between devices, flip(): return lax.ppermute(block, axis, [(i, i ^ bits) for i in range(count)])  28.9 us
    pallas_call x19, Pallas kernels, local(): pl.pallas_call(body, out_shape=tuple(outs), in_specs=[spec] * len(args),...  10.7 us
    ppermute x1, waiting for transfers between devices, shards_of_four(): lax.ppermute(finished[0], 'section', [(i, i - 4) for i in range(4, sectio...  5.37 us
    pallas_call x2, Pallas kernels, gradient(): pl.pallas_call(body, out_shape=jax.ShapeDtypeStruct(shape, BF16), in_spec...  5.13 us
    pallas_call x2, Pallas kernels, load(): pl.pallas_call(load_kernel, out_shape=tuple((resident(a.shape, a.dtype) f...  4.49 us
  transfers between devices with their start and end apart: 30, of which 20 were waited for; matrix products, arithmetic and copies ran while one was open for 0% of the time, Pallas kernels for 17%

profile of v1, /device:TPU:0, one launch (start us, length us, event | category | flops | bytes accessed | tf_op | source)
XLA Modules:
  0.0 101.5 jit_solution(9218854267604912133)
XLA Ops:
  0.6 0.5 collective-permute-start.1
  1.1 2.6 %collective-permute-start = (bf16[192,256]{1,0:T(8,128)(2,1)}, bf16[192,256]{1,0:T(8,128)(2,1)S(1)}, u32[]{:S(2)}, u32[]{:S(2)}) collective-permute-start(bf16[192,256]{1,0:T(8,128)(2,1)} %bitcast.14), channel_id=1, source_target_pairs={{0,2},{1,3},{2,0},{3,1},{4,6},{5,7},{6,4},{7,5},{8,10},{9,11},{10,... | collective-permute-start | bytes 294920 | tf_op jit(solution)/shard_map/ppermute | solution.py:16
  3.7 0.7 collective-permute-start.3
  4.4 2.2 %shard_map.84 = (bf16[1024,2048]{1,0:T(8,128)(2,1)S(1)}, bf16[192,256]{1,0:T(8,128)(2,1)S(1)}, f32[1,1024]{1,0:T(1,128)S(1)}) custom-call(bf16[1024,2048]{1,0:T(8,128)(2,1)} %bitcast.7, bf16[192,256]{1,0:T(8,128)(2,1)} %bitcast.15, f32[1,1024]{1,0:T(1,128)} %refs_2_.1), custom_call_target="tpu_custom_call" | custom-call | bytes 8593408 | tf_op jit(solution)/shard_map/pallas_call | solution.py:240
  6.6 0.7 collective-permute-done.x2
  7.3 0.6 shard_map.85.before
  7.9 0.7 collective-permute-done.2.x3
  8.6 0.6 shard_map.86
  9.2 1.9 %collective-permute-start.7 = (bf16[208,512]{1,0:T(8,128)(2,1)S(1)}, bf16[208,512]{1,0:T(8,128)(2,1)S(1)}, u32[]{:S(2)}, u32[]{:S(2)}) collective-permute-start(bf16[208,512]{1,0:T(8,128)(2,1)S(1)} %get-tuple-element.75), channel_id=1, source_target_pairs={{0,4},{4,0},{8,12},{12,8},{16,20},{20,16},{24,28},{28,24},{1,5},{5... | collective-permute-start | bytes 638984 | tf_op jit(solution)/shard_map/ppermute | solution.py:16
  11.1 1.6 %collective-permute-start.8 = (bf16[208,512]{1,0:T(8,128)(2,1)S(1)}, bf16[208,512]{1,0:T(8,128)(2,1)S(1)}, u32[]{:S(2)}, u32[]{:S(2)}) collective-permute-start(bf16[208,512]{1,0:T(8,128)(2,1)S(1)} %get-tuple-element.76), channel_id=1, source_target_pairs={{0,8},{4,12},{8,0},{12,4},{16,24},{20,28},{24,16},{28,20},{1,9},{5... | collective-permute-start | bytes 638984 | tf_op jit(solution)/shard_map/ppermute | solution.py:16
  12.7 0.1 collective-permute-start.9
  12.8 2.3 %shard_map.87 = (bf16[2048,1024]{1,0:T(8,128)(2,1)S(1)}, bf16[192,1024]{1,0:T(8,128)(2,1)S(1)}) custom-call(bf16[2048,1024]{1,0:T(8,128)(2,1)} %bitcast.9, bf16[192,1024]{1,0:T(8,128)(2,1)} %bitcast.12), custom_call_target="tpu_custom_call" | custom-call | bytes 9175040 | tf_op jit(solution)/shard_map/pallas_call | solution.py:240
  15.1 1.6 %shard_map.88 = (f32[192,512]{1,0:T(8,128)S(1)}, bf16[192,512]{1,0:T(8,128)(2,1)S(1)}, bf16[192,512]{1,0:T(8,128)(2,1)S(1)}, bf16[192,512]{1,0:T(8,128)(2,1)S(1)}, bf16[192,1024]{1,0:T(8,128)(2,1)S(1)}) custom-call(bf16[192,1024]{1,0:T(8,128)(2,1)S(1)} %get-tuple-element.68.cot, bf16[192,1024]{1,0:T(8,128)(2,1)S(1)} %collective-permute-done.3.sent, ...), custom_call_target="tpu_custom_call" | custom-call | flops 805306368 | bytes 4980736 | tf_op jit(solution)/shard_map/pallas_call | solution.py:195
  16.6 1.9 %collective-permute-start.4 = (bf16[192,512]{1,0:T(8,128)(2,1)S(1)}, bf16[192,512]{1,0:T(8,128)(2,1)S(1)}, u32[]{:S(2)}, u32[]{:S(2)}) collective-permute-start(bf16[192,512]{1,0:T(8,128)(2,1)S(1)} %get-tuple-element.71), channel_id=1, source_target_pairs={{0,4},{4,0},{8,12},{12,8},{16,20},{20,16},{24,28},{28,24},{1,5},{5... | collective-permute-start | bytes 589832 | tf_op jit(solution)/shard_map/ppermute | solution.py:16
  18.5 1.6 %collective-permute-start.5 = (bf16[192,512]{1,0:T(8,128)(2,1)S(1)}, bf16[192,512]{1,0:T(8,128)(2,1)S(1)}, u32[]{:S(2)}, u32[]{:S(2)}) collective-permute-start(bf16[192,512]{1,0:T(8,128)(2,1)S(1)} %get-tuple-element.72), channel_id=1, source_target_pairs={{0,8},{4,12},{8,0},{12,4},{16,24},{20,28},{24,16},{28,20},{1,9},{5... | collective-permute-start | bytes 589832 | tf_op jit(solution)/shard_map/ppermute | solution.py:16
  20.2 3.3 %collective-permute-done.9.g3 = bf16[208,512]{1,0:T(8,128)(2,1)S(1)} collective-permute-done((bf16[208,512]{1,0:T(8,128)(2,1)S(1)}, bf16[208,512]{1,0:T(8,128)(2,1)S(1)}, u32[]{:S(2)}, u32[]{:S(2)}) %collective-permute-start.9) | collective-permute-done | bytes 213024 | tf_op jit(solution)/shard_map/ppermute | solution.py:16
  23.5 0.6 shard_map.89
  24.1 3.4 %collective-permute-done.4.g1 = bf16[192,512]{1,0:T(8,128)(2,1)S(1)} collective-permute-done((bf16[192,512]{1,0:T(8,128)(2,1)S(1)}, bf16[192,512]{1,0:T(8,128)(2,1)S(1)}, u32[]{:S(2)}, u32[]{:S(2)}) %collective-permute-start.4) | collective-permute-done | bytes 196640 | tf_op jit(solution)/shard_map/ppermute | solution.py:16
  27.5 0.5 collective-permute-done.5.g2
  28.1 2.9 %collective-permute-done.6.g3 = bf16[192,512]{1,0:T(8,128)(2,1)S(1)} collective-permute-done((bf16[192,512]{1,0:T(8,128)(2,1)S(1)}, bf16[192,512]{1,0:T(8,128)(2,1)S(1)}, u32[]{:S(2)}, u32[]{:S(2)}) %collective-permute-start.6) | collective-permute-done | bytes 196640 | tf_op jit(solution)/shard_map/ppermute | solution.py:16
  31.0 0.2 shard_map.90.refs_0_.p0
  31.2 2.7 %collective-permute-start.12 = (bf16[208,512]{1,0:T(8,128)(2,1)S(1)}, bf16[208,512]{1,0:T(8,128)(2,1)S(1)}, u32[]{:S(2)}, u32[]{:S(2)}) collective-permute-start(bf16[208,512]{1,0:T(8,128)(2,1)S(1)} %shard_map.90.refs_0_.p0), channel_id=1, source_target_pairs={{0,12},{4,8},{8,4},{12,0},{16,28},{20,24},{24,20},{28,16},{1,13},{... | collective-permute-start | bytes 638984 | tf_op jit(solution)/shard_map/ppermute | solution.py:16
  33.9 0.5 collective-permute-start.11
  34.4 0.4 collective-permute-start.10
  34.8 0.5 shard_map.91.refs_3_
  35.3 5.1 %collective-permute-done.12.refs_0_.p3 = bf16[208,512]{1,0:T(8,128)(2,1)S(1)} collective-permute-done((bf16[208,512]{1,0:T(8,128)(2,1)S(1)}, bf16[208,512]{1,0:T(8,128)(2,1)S(1)}, u32[]{:S(2)}, u32[]{:S(2)}) %collective-permute-start.12) | collective-permute-done | bytes 213024 | tf_op jit(solution)/shard_map/ppermute | solution.py:16
  40.4 2.8 %collective-permute-done.11.refs_1_.p2 = bf16[208,512]{1,0:T(8,128)(2,1)S(1)} collective-permute-done((bf16[208,512]{1,0:T(8,128)(2,1)S(1)}, bf16[208,512]{1,0:T(8,128)(2,1)S(1)}, u32[]{:S(2)}, u32[]{:S(2)}) %collective-permute-start.11) | collective-permute-done | bytes 213024 | tf_op jit(solution)/shard_map/ppermute | solution.py:16
  43.1 0.8 shard_map.92.earlier
  44.0 0.5 shard_map.93
  44.6 1.5 %collective-permute-done.13.got = bf16[208,512]{1,0:T(8,128)(2,1)S(1)} collective-permute-done((bf16[208,512]{1,0:T(8,128)(2,1)S(1)}, bf16[208,512]{1,0:T(8,128)(2,1)S(1)}, u32[]{:S(2)}, u32[]{:S(2)}) %collective-permute-start.13) | collective-permute-done | bytes 213024 | tf_op jit(solution)/shard_map/ppermute | solution.py:16
  46.1 1.6 %collective-permute-start.14 = (bf16[208,256]{1,0:T(8,128)(2,1)S(1)}, bf16[208,256]{1,0:T(8,128)(2,1)S(1)}, u32[]{:S(2)}, u32[]{:S(2)}) collective-permute-start(bf16[208,256]{1,0:T(8,128)(2,1)S(1)} %get-tuple-element.85), channel_id=1, source_target_pairs={{0,2},{1,3},{2,0},{3,1},{4,6},{5,7},{6,4},{7,5},{8,10},{9,11},{10,... | collective-permute-start | bytes 319496 | tf_op jit(solution)/shard_map/ppermute | solution.py:16
  47.7 3.5 %collective-permute-done.14.got = bf16[208,256]{1,0:T(8,128)(2,1)S(1)} collective-permute-done((bf16[208,256]{1,0:T(8,128)(2,1)S(1)}, bf16[208,256]{1,0:T(8,128)(2,1)S(1)}, u32[]{:S(2)}, u32[]{:S(2)}) %collective-permute-start.14) | collective-permute-done | bytes 106528 | tf_op jit(solution)/shard_map/ppermute | solution.py:16
  51.2 0.2 shard_map.95
  51.4 1.3 %collective-permute-start.15 = (bf16[192,256]{1,0:T(8,128)(2,1)S(1)}, bf16[192,256]{1,0:T(8,128)(2,1)S(1)}, u32[]{:S(2)}, u32[]{:S(2)}) collective-permute-start(bf16[192,256]{1,0:T(8,128)(2,1)S(1)} %shard_map.95), channel_id=1, source_target_pairs={{16,0},{20,4},{24,8},{28,12},{17,1},{21,5},{25,9},{29,13},{18,2},{... | collective-permute-start | bytes 294920 | tf_op jit(solution)/shard_map/ppermute | solution.py:590
  52.7 1.6 %collective-permute-start.21 = (bf16[192,512]{1,0:T(8,128)(2,1)S(1)}, bf16[192,512]{1,0:T(8,128)(2,1)S(1)}, u32[]{:S(2)}, u32[]{:S(2)}) collective-permute-start(bf16[192,512]{1,0:T(8,128)(2,1)S(1)} %get-tuple-element.91.h0), channel_id=1, source_target_pairs={{0,12},{4,8},{8,4},{12,0},{16,28},{20,24},{24,20},{28,16},{1,13},{... | collective-permute-start | bytes 589832 | tf_op jit(solution)/shard_map/ppermute | solution.py:16
  54.3 0.5 collective-permute-start.20
  54.7 1.5 %collective-permute-start.19 = (bf16[192,512]{1,0:T(8,128)(2,1)S(1)}, bf16[192,512]{1,0:T(8,128)(2,1)S(1)}, u32[]{:S(2)}, u32[]{:S(2)}) collective-permute-start(bf16[192,512]{1,0:T(8,128)(2,1)S(1)} %get-tuple-element.91.h0), channel_id=1, source_target_pairs={{0,4},{4,0},{8,12},{12,8},{16,20},{20,16},{24,28},{28,24},{1,5},{5... | collective-permute-start | bytes 589832 | tf_op jit(solution)/shard_map/ppermute | solution.py:16
  56.2 5.4 %collective-permute-done.15.refs_0_.refs_4_ = bf16[192,256]{1,0:T(8,128)(2,1)S(1)} collective-permute-done((bf16[192,256]{1,0:T(8,128)(2,1)S(1)}, bf16[192,256]{1,0:T(8,128)(2,1)S(1)}, u32[]{:S(2)}, u32[]{:S(2)}) %collective-permute-start.15) | collective-permute-done | bytes 98336 | tf_op jit(solution)/shard_map/ppermute | solution.py:590
  61.6 1.4 %collective-permute-start.16 = (bf16[192,256]{1,0:T(8,128)(2,1)S(1)}, bf16[192,256]{1,0:T(8,128)(2,1)S(1)}, u32[]{:S(2)}, u32[]{:S(2)}) collective-permute-start(bf16[192,256]{1,0:T(8,128)(2,1)S(1)} %collective-permute-done.15.refs_0_.refs_4_), channel_id=1, source_target_pairs={{0,2},{1,3},{2,0},{3,1},{4,6},{5,7},{6,4},{7,5},{8,10},{9,11},{10,... | collective-permute-start | bytes 294920 | tf_op jit(solution)/shard_map/ppermute | solution.py:16
  63.0 3.3 %collective-permute-done.16.refs_1_.refs_6_ = bf16[192,256]{1,0:T(8,128)(2,1)S(1)} collective-permute-done((bf16[192,256]{1,0:T(8,128)(2,1)S(1)}, bf16[192,256]{1,0:T(8,128)(2,1)S(1)}, u32[]{:S(2)}, u32[]{:S(2)}) %collective-permute-start.16) | collective-permute-done | bytes 98336 | tf_op jit(solution)/shard_map/ppermute | solution.py:16
  66.3 0.5 shard_map.96.refs_4_
  66.8 0.9 shard_map.97.refs_3_
  67.7 0.8 shard_map.98
  68.5 0.6 collective-permute-start.22
  69.0 3.0 %collective-permute-start.24 = (bf16[192,512]{1,0:T(8,128)(2,1)S(1)}, bf16[192,512]{1,0:T(8,128)(2,1)S(1)}, u32[]{:S(2)}, u32[]{:S(2)}) collective-permute-start(bf16[192,512]{1,0:T(8,128)(2,1)S(1)} %get-tuple-element.99), channel_id=1, source_target_pairs={{0,12},{4,8},{8,4},{12,0},{16,28},{20,24},{24,20},{28,16},{1,13},{... | collective-permute-start | bytes 589832 | tf_op jit(solution)/shard_map/ppermute | solution.py:16
  72.0 2.5 %shard_map.99 = bf16[2048,1024]{1,0:T(8,128)(2,1)} custom-call(bf16[192,512]{1,0:T(8,128)(2,1)S(1)} %get-tuple-element.91.h0, bf16[192,512]{1,0:T(8,128)(2,1)S(1)} %collective-permute-done.19.h1, bf16[192,512]{1,0:T(8,128)(2,1)S(1)} %collective-permute-done.20.h2, bf16[192,512]{1,0:T(8,128)(2,1)S(1)} %collective-permute-done.21.h3, ...), custom_call_target="tpu_custom_call" | custom-call | flops 805306368 | bytes 4194304 | tf_op jit(solution)/shard_map/pallas_call | solution.py:474
  74.5 1.3 %collective-permute-done.22.g1 = bf16[192,512]{1,0:T(8,128)(2,1)S(1)} collective-permute-done((bf16[192,512]{1,0:T(8,128)(2,1)S(1)}, bf16[192,512]{1,0:T(8,128)(2,1)S(1)}, u32[]{:S(2)}, u32[]{:S(2)}) %collective-permute-start.22) | collective-permute-done | bytes 196640 | tf_op jit(solution)/shard_map/ppermute | solution.py:16
  75.8 0.9 collective-permute-done.23.g2
  76.8 4.5 %collective-permute-done.24.g3 = bf16[192,512]{1,0:T(8,128)(2,1)S(1)} collective-permute-done((bf16[192,512]{1,0:T(8,128)(2,1)S(1)}, bf16[192,512]{1,0:T(8,128)(2,1)S(1)}, u32[]{:S(2)}, u32[]{:S(2)}) %collective-permute-start.24) | collective-permute-done | bytes 196640 | tf_op jit(solution)/shard_map/ppermute | solution.py:16
  81.2 0.2 shard_map.100.refs_0_.p0
  81.5 0.3 collective-permute-start.27
  81.8 1.7 %collective-permute-start.26 = (bf16[208,512]{1,0:T(8,128)(2,1)S(1)}, bf16[208,512]{1,0:T(8,128)(2,1)S(1)}, u32[]{:S(2)}, u32[]{:S(2)}) collective-permute-start(bf16[208,512]{1,0:T(8,128)(2,1)S(1)} %shard_map.100.refs_0_.p0), channel_id=1, source_target_pairs={{0,8},{4,12},{8,0},{12,4},{16,24},{20,28},{24,16},{28,20},{1,9},{5... | collective-permute-start | bytes 638984 | tf_op jit(solution)/shard_map/ppermute | solution.py:16
  83.5 1.5 %collective-permute-start.25 = (bf16[208,512]{1,0:T(8,128)(2,1)S(1)}, bf16[208,512]{1,0:T(8,128)(2,1)S(1)}, u32[]{:S(2)}, u32[]{:S(2)}) collective-permute-start(bf16[208,512]{1,0:T(8,128)(2,1)S(1)} %shard_map.100.refs_0_.p0), channel_id=1, source_target_pairs={{0,4},{4,0},{8,12},{12,8},{16,20},{20,16},{24,28},{28,24},{1,5},{5... | collective-permute-start | bytes 638984 | tf_op jit(solution)/shard_map/ppermute | solution.py:16
  85.0 0.5 shard_map.101.refs_3_
  85.5 5.1 %collective-permute-done.27.refs_0_.p3 = bf16[208,512]{1,0:T(8,128)(2,1)S(1)} collective-permute-done((bf16[208,512]{1,0:T(8,128)(2,1)S(1)}, bf16[208,512]{1,0:T(8,128)(2,1)S(1)}, u32[]{:S(2)}, u32[]{:S(2)}) %collective-permute-start.27) | collective-permute-done | bytes 213024 | tf_op jit(solution)/shard_map/ppermute | solution.py:16
  90.7 1.9 %collective-permute-done.26.refs_1_.p2 = bf16[208,512]{1,0:T(8,128)(2,1)S(1)} collective-permute-done((bf16[208,512]{1,0:T(8,128)(2,1)S(1)}, bf16[208,512]{1,0:T(8,128)(2,1)S(1)}, u32[]{:S(2)}, u32[]{:S(2)}) %collective-permute-start.26) | collective-permute-done | bytes 213024 | tf_op jit(solution)/shard_map/ppermute | solution.py:16
  92.6 0.8 shard_map.102.earlier
  93.5 0.1 collective-permute-done.25.p1
  93.6 0.5 shard_map.103
  94.2 1.4 %collective-permute-done.28.got = bf16[208,512]{1,0:T(8,128)(2,1)S(1)} collective-permute-done((bf16[208,512]{1,0:T(8,128)(2,1)S(1)}, bf16[208,512]{1,0:T(8,128)(2,1)S(1)}, u32[]{:S(2)}, u32[]{:S(2)}) %collective-permute-start.28) | collective-permute-done | bytes 213024 | tf_op jit(solution)/shard_map/ppermute | solution.py:16
  95.7 1.4 %collective-permute-start.29 = (bf16[208,256]{1,0:T(8,128)(2,1)S(1)}, bf16[208,256]{1,0:T(8,128)(2,1)S(1)}, u32[]{:S(2)}, u32[]{:S(2)}) collective-permute-start(bf16[208,256]{1,0:T(8,128)(2,1)S(1)} %get-tuple-element.102), channel_id=1, source_target_pairs={{0,2},{1,3},{2,0},{3,1},{4,6},{5,7},{6,4},{7,5},{8,10},{9,11},{10,... | collective-permute-start | bytes 319496 | tf_op jit(solution)/shard_map/ppermute | solution.py:16
  97.0 2.6 %shard_map.105 = bf16[1024,2048]{1,0:T(8,128)(2,1)} custom-call(bf16[208,512]{1,0:T(8,128)(2,1)S(1)} %shard_map.100.refs_0_.p0, bf16[208,512]{1,0:T(8,128)(2,1)S(1)} %collective-permute-done.25.p1, bf16[208,512]{1,0:T(8,128)(2,1)S(1)} %collective-permute-done.26.refs_1_.p2, bf16[208,512]{1,0:T(8,128)(2,1)S(1)} %collective-permute-done.27.refs_0_.p3, ...), custom_call_target="tpu_custom_call" | custom-call | flops 805306368 | bytes 4194304 | tf_op jit(solution)/shard_map/pallas_call | solution.py:474
  99.7 1.1 %collective-permute-done.29.got = bf16[208,256]{1,0:T(8,128)(2,1)S(1)} collective-permute-done((bf16[208,256]{1,0:T(8,128)(2,1)S(1)}, bf16[208,256]{1,0:T(8,128)(2,1)S(1)}, u32[]{:S(2)}, u32[]{:S(2)}) %collective-permute-start.29) | collective-permute-done | bytes 106528 | tf_op jit(solution)/shard_map/ppermute | solution.py:16
  100.7 0.8 shard_map.106
  (19 shorter events, 0.4 us)
Async XLA Ops:
  0.6 6.0 %collective-permute-start.1 = (bf16[192,256]{1,0:T(8,128)(2,1)}, bf16[192,256]{1,0:T(8,128)(2,1)S(1)}, u32[]{:S(2)}, u32[]{:S(2)}) collective-permute-start(bf16[192,256]{1,0:T(8,128)(2,1)} %bitcast.13), channel_id=1, source_target_pairs={{0,1},{1,0},{2,3},{3,2},{4,5},{5,4},{6,7},{7,6},{8,9},{9,8},{10,11... | collective-permute-start | bytes 294920 | tf_op jit(solution)/shard_map/ppermute | solution.py:16
  1.1 6.2 %collective-permute-start = (bf16[192,256]{1,0:T(8,128)(2,1)}, bf16[192,256]{1,0:T(8,128)(2,1)S(1)}, u32[]{:S(2)}, u32[]{:S(2)}) collective-permute-start(bf16[192,256]{1,0:T(8,128)(2,1)} %bitcast.14), channel_id=1, source_target_pairs={{0,2},{1,3},{2,0},{3,1},{4,6},{5,7},{6,4},{7,5},{8,10},{9,11},{10,... | collective-permute-start | bytes 294920 | tf_op jit(solution)/shard_map/ppermute | solution.py:16
  3.7 11.4 %collective-permute-start.3 = (bf16[192,1024]{1,0:T(8,128)(2,1)}, bf16[192,1024]{1,0:T(8,128)(2,1)S(1)}, u32[]{:S(2)}, u32[]{:S(2)}) collective-permute-start(bf16[192,1024]{1,0:T(8,128)(2,1)} %bitcast.11), channel_id=1, source_target_pairs={{20,17},{16,18},{24,19},{17,20},{29,22},{21,23},{26,24},{18,25},{3... | collective-permute-start | bytes 1179656 | tf_op jit(solution)/shard_map/ppermute | solution.py:506
  7.3 1.3 %collective-permute-start.2 = (bf16[192,256]{1,0:T(8,128)(2,1)S(1)}, bf16[192,256]{1,0:T(8,128)(2,1)S(1)}, u32[]{:S(2)}, u32[]{:S(2)}) collective-permute-start(bf16[192,256]{1,0:T(8,128)(2,1)S(1)} %collective-permute-done.x2), channel_id=1, source_target_pairs={{0,1},{1,0},{2,3},{3,2},{4,5},{5,4},{6,7},{7,6},{8,9},{9,8},{10,11... | collective-permute-start | bytes 294920 | tf_op jit(solution)/shard_map/ppermute | solution.py:16
  9.2 10.9 %collective-permute-start.7 = (bf16[208,512]{1,0:T(8,128)(2,1)S(1)}, bf16[208,512]{1,0:T(8,128)(2,1)S(1)}, u32[]{:S(2)}, u32[]{:S(2)}) collective-permute-start(bf16[208,512]{1,0:T(8,128)(2,1)S(1)} %get-tuple-element.75), channel_id=1, source_target_pairs={{0,4},{4,0},{8,12},{12,8},{16,20},{20,16},{24,28},{28,24},{1,5},{5... | collective-permute-start | bytes 638984 | tf_op jit(solution)/shard_map/ppermute | solution.py:16
  11.1 9.1 %collective-permute-start.8 = (bf16[208,512]{1,0:T(8,128)(2,1)S(1)}, bf16[208,512]{1,0:T(8,128)(2,1)S(1)}, u32[]{:S(2)}, u32[]{:S(2)}) collective-permute-start(bf16[208,512]{1,0:T(8,128)(2,1)S(1)} %get-tuple-element.76), channel_id=1, source_target_pairs={{0,8},{4,12},{8,0},{12,4},{16,24},{20,28},{24,16},{28,20},{1,9},{5... | collective-permute-start | bytes 638984 | tf_op jit(solution)/shard_map/ppermute | solution.py:16
  12.7 10.8 %collective-permute-start.9 = (bf16[208,512]{1,0:T(8,128)(2,1)S(1)}, bf16[208,512]{1,0:T(8,128)(2,1)S(1)}, u32[]{:S(2)}, u32[]{:S(2)}) collective-permute-start(bf16[208,512]{1,0:T(8,128)(2,1)S(1)} %get-tuple-element.77), channel_id=1, source_target_pairs={{0,12},{4,8},{8,4},{12,0},{16,28},{20,24},{24,20},{28,16},{1,13},{... | collective-permute-start | bytes 638984 | tf_op jit(solution)/shard_map/ppermute | solution.py:16
  16.6 10.9 %collective-permute-start.4 = (bf16[192,512]{1,0:T(8,128)(2,1)S(1)}, bf16[192,512]{1,0:T(8,128)(2,1)S(1)}, u32[]{:S(2)}, u32[]{:S(2)}) collective-permute-start(bf16[192,512]{1,0:T(8,128)(2,1)S(1)} %get-tuple-element.71), channel_id=1, source_target_pairs={{0,4},{4,0},{8,12},{12,8},{16,20},{20,16},{24,28},{28,24},{1,5},{5... | collective-permute-start | bytes 589832 | tf_op jit(solution)/shard_map/ppermute | solution.py:16
  18.5 9.5 %collective-permute-start.5 = (bf16[192,512]{1,0:T(8,128)(2,1)S(1)}, bf16[192,512]{1,0:T(8,128)(2,1)S(1)}, u32[]{:S(2)}, u32[]{:S(2)}) collective-permute-start(bf16[192,512]{1,0:T(8,128)(2,1)S(1)} %get-tuple-element.72), channel_id=1, source_target_pairs={{0,8},{4,12},{8,0},{12,4},{16,24},{20,28},{24,16},{28,20},{1,9},{5... | collective-permute-start | bytes 589832 | tf_op jit(solution)/shard_map/ppermute | solution.py:16
  20.1 10.9 %collective-permute-start.6 = (bf16[192,512]{1,0:T(8,128)(2,1)S(1)}, bf16[192,512]{1,0:T(8,128)(2,1)S(1)}, u32[]{:S(2)}, u32[]{:S(2)}) collective-permute-start(bf16[192,512]{1,0:T(8,128)(2,1)S(1)} %get-tuple-element.73), channel_id=1, source_target_pairs={{0,12},{4,8},{8,4},{12,0},{16,28},{20,24},{24,20},{28,16},{1,13},{... | collective-permute-start | bytes 589832 | tf_op jit(solution)/shard_map/ppermute | solution.py:16
  31.2 9.2 %collective-permute-start.12 = (bf16[208,512]{1,0:T(8,128)(2,1)S(1)}, bf16[208,512]{1,0:T(8,128)(2,1)S(1)}, u32[]{:S(2)}, u32[]{:S(2)}) collective-permute-start(bf16[208,512]{1,0:T(8,128)(2,1)S(1)} %shard_map.90.refs_0_.p0), channel_id=1, source_target_pairs={{0,12},{4,8},{8,4},{12,0},{16,28},{20,24},{24,20},{28,16},{1,13},{... | collective-permute-start | bytes 638984 | tf_op jit(solution)/shard_map/ppermute | solution.py:16
  33.9 9.2 %collective-permute-start.11 = (bf16[208,512]{1,0:T(8,128)(2,1)S(1)}, bf16[208,512]{1,0:T(8,128)(2,1)S(1)}, u32[]{:S(2)}, u32[]{:S(2)}) collective-permute-start(bf16[208,512]{1,0:T(8,128)(2,1)S(1)} %shard_map.90.refs_0_.p0), channel_id=1, source_target_pairs={{0,8},{4,12},{8,0},{12,4},{16,24},{20,28},{24,16},{28,20},{1,9},{5... | collective-permute-start | bytes 638984 | tf_op jit(solution)/shard_map/ppermute | solution.py:16
  34.4 9.6 %collective-permute-start.10 = (bf16[208,512]{1,0:T(8,128)(2,1)S(1)}, bf16[208,512]{1,0:T(8,128)(2,1)S(1)}, u32[]{:S(2)}, u32[]{:S(2)}) collective-permute-start(bf16[208,512]{1,0:T(8,128)(2,1)S(1)} %shard_map.90.refs_0_.p0), channel_id=1, source_target_pairs={{0,4},{4,0},{8,12},{12,8},{16,20},{20,16},{24,28},{28,24},{1,5},{5... | collective-permute-start | bytes 638984 | tf_op jit(solution)/shard_map/ppermute | solution.py:16
  44.5 1.5 %collective-permute-start.13 = (bf16[208,512]{1,0:T(8,128)(2,1)S(1)}, bf16[208,512]{1,0:T(8,128)(2,1)S(1)}, u32[]{:S(2)}, u32[]{:S(2)}) collective-permute-start(bf16[208,512]{1,0:T(8,128)(2,1)S(1)} %get-tuple-element.81), channel_id=1, source_target_pairs={{0,1},{1,0},{2,3},{3,2},{4,5},{5,4},{6,7},{7,6},{8,9},{9,8},{10,11... | collective-permute-start | bytes 638984 | tf_op jit(solution)/shard_map/ppermute | solution.py:16
  46.1 5.1 %collective-permute-start.14 = (bf16[208,256]{1,0:T(8,128)(2,1)S(1)}, bf16[208,256]{1,0:T(8,128)(2,1)S(1)}, u32[]{:S(2)}, u32[]{:S(2)}) collective-permute-start(bf16[208,256]{1,0:T(8,128)(2,1)S(1)} %get-tuple-element.85), channel_id=1, source_target_pairs={{0,2},{1,3},{2,0},{3,1},{4,6},{5,7},{6,4},{7,5},{8,10},{9,11},{10,... | collective-permute-start | bytes 319496 | tf_op jit(solution)/shard_map/ppermute | solution.py:16
  51.4 10.2 %collective-permute-start.15 = (bf16[192,256]{1,0:T(8,128)(2,1)S(1)}, bf16[192,256]{1,0:T(8,128)(2,1)S(1)}, u32[]{:S(2)}, u32[]{:S(2)}) collective-permute-start(bf16[192,256]{1,0:T(8,128)(2,1)S(1)} %shard_map.95), channel_id=1, source_target_pairs={{16,0},{20,4},{24,8},{28,12},{17,1},{21,5},{25,9},{29,13},{18,2},{... | collective-permute-start | bytes 294920 | tf_op jit(solution)/shard_map/ppermute | solution.py:590
  52.7 13.6 %collective-permute-start.21 = (bf16[192,512]{1,0:T(8,128)(2,1)S(1)}, bf16[192,512]{1,0:T(8,128)(2,1)S(1)}, u32[]{:S(2)}, u32[]{:S(2)}) collective-permute-start(bf16[192,512]{1,0:T(8,128)(2,1)S(1)} %get-tuple-element.91.h0), channel_id=1, source_target_pairs={{0,12},{4,8},{8,4},{12,0},{16,28},{20,24},{24,20},{28,16},{1,13},{... | collective-permute-start | bytes 589832 | tf_op jit(solution)/shard_map/ppermute | solution.py:16
  54.3 12.0 %collective-permute-start.20 = (bf16[192,512]{1,0:T(8,128)(2,1)S(1)}, bf16[192,512]{1,0:T(8,128)(2,1)S(1)}, u32[]{:S(2)}, u32[]{:S(2)}) collective-permute-start(bf16[192,512]{1,0:T(8,128)(2,1)S(1)} %get-tuple-element.91.h0), channel_id=1, source_target_pairs={{0,8},{4,12},{8,0},{12,4},{16,24},{20,28},{24,16},{28,20},{1,9},{5... | collective-permute-start | bytes 589832 | tf_op jit(solution)/shard_map/ppermute | solution.py:16
  54.7 11.5 %collective-permute-start.19 = (bf16[192,512]{1,0:T(8,128)(2,1)S(1)}, bf16[192,512]{1,0:T(8,128)(2,1)S(1)}, u32[]{:S(2)}, u32[]{:S(2)}) collective-permute-start(bf16[192,512]{1,0:T(8,128)(2,1)S(1)} %get-tuple-element.91.h0), channel_id=1, source_target_pairs={{0,4},{4,0},{8,12},{12,8},{16,20},{20,16},{24,28},{28,24},{1,5},{5... | collective-permute-start | bytes 589832 | tf_op jit(solution)/shard_map/ppermute | solution.py:16
  61.6 4.7 %collective-permute-start.16 = (bf16[192,256]{1,0:T(8,128)(2,1)S(1)}, bf16[192,256]{1,0:T(8,128)(2,1)S(1)}, u32[]{:S(2)}, u32[]{:S(2)}) collective-permute-start(bf16[192,256]{1,0:T(8,128)(2,1)S(1)} %collective-permute-done.15.refs_0_.refs_4_), channel_id=1, source_target_pairs={{0,2},{1,3},{2,0},{3,1},{4,6},{5,7},{6,4},{7,5},{8,10},{9,11},{10,... | collective-permute-start | bytes 294920 | tf_op jit(solution)/shard_map/ppermute | solution.py:16
  63.0 3.8 %collective-permute-start.18 = (bf16[192,256]{1,0:T(8,128)(2,1)S(1)}, bf16[192,256]{1,0:T(8,128)(2,1)S(1)}, u32[]{:S(2)}, u32[]{:S(2)}) collective-permute-start(bf16[192,256]{1,0:T(8,128)(2,1)S(1)} %collective-permute-done.15.refs_0_.refs_4_), channel_id=1, source_target_pairs={{0,1},{1,0},{2,3},{3,2},{4,5},{5,4},{6,7},{7,6},{8,9},{9,8},{10,11... | collective-permute-start | bytes 294920 | tf_op jit(solution)/shard_map/ppermute | solution.py:16
  66.3 1.4 %collective-permute-start.17 = (bf16[192,256]{1,0:T(8,128)(2,1)S(1)}, bf16[192,256]{1,0:T(8,128)(2,1)S(1)}, u32[]{:S(2)}, u32[]{:S(2)}) collective-permute-start(bf16[192,256]{1,0:T(8,128)(2,1)S(1)} %collective-permute-done.16.refs_1_.refs_6_), channel_id=1, source_target_pairs={{0,1},{1,0},{2,3},{3,2},{4,5},{5,4},{6,7},{7,6},{8,9},{9,8},{10,11... | collective-permute-start | bytes 294920 | tf_op jit(solution)/shard_map/ppermute | solution.py:16
  68.5 7.4 %collective-permute-start.22 = (bf16[192,512]{1,0:T(8,128)(2,1)S(1)}, bf16[192,512]{1,0:T(8,128)(2,1)S(1)}, u32[]{:S(2)}, u32[]{:S(2)}) collective-permute-start(bf16[192,512]{1,0:T(8,128)(2,1)S(1)} %get-tuple-element.97), channel_id=1, source_target_pairs={{0,4},{4,0},{8,12},{12,8},{16,20},{20,16},{24,28},{28,24},{1,5},{5... | collective-permute-start | bytes 589832 | tf_op jit(solution)/shard_map/ppermute | solution.py:16
  69.0 7.7 %collective-permute-start.23 = (bf16[192,512]{1,0:T(8,128)(2,1)S(1)}, bf16[192,512]{1,0:T(8,128)(2,1)S(1)}, u32[]{:S(2)}, u32[]{:S(2)}) collective-permute-start(bf16[192,512]{1,0:T(8,128)(2,1)S(1)} %get-tuple-element.98), channel_id=1, source_target_pairs={{0,8},{4,12},{8,0},{12,4},{16,24},{20,28},{24,16},{28,20},{1,9},{5... | collective-permute-start | bytes 589832 | tf_op jit(solution)/shard_map/ppermute | solution.py:16
  69.0 12.2 %collective-permute-start.24 = (bf16[192,512]{1,0:T(8,128)(2,1)S(1)}, bf16[192,512]{1,0:T(8,128)(2,1)S(1)}, u32[]{:S(2)}, u32[]{:S(2)}) collective-permute-start(bf16[192,512]{1,0:T(8,128)(2,1)S(1)} %get-tuple-element.99), channel_id=1, source_target_pairs={{0,12},{4,8},{8,4},{12,0},{16,28},{20,24},{24,20},{28,16},{1,13},{... | collective-permute-start | bytes 589832 | tf_op jit(solution)/shard_map/ppermute | solution.py:16
  81.5 9.2 %collective-permute-start.27 = (bf16[208,512]{1,0:T(8,128)(2,1)S(1)}, bf16[208,512]{1,0:T(8,128)(2,1)S(1)}, u32[]{:S(2)}, u32[]{:S(2)}) collective-permute-start(bf16[208,512]{1,0:T(8,128)(2,1)S(1)} %shard_map.100.refs_0_.p0), channel_id=1, source_target_pairs={{0,12},{4,8},{8,4},{12,0},{16,28},{20,24},{24,20},{28,16},{1,13},{... | collective-permute-start | bytes 638984 | tf_op jit(solution)/shard_map/ppermute | solution.py:16
  81.8 10.8 %collective-permute-start.26 = (bf16[208,512]{1,0:T(8,128)(2,1)S(1)}, bf16[208,512]{1,0:T(8,128)(2,1)S(1)}, u32[]{:S(2)}, u32[]{:S(2)}) collective-permute-start(bf16[208,512]{1,0:T(8,128)(2,1)S(1)} %shard_map.100.refs_0_.p0), channel_id=1, source_target_pairs={{0,8},{4,12},{8,0},{12,4},{16,24},{20,28},{24,16},{28,20},{1,9},{5... | collective-permute-start | bytes 638984 | tf_op jit(solution)/shard_map/ppermute | solution.py:16
  83.5 10.1 %collective-permute-start.25 = (bf16[208,512]{1,0:T(8,128)(2,1)S(1)}, bf16[208,512]{1,0:T(8,128)(2,1)S(1)}, u32[]{:S(2)}, u32[]{:S(2)}) collective-permute-start(bf16[208,512]{1,0:T(8,128)(2,1)S(1)} %shard_map.100.refs_0_.p0), channel_id=1, source_target_pairs={{0,4},{4,0},{8,12},{12,8},{16,20},{20,16},{24,28},{28,24},{1,5},{5... | collective-permute-start | bytes 638984 | tf_op jit(solution)/shard_map/ppermute | solution.py:16
  94.1 1.5 %collective-permute-start.28 = (bf16[208,512]{1,0:T(8,128)(2,1)S(1)}, bf16[208,512]{1,0:T(8,128)(2,1)S(1)}, u32[]{:S(2)}, u32[]{:S(2)}) collective-permute-start(bf16[208,512]{1,0:T(8,128)(2,1)S(1)} %get-tuple-element.101), channel_id=1, source_target_pairs={{0,1},{1,0},{2,3},{3,2},{4,5},{5,4},{6,7},{7,6},{8,9},{9,8},{10,11... | collective-permute-start | bytes 638984 | tf_op jit(solution)/shard_map/ppermute | solution.py:16
  95.7 5.1 %collective-permute-start.29 = (bf16[208,256]{1,0:T(8,128)(2,1)S(1)}, bf16[208,256]{1,0:T(8,128)(2,1)S(1)}, u32[]{:S(2)}, u32[]{:S(2)}) collective-permute-start(bf16[208,256]{1,0:T(8,128)(2,1)S(1)} %get-tuple-element.102), channel_id=1, source_target_pairs={{0,2},{1,3},{2,0},{3,1},{4,6},{5,7},{6,4},{7,5},{8,10},{9,11},{10,... | collective-permute-start | bytes 319496 | tf_op jit(solution)/shard_map/ppermute | solution.py:16

commit v2 on v1

--- a/solution.py
+++ b/solution.py
@@ -181,6 +181,7 @@
 
 
 SIDE = 16
+LANES = 128
 GELU_IN = 0.7978845608028654
 GELU_CUBE = 0.044715
 
@@ -227,6 +228,35 @@
     return wide[0:1] + wide[1:2]
 
 
+def packed_shape(rows, piece):
+    return (piece // LANES * rows + SIDE, LANES)
+
+
+def pack_block(row):
+    lead = row.astype(BF16).astype(F32)
+    count = row.shape[1] // LANES
+    at = lax.broadcasted_iota(jnp.int32, (SIDE, LANES), 0)
+    block = jnp.zeros((SIDE, LANES), F32)
+    for i in range(count):
+        lanes = slice(i * LANES, (i + 1) * LANES)
+        block = jnp.where(at == i, lead[:, lanes], jnp.where(at == count + i, (row - lead)[:, lanes], block))
+    return block.astype(BF16)
+
+
+def pack_row(block, count):
+    wide = block.astype(F32)
+    return jnp.concatenate([wide[i:i + 1] + wide[count + i:count + i + 1] for i in range(count)], axis=1)
+
+
+def lane_blocks(rows):
+    return -(-rows // LANES)
+
+
+def unpack(packed, rows):
+    blocks = (packed.shape[0] - SIDE) // rows
+    return jnp.concatenate([packed[i * rows:(i + 1) * rows] for i in range(blocks)], axis=1)
+
+
 def load_kernel(*refs):
     count = len(refs) // 2
     copies = [pltpu.make_async_copy(refs[i], refs[count + i], refs[-1].at[i]) for i in range(count)]
@@ -285,20 +315,21 @@
     spread_in_part(x1, lane ^ 1, gain, weight, mine, total, False)
 
 
-def spread_in_last_kernel(x0, x1, x2, x3, gain, weight, before, own, s1, s2, s3, x_full, total):
+def spread_in_last_kernel(x0, x1, x2, x3, gain, weight, before, own, s1, s2, s3, x_full, squares, total):
     mine, lane = place()
     rows, share = x0.shape
     piece = own.shape[1]
     total[...] = before[...]
     spread_in_part(x2, lane ^ 2, gain, weight, mine, total, False)
     spread_in_part(x3, lane ^ 3, gain, weight, mine, total, False)
-    row = as_row(square_sum(x0) + square_sum(x1) + square_sum(x2) + square_sum(x3), piece)
-    block = side_block(row)
+    column = square_sum(x0) + square_sum(x1) + square_sum(x2) + square_sum(x3)
+    block = pack_block(as_row(column, lane_blocks(rows) * LANES))
     for d, out in ((3, s3), (2, s2), (1, s1)):
-        out[:rows] = total[:, d * piece:(d + 1) * piece].astype(BF16)
-        out[rows:] = block
-    own[:rows] = total[:, :piece]
-    own[rows:] = jnp.broadcast_to(row, (SIDE, piece))
+        for i in range(piece // LANES):
+            out[i * rows:(i + 1) * rows] = total[:, d * piece + i * LANES:d * piece + (i + 1) * LANES].astype(BF16)
+        out[piece // LANES * rows:] = block
+    own[...] = total[:, :piece]
+    squares[...] = column
     for d, part in enumerate((x0, x1, x2, x3)):
         x_full[:, slot(lane ^ d, share)] = part[...]
 
@@ -363,34 +394,42 @@
                 dy[:, slot(lane ^ d, share)] = part[...]
 
 
-def act_kernel(width, own, g1, g2, g3, act, slope, hid, scale):
-    rows = act.shape[0]
-    row = own[rows:rows + 1] + side_row(g1[rows:]) + side_row(g2[rows:]) + side_row(g3[rows:])
-    r = lax.rsqrt(as_column(row, rows) / width + 1e-06)
+def act_kernel(width, own, squares, g1, g2, g3, act, slope, hid, scale):
+    rows, piece = act.shape
+    count = lane_blocks(rows)
+    sums = piece // LANES * rows
+    row = pack_row(g1[sums:], count) + pack_row(g2[sums:], count) + pack_row(g3[sums:], count)
+    r = lax.rsqrt((squares[...] + as_column(row, rows)) / width + 1e-06)
     scale[...] = r
-    a = (own[:rows] + g1[:rows].astype(F32) + g2[:rows].astype(F32) + g3[:rows].astype(F32)) * r
-    act[...] = a
-    square = a * a
-    t = jnp.tanh(GELU_IN * (a + GELU_CUBE * (square * a)))
-    half = 0.5 * (1.0 + t)
-    hid[...] = (a * half).astype(BF16)
-    slope[...] = half + 0.5 * a * (1.0 - t * t) * (GELU_IN * (1.0 + 3.0 * GELU_CUBE * square))
+    for i in range(piece // LANES):
+        at = slice(i * LANES, (i + 1) * LANES)
+        got = slice(i * rows, (i + 1) * rows)
+        a = (own[:, at] + g1[got].astype(F32) + g2[got].astype(F32) + g3[got].astype(F32)) * r
+        act[:, at] = a
+        square = a * a
+        t = jnp.tanh(GELU_IN * (a + GELU_CUBE * (square * a)))
+        half = 0.5 * (1.0 + t)
+        hid[:, at] = (a * half).astype(BF16)
+        slope[:, at] = half + 0.5 * a * (1.0 - t * t) * (GELU_IN * (1.0 + 3.0 * GELU_CUBE * square))
 
 
 def dact_kernel(own, g1, g2, g3, act, slope, pay):
     rows, piece = own.shape
     dhid = own[...] + g1[...].astype(F32) + g2[...].astype(F32) + g3[...].astype(F32)
     da = (dhid * slope[...]).astype(BF16)
-    pay[:rows] = da
-    pay[rows:] = side_block(as_row(jnp.sum(da.astype(F32) * act[...], axis=1, keepdims=True), piece))
+    blocks = piece // LANES
+    for i in range(blocks):
+        pay[i * rows:(i + 1) * rows] = da[:, i * LANES:(i + 1) * LANES]
+    column = jnp.sum(da.astype(F32) * act[...], axis=1, keepdims=True)
+    pay[blocks * rows:] = pack_block(as_row(column, lane_blocks(rows) * LANES))
 
 
 def back_part(part, j, weight, mine, lane, total, begin):
-    rows = total.shape[0]
-    piece = part.shape[1]
+    value = unpack(part, total.shape[0])
+    piece = value.shape[1]
     share = weight.shape[0] // 4
     for d in (1, 3, 0, 2):
-        block = dot_nt(part[:rows], weight[slot(lane ^ d, share), slot(mine ^ j, piece)])
+        block = dot_nt(value, weight[slot(lane ^ d, share), slot(mine ^ j, piece)])
         columns = slice(d * share, (d + 1) * share)
         total[:, columns] = block if begin else total[:, columns] + block
 
@@ -411,7 +450,10 @@
     share = weight.shape[0] // 4
     total[...] = earlier[...]
     back_part(p1, 1, weight, mine, lane, total, False)
-    row = side_row(p0[rows:]) + side_row(p1[rows:]) + side_row(p2[rows:]) + side_row(p3[rows:])
+    sums = p0.shape[0] - SIDE
+    row = sum(pack_row(part[sums:], lane_blocks(rows)) for part in (p0, p1, p2, p3))
+    if row.shape[1] < keep.shape[1]:
+        row = jnp.concatenate([row, jnp.zeros((1, keep.shape[1] - row.shape[1]), F32)], axis=1)
     for at, d in ((0, 1), (1, 3)):
         send[:rows, at * share:(at + 1) * share] = total[:, d * share:(d + 1) * share].astype(BF16)
     send[rows:] = side_block(row)
@@ -459,11 +501,11 @@
 def grad_in_kernel(p0, p1, p2, p3, x_full, gain, scale, out, scaled, held, sems):
     mine, _ = place()
     rows = x_full.shape[0]
-    piece = p0.shape[1]
+    piece = (p0.shape[0] - SIDE) // rows * LANES
     scaled[...] = (x_full[...].astype(F32) * scale[...] * gain[...]).astype(BF16)
     copies = []
     for d, part in enumerate((p0, p1, p2, p3)):
-        held[d] = dot_tn(scaled[...], part[:rows]).astype(BF16)
+        held[d] = dot_tn(scaled[...], unpack(part, rows)).astype(BF16)
         copies.append(pltpu.make_async_copy(held.at[d], out.at[:, slot(mine ^ d, piece)], sems.at[d]))
         copies[-1].start()
     for copy in copies:
@@ -506,11 +548,12 @@
     sent = lax.ppermute(cot, ("section", "dp"), [((i // 4 ^ near) * 4 + i // 4 % 4, i) for i in top for near in (1, 0, 2) if i // 4 % 4 ^ i % 4 == (2, 1, 3)[near]])
     x3 = flip(x2, "dp", 1)
 
-    wide = (rows + SIDE, piece)
+    packed = packed_shape(rows, piece)
     (begun,) = local(spread_in_first_kernel, [resident((rows, hidden), F32)], x0, x1, gain, weight_in, flops=work)
-    own, s1, s2, s3, x_full = local(
+    own, s1, s2, s3, x_full, squares = local(
         spread_in_last_kernel,
-        [resident(wide, F32)] + [resident(wide, BF16)] * 3 + [resident((rows, quarter), BF16)],
+        [resident((rows, piece), F32)] + [resident(packed, BF16)] * 3
+        + [resident((rows, quarter), BF16), resident((rows, 1), F32)],
         x0, x1, x2, x3, gain, weight_in, begun,
         scratch=[pltpu.VMEM((rows, hidden), F32)], flops=work,
     )
@@ -522,7 +565,7 @@
     act, slope, hid, scale = local(
         functools.partial(act_kernel, width),
         [resident((rows, piece), F32), resident((rows, piece), F32), resident((rows, piece), BF16), resident((rows, 1), F32)],
-        own, g1, g2, g3,
+        own, squares, g1, g2, g3,
     )
 
     spread_outs = [resident((rows, piece), F32)] + [resident((rows, piece), BF16)] * 3 + [resident((rows, quarter), BF16)]
@@ -553,7 +596,7 @@
         if final:
             grad_out = gradient(grad_out_kernel, (hidden, quarter), (piece, quarter), *hids, dy, flops=work)
             own, grad_out = lax.optimization_barrier((own, grad_out))
-        (pay,) = local(dact_kernel, [resident(wide, BF16)], own, g1, g2, g3, act, slope)
+        (pay,) = local(dact_kernel, [resident(packed, BF16)], own, g1, g2, g3, act, slope)
         p3 = flip(pay, "section", 3)
         p2 = flip(pay, "section", 2)
         p1 = flip(pay, "section", 1)

time: 102 us -> 100 us (0.980)
  waiting for transfers between devices: 49.5 us -> 48.3 us
    ppermute x28, waiting for transfers between devices: 44.1 us -> 42.8 us  [flip(): return lax.ppermute(block, axis, [(i, i ^ bits) for i in range(count)])]
where the time goes in v2:
time: 100 us
  waiting for transfers between devices  48.3 us (48%)
  starting transfers between devices  30.6 us (31%)
  Pallas kernels  20.3 us (20%)
    ppermute x28, waiting for transfers between devices, flip(): return lax.ppermute(block, axis, [(i, i ^ bits) for i in range(count)])  42.8 us
    ppermute x28, starting transfers between devices, flip(): return lax.ppermute(block, axis, [(i, i ^ bits) for i in range(count)])  28.6 us
    pallas_call x19, Pallas kernels, local(): pl.pallas_call(body, out_shape=tuple(outs), in_specs=[spec] * len(args),...  10.6 us
    ppermute x1, waiting for transfers between devices, shards_of_four(): lax.ppermute(finished[0], 'section', [(i, i - 4) for i in range(4, sectio...  5.57 us
    pallas_call x2, Pallas kernels, gradient(): pl.pallas_call(body, out_shape=jax.ShapeDtypeStruct(shape, BF16), in_spec...  5.13 us
    pallas_call x2, Pallas kernels, load(): pl.pallas_call(load_kernel, out_shape=tuple((resident(a.shape, a.dtype) f...  4.49 us
  transfers between devices with their start and end apart: 30, of which 20 were waited for; matrix products, arithmetic and copies ran while one was open for 0% of the time, Pallas kernels for 17%

profile of v2, /device:TPU:0, one launch (start us, length us, event | category | flops | bytes accessed | tf_op | source)
XLA Modules:
  0.0 100.1 jit_solution(18337329958879231046)
XLA Ops:
  0.6 0.5 collective-permute-start.1
  1.1 2.6 %collective-permute-start = (bf16[192,256]{1,0:T(8,128)(2,1)}, bf16[192,256]{1,0:T(8,128)(2,1)S(1)}, u32[]{:S(2)}, u32[]{:S(2)}) collective-permute-start(bf16[192,256]{1,0:T(8,128)(2,1)} %bitcast.14), channel_id=1, source_target_pairs={{0,2},{1,3},{2,0},{3,1},{4,6},{5,7},{6,4},{7,5},{8,10},{9,11},{10,... | collective-permute-start | bytes 294920 | tf_op jit(solution)/shard_map/ppermute | solution.py:16
  3.7 0.7 collective-permute-start.3
  4.4 2.2 %shard_map.84 = (bf16[1024,2048]{1,0:T(8,128)(2,1)S(1)}, bf16[192,256]{1,0:T(8,128)(2,1)S(1)}, f32[1,1024]{1,0:T(1,128)S(1)}) custom-call(bf16[1024,2048]{1,0:T(8,128)(2,1)} %bitcast.7, bf16[192,256]{1,0:T(8,128)(2,1)} %bitcast.15, f32[1,1024]{1,0:T(1,128)} %refs_2_.1), custom_call_target="tpu_custom_call" | custom-call | bytes 8593408 | tf_op jit(solution)/shard_map/pallas_call | solution.py:270
  6.6 0.7 collective-permute-done.x2
  7.3 0.6 shard_map.85.before
  7.9 0.7 collective-permute-done.2.x3
  8.6 0.6 shard_map.86
  9.2 1.9 %collective-permute-start.7 = (bf16[784,128]{1,0:T(8,128)(2,1)S(1)}, bf16[784,128]{1,0:T(8,128)(2,1)S(1)}, u32[]{:S(2)}, u32[]{:S(2)}) collective-permute-start(bf16[784,128]{1,0:T(8,128)(2,1)S(1)} %get-tuple-element.77), channel_id=1, source_target_pairs={{0,4},{4,0},{8,12},{12,8},{16,20},{20,16},{24,28},{28,24},{1,5},{5... | collective-permute-start | bytes 602120 | tf_op jit(solution)/shard_map/ppermute | solution.py:16
  11.1 1.6 %collective-permute-start.8 = (bf16[784,128]{1,0:T(8,128)(2,1)S(1)}, bf16[784,128]{1,0:T(8,128)(2,1)S(1)}, u32[]{:S(2)}, u32[]{:S(2)}) collective-permute-start(bf16[784,128]{1,0:T(8,128)(2,1)S(1)} %get-tuple-element.78), channel_id=1, source_target_pairs={{0,8},{4,12},{8,0},{12,4},{16,24},{20,28},{24,16},{28,20},{1,9},{5... | collective-permute-start | bytes 602120 | tf_op jit(solution)/shard_map/ppermute | solution.py:16
  12.7 0.1 collective-permute-start.9
  12.8 2.3 %shard_map.87 = (bf16[2048,1024]{1,0:T(8,128)(2,1)S(1)}, bf16[192,1024]{1,0:T(8,128)(2,1)S(1)}) custom-call(bf16[2048,1024]{1,0:T(8,128)(2,1)} %bitcast.8, bf16[192,1024]{1,0:T(8,128)(2,1)} %bitcast.12), custom_call_target="tpu_custom_call" | custom-call | bytes 9175040 | tf_op jit(solution)/shard_map/pallas_call | solution.py:270
  15.1 1.6 %shard_map.88 = (f32[192,512]{1,0:T(8,128)S(1)}, bf16[192,512]{1,0:T(8,128)(2,1)S(1)}, bf16[192,512]{1,0:T(8,128)(2,1)S(1)}, bf16[192,512]{1,0:T(8,128)(2,1)S(1)}, bf16[192,1024]{1,0:T(8,128)(2,1)S(1)}) custom-call(bf16[192,1024]{1,0:T(8,128)(2,1)S(1)} %get-tuple-element.69.cot, bf16[192,1024]{1,0:T(8,128)(2,1)S(1)} %collective-permute-done.3.sent, ...), custom_call_target="tpu_custom_call" | custom-call | flops 805306368 | bytes 4980736 | tf_op jit(solution)/shard_map/pallas_call | solution.py:196
  16.7 1.9 %collective-permute-start.4 = (bf16[192,512]{1,0:T(8,128)(2,1)S(1)}, bf16[192,512]{1,0:T(8,128)(2,1)S(1)}, u32[]{:S(2)}, u32[]{:S(2)}) collective-permute-start(bf16[192,512]{1,0:T(8,128)(2,1)S(1)} %get-tuple-element.72), channel_id=1, source_target_pairs={{0,4},{4,0},{8,12},{12,8},{16,20},{20,16},{24,28},{28,24},{1,5},{5... | collective-permute-start | bytes 589832 | tf_op jit(solution)/shard_map/ppermute | solution.py:16
  18.5 1.6 %collective-permute-start.5 = (bf16[192,512]{1,0:T(8,128)(2,1)S(1)}, bf16[192,512]{1,0:T(8,128)(2,1)S(1)}, u32[]{:S(2)}, u32[]{:S(2)}) collective-permute-start(bf16[192,512]{1,0:T(8,128)(2,1)S(1)} %get-tuple-element.73), channel_id=1, source_target_pairs={{0,8},{4,12},{8,0},{12,4},{16,24},{20,28},{24,16},{28,20},{1,9},{5... | collective-permute-start | bytes 589832 | tf_op jit(solution)/shard_map/ppermute | solution.py:16
  20.2 2.8 %collective-permute-done.9.g3 = bf16[784,128]{1,0:T(8,128)(2,1)S(1)} collective-permute-done((bf16[784,128]{1,0:T(8,128)(2,1)S(1)}, bf16[784,128]{1,0:T(8,128)(2,1)S(1)}, u32[]{:S(2)}, u32[]{:S(2)}) %collective-permute-start.9) | collective-permute-done | bytes 200736 | tf_op jit(solution)/shard_map/ppermute | solution.py:16
  23.0 0.5 shard_map.89
  23.5 3.6 %collective-permute-done.4.g1 = bf16[192,512]{1,0:T(8,128)(2,1)S(1)} collective-permute-done((bf16[192,512]{1,0:T(8,128)(2,1)S(1)}, bf16[192,512]{1,0:T(8,128)(2,1)S(1)}, u32[]{:S(2)}, u32[]{:S(2)}) %collective-permute-start.4) | collective-permute-done | bytes 196640 | tf_op jit(solution)/shard_map/ppermute | solution.py:16
  27.1 0.4 collective-permute-done.5.g2
  27.5 2.9 %collective-permute-done.6.g3 = bf16[192,512]{1,0:T(8,128)(2,1)S(1)} collective-permute-done((bf16[192,512]{1,0:T(8,128)(2,1)S(1)}, bf16[192,512]{1,0:T(8,128)(2,1)S(1)}, u32[]{:S(2)}, u32[]{:S(2)}) %collective-permute-start.6) | collective-permute-done | bytes 196640 | tf_op jit(solution)/shard_map/ppermute | solution.py:16
  30.4 0.2 shard_map.90.refs_0_.p0
  30.7 2.7 %collective-permute-start.12 = (bf16[784,128]{1,0:T(8,128)(2,1)S(1)}, bf16[784,128]{1,0:T(8,128)(2,1)S(1)}, u32[]{:S(2)}, u32[]{:S(2)}) collective-permute-start(bf16[784,128]{1,0:T(8,128)(2,1)S(1)} %shard_map.90.refs_0_.p0), channel_id=1, source_target_pairs={{0,12},{4,8},{8,4},{12,0},{16,28},{20,24},{24,20},{28,16},{1,13},{... | collective-permute-start | bytes 602120 | tf_op jit(solution)/shard_map/ppermute | solution.py:16
  33.4 0.4 collective-permute-start.11
  33.9 0.4 collective-permute-start.10
  34.2 0.5 shard_map.91.refs_3_
  34.7 4.8 %collective-permute-done.12.refs_0_.p3 = bf16[784,128]{1,0:T(8,128)(2,1)S(1)} collective-permute-done((bf16[784,128]{1,0:T(8,128)(2,1)S(1)}, bf16[784,128]{1,0:T(8,128)(2,1)S(1)}, u32[]{:S(2)}, u32[]{:S(2)}) %collective-permute-start.12) | collective-permute-done | bytes 200736 | tf_op jit(solution)/shard_map/ppermute | solution.py:16
  39.5 2.5 %collective-permute-done.11.refs_1_.p2 = bf16[784,128]{1,0:T(8,128)(2,1)S(1)} collective-permute-done((bf16[784,128]{1,0:T(8,128)(2,1)S(1)}, bf16[784,128]{1,0:T(8,128)(2,1)S(1)}, u32[]{:S(2)}, u32[]{:S(2)}) %collective-permute-start.11) | collective-permute-done | bytes 200736 | tf_op jit(solution)/shard_map/ppermute | solution.py:16
  42.0 0.8 shard_map.92.earlier
  42.9 0.5 shard_map.93
  43.5 1.5 %collective-permute-done.13.got = bf16[208,512]{1,0:T(8,128)(2,1)S(1)} collective-permute-done((bf16[208,512]{1,0:T(8,128)(2,1)S(1)}, bf16[208,512]{1,0:T(8,128)(2,1)S(1)}, u32[]{:S(2)}, u32[]{:S(2)}) %collective-permute-start.13) | collective-permute-done | bytes 213024 | tf_op jit(solution)/shard_map/ppermute | solution.py:16
  45.0 1.6 %collective-permute-start.14 = (bf16[208,256]{1,0:T(8,128)(2,1)S(1)}, bf16[208,256]{1,0:T(8,128)(2,1)S(1)}, u32[]{:S(2)}, u32[]{:S(2)}) collective-permute-start(bf16[208,256]{1,0:T(8,128)(2,1)S(1)} %get-tuple-element.87), channel_id=1, source_target_pairs={{0,2},{1,3},{2,0},{3,1},{4,6},{5,7},{6,4},{7,5},{8,10},{9,11},{10,... | collective-permute-start | bytes 319496 | tf_op jit(solution)/shard_map/ppermute | solution.py:16
  46.6 3.5 %collective-permute-done.14.got = bf16[208,256]{1,0:T(8,128)(2,1)S(1)} collective-permute-done((bf16[208,256]{1,0:T(8,128)(2,1)S(1)}, bf16[208,256]{1,0:T(8,128)(2,1)S(1)}, u32[]{:S(2)}, u32[]{:S(2)}) %collective-permute-start.14) | collective-permute-done | bytes 106528 | tf_op jit(solution)/shard_map/ppermute | solution.py:16
  50.1 0.2 shard_map.95
  50.3 1.3 %collective-permute-start.15 = (bf16[192,256]{1,0:T(8,128)(2,1)S(1)}, bf16[192,256]{1,0:T(8,128)(2,1)S(1)}, u32[]{:S(2)}, u32[]{:S(2)}) collective-permute-start(bf16[192,256]{1,0:T(8,128)(2,1)S(1)} %shard_map.95), channel_id=1, source_target_pairs={{16,0},{20,4},{24,8},{28,12},{17,1},{21,5},{25,9},{29,13},{18,2},{... | collective-permute-start | bytes 294920 | tf_op jit(solution)/shard_map/ppermute | solution.py:633
  51.6 1.7 %collective-permute-start.21 = (bf16[192,512]{1,0:T(8,128)(2,1)S(1)}, bf16[192,512]{1,0:T(8,128)(2,1)S(1)}, u32[]{:S(2)}, u32[]{:S(2)}) collective-permute-start(bf16[192,512]{1,0:T(8,128)(2,1)S(1)} %get-tuple-element.93.h0), channel_id=1, source_target_pairs={{0,12},{4,8},{8,4},{12,0},{16,28},{20,24},{24,20},{28,16},{1,13},{... | collective-permute-start | bytes 589832 | tf_op jit(solution)/shard_map/ppermute | solution.py:16
  53.2 0.4 collective-permute-start.20
  53.7 1.5 %collective-permute-start.19 = (bf16[192,512]{1,0:T(8,128)(2,1)S(1)}, bf16[192,512]{1,0:T(8,128)(2,1)S(1)}, u32[]{:S(2)}, u32[]{:S(2)}) collective-permute-start(bf16[192,512]{1,0:T(8,128)(2,1)S(1)} %get-tuple-element.93.h0), channel_id=1, source_target_pairs={{0,4},{4,0},{8,12},{12,8},{16,20},{20,16},{24,28},{28,24},{1,5},{5... | collective-permute-start | bytes 589832 | tf_op jit(solution)/shard_map/ppermute | solution.py:16
  55.1 5.6 %collective-permute-done.15.refs_0_.refs_4_ = bf16[192,256]{1,0:T(8,128)(2,1)S(1)} collective-permute-done((bf16[192,256]{1,0:T(8,128)(2,1)S(1)}, bf16[192,256]{1,0:T(8,128)(2,1)S(1)}, u32[]{:S(2)}, u32[]{:S(2)}) %collective-permute-start.15) | collective-permute-done | bytes 98336 | tf_op jit(solution)/shard_map/ppermute | solution.py:633
  60.7 1.2 %collective-permute-start.16 = (bf16[192,256]{1,0:T(8,128)(2,1)S(1)}, bf16[192,256]{1,0:T(8,128)(2,1)S(1)}, u32[]{:S(2)}, u32[]{:S(2)}) collective-permute-start(bf16[192,256]{1,0:T(8,128)(2,1)S(1)} %collective-permute-done.15.refs_0_.refs_4_), channel_id=1, source_target_pairs={{0,2},{1,3},{2,0},{3,1},{4,6},{5,7},{6,4},{7,5},{8,10},{9,11},{10,... | collective-permute-start | bytes 294920 | tf_op jit(solution)/shard_map/ppermute | solution.py:16
  61.9 3.4 %collective-permute-done.16.refs_1_.refs_6_ = bf16[192,256]{1,0:T(8,128)(2,1)S(1)} collective-permute-done((bf16[192,256]{1,0:T(8,128)(2,1)S(1)}, bf16[192,256]{1,0:T(8,128)(2,1)S(1)}, u32[]{:S(2)}, u32[]{:S(2)}) %collective-permute-start.16) | collective-permute-done | bytes 98336 | tf_op jit(solution)/shard_map/ppermute | solution.py:16
  65.3 0.5 shard_map.96.refs_4_
  65.9 0.9 shard_map.97.refs_3_
  66.8 0.7 shard_map.98
  67.5 0.5 collective-permute-start.22
  68.0 3.1 %collective-permute-start.24 = (bf16[192,512]{1,0:T(8,128)(2,1)S(1)}, bf16[192,512]{1,0:T(8,128)(2,1)S(1)}, u32[]{:S(2)}, u32[]{:S(2)}) collective-permute-start(bf16[192,512]{1,0:T(8,128)(2,1)S(1)} %get-tuple-element.101), channel_id=1, source_target_pairs={{0,12},{4,8},{8,4},{12,0},{16,28},{20,24},{24,20},{28,16},{1,13},{... | collective-permute-start | bytes 589832 | tf_op jit(solution)/shard_map/ppermute | solution.py:16
  71.1 2.5 %shard_map.99 = bf16[2048,1024]{1,0:T(8,128)(2,1)} custom-call(bf16[192,512]{1,0:T(8,128)(2,1)S(1)} %get-tuple-element.93.h0, bf16[192,512]{1,0:T(8,128)(2,1)S(1)} %collective-permute-done.19.h1, bf16[192,512]{1,0:T(8,128)(2,1)S(1)} %collective-permute-done.20.h2, bf16[192,512]{1,0:T(8,128)(2,1)S(1)} %collective-permute-done.21.h3, ...), custom_call_target="tpu_custom_call" | custom-call | flops 805306368 | bytes 4194304 | tf_op jit(solution)/shard_map/pallas_call | solution.py:516
  73.6 1.3 %collective-permute-done.22.g1 = bf16[192,512]{1,0:T(8,128)(2,1)S(1)} collective-permute-done((bf16[192,512]{1,0:T(8,128)(2,1)S(1)}, bf16[192,512]{1,0:T(8,128)(2,1)S(1)}, u32[]{:S(2)}, u32[]{:S(2)}) %collective-permute-start.22) | collective-permute-done | bytes 196640 | tf_op jit(solution)/shard_map/ppermute | solution.py:16
  74.9 0.8 collective-permute-done.23.g2
  75.7 4.6 %collective-permute-done.24.g3 = bf16[192,512]{1,0:T(8,128)(2,1)S(1)} collective-permute-done((bf16[192,512]{1,0:T(8,128)(2,1)S(1)}, bf16[192,512]{1,0:T(8,128)(2,1)S(1)}, u32[]{:S(2)}, u32[]{:S(2)}) %collective-permute-start.24) | collective-permute-done | bytes 196640 | tf_op jit(solution)/shard_map/ppermute | solution.py:16
  80.3 0.2 shard_map.100.refs_0_.p0
  80.5 0.2 collective-permute-start.27
  80.7 1.7 %collective-permute-start.26 = (bf16[784,128]{1,0:T(8,128)(2,1)S(1)}, bf16[784,128]{1,0:T(8,128)(2,1)S(1)}, u32[]{:S(2)}, u32[]{:S(2)}) collective-permute-start(bf16[784,128]{1,0:T(8,128)(2,1)S(1)} %shard_map.100.refs_0_.p0), channel_id=1, source_target_pairs={{0,8},{4,12},{8,0},{12,4},{16,24},{20,28},{24,16},{28,20},{1,9},{5... | collective-permute-start | bytes 602120 | tf_op jit(solution)/shard_map/ppermute | solution.py:16
  82.4 1.6 %collective-permute-start.25 = (bf16[784,128]{1,0:T(8,128)(2,1)S(1)}, bf16[784,128]{1,0:T(8,128)(2,1)S(1)}, u32[]{:S(2)}, u32[]{:S(2)}) collective-permute-start(bf16[784,128]{1,0:T(8,128)(2,1)S(1)} %shard_map.100.refs_0_.p0), channel_id=1, source_target_pairs={{0,4},{4,0},{8,12},{12,8},{16,20},{20,16},{24,28},{28,24},{1,5},{5... | collective-permute-start | bytes 602120 | tf_op jit(solution)/shard_map/ppermute | solution.py:16
  84.1 0.5 shard_map.101.refs_3_
  84.6 4.9 %collective-permute-done.27.refs_0_.p3 = bf16[784,128]{1,0:T(8,128)(2,1)S(1)} collective-permute-done((bf16[784,128]{1,0:T(8,128)(2,1)S(1)}, bf16[784,128]{1,0:T(8,128)(2,1)S(1)}, u32[]{:S(2)}, u32[]{:S(2)}) %collective-permute-start.27) | collective-permute-done | bytes 200736 | tf_op jit(solution)/shard_map/ppermute | solution.py:16
  89.4 1.6 %collective-permute-done.26.refs_1_.p2 = bf16[784,128]{1,0:T(8,128)(2,1)S(1)} collective-permute-done((bf16[784,128]{1,0:T(8,128)(2,1)S(1)}, bf16[784,128]{1,0:T(8,128)(2,1)S(1)}, u32[]{:S(2)}, u32[]{:S(2)}) %collective-permute-start.26) | collective-permute-done | bytes 200736 | tf_op jit(solution)/shard_map/ppermute | solution.py:16
  91.0 0.8 shard_map.102.earlier
  91.8 0.2 collective-permute-done.25.p1
  92.1 0.5 shard_map.103
  92.7 1.4 %collective-permute-done.28.got = bf16[208,512]{1,0:T(8,128)(2,1)S(1)} collective-permute-done((bf16[208,512]{1,0:T(8,128)(2,1)S(1)}, bf16[208,512]{1,0:T(8,128)(2,1)S(1)}, u32[]{:S(2)}, u32[]{:S(2)}) %collective-permute-start.28) | collective-permute-done | bytes 213024 | tf_op jit(solution)/shard_map/ppermute | solution.py:16
  94.2 1.3 %collective-permute-start.29 = (bf16[208,256]{1,0:T(8,128)(2,1)S(1)}, bf16[208,256]{1,0:T(8,128)(2,1)S(1)}, u32[]{:S(2)}, u32[]{:S(2)}) collective-permute-start(bf16[208,256]{1,0:T(8,128)(2,1)S(1)} %get-tuple-element.104), channel_id=1, source_target_pairs={{0,2},{1,3},{2,0},{3,1},{4,6},{5,7},{6,4},{7,5},{8,10},{9,11},{10,... | collective-permute-start | bytes 319496 | tf_op jit(solution)/shard_map/ppermute | solution.py:16
  95.5 2.6 %shard_map.105 = bf16[1024,2048]{1,0:T(8,128)(2,1)} custom-call(bf16[784,128]{1,0:T(8,128)(2,1)S(1)} %shard_map.100.refs_0_.p0, bf16[784,128]{1,0:T(8,128)(2,1)S(1)} %collective-permute-done.25.p1, bf16[784,128]{1,0:T(8,128)(2,1)S(1)} %collective-permute-done.26.refs_1_.p2, bf16[784,128]{1,0:T(8,128)(2,1)S(1)} %collective-permute-done.27.refs_0_.p3, ...), custom_call_target="tpu_custom_call" | custom-call | flops 805306368 | bytes 4194304 | tf_op jit(solution)/shard_map/pallas_call | solution.py:516
  98.1 1.2 %collective-permute-done.29.got = bf16[208,256]{1,0:T(8,128)(2,1)S(1)} collective-permute-done((bf16[208,256]{1,0:T(8,128)(2,1)S(1)}, bf16[208,256]{1,0:T(8,128)(2,1)S(1)}, u32[]{:S(2)}, u32[]{:S(2)}) %collective-permute-start.29) | collective-permute-done | bytes 106528 | tf_op jit(solution)/shard_map/ppermute | solution.py:16
  99.3 0.8 shard_map.106
  (19 shorter events, 0.5 us)
Async XLA Ops:
  0.6 6.0 %collective-permute-start.1 = (bf16[192,256]{1,0:T(8,128)(2,1)}, bf16[192,256]{1,0:T(8,128)(2,1)S(1)}, u32[]{:S(2)}, u32[]{:S(2)}) collective-permute-start(bf16[192,256]{1,0:T(8,128)(2,1)} %bitcast.13), channel_id=1, source_target_pairs={{0,1},{1,0},{2,3},{3,2},{4,5},{5,4},{6,7},{7,6},{8,9},{9,8},{10,11... | collective-permute-start | bytes 294920 | tf_op jit(solution)/shard_map/ppermute | solution.py:16
  1.1 6.2 %collective-permute-start = (bf16[192,256]{1,0:T(8,128)(2,1)}, bf16[192,256]{1,0:T(8,128)(2,1)S(1)}, u32[]{:S(2)}, u32[]{:S(2)}) collective-permute-start(bf16[192,256]{1,0:T(8,128)(2,1)} %bitcast.14), channel_id=1, source_target_pairs={{0,2},{1,3},{2,0},{3,1},{4,6},{5,7},{6,4},{7,5},{8,10},{9,11},{10,... | collective-permute-start | bytes 294920 | tf_op jit(solution)/shard_map/ppermute | solution.py:16
  3.7 11.4 %collective-permute-start.3 = (bf16[192,1024]{1,0:T(8,128)(2,1)}, bf16[192,1024]{1,0:T(8,128)(2,1)S(1)}, u32[]{:S(2)}, u32[]{:S(2)}) collective-permute-start(bf16[192,1024]{1,0:T(8,128)(2,1)} %bitcast.11), channel_id=1, source_target_pairs={{20,17},{16,18},{24,19},{17,20},{29,22},{21,23},{26,24},{18,25},{3... | collective-permute-start | bytes 1179656 | tf_op jit(solution)/shard_map/ppermute | solution.py:548
  7.3 1.3 %collective-permute-start.2 = (bf16[192,256]{1,0:T(8,128)(2,1)S(1)}, bf16[192,256]{1,0:T(8,128)(2,1)S(1)}, u32[]{:S(2)}, u32[]{:S(2)}) collective-permute-start(bf16[192,256]{1,0:T(8,128)(2,1)S(1)} %collective-permute-done.x2), channel_id=1, source_target_pairs={{0,1},{1,0},{2,3},{3,2},{4,5},{5,4},{6,7},{7,6},{8,9},{9,8},{10,11... | collective-permute-start | bytes 294920 | tf_op jit(solution)/shard_map/ppermute | solution.py:16
  9.2 10.8 %collective-permute-start.7 = (bf16[784,128]{1,0:T(8,128)(2,1)S(1)}, bf16[784,128]{1,0:T(8,128)(2,1)S(1)}, u32[]{:S(2)}, u32[]{:S(2)}) collective-permute-start(bf16[784,128]{1,0:T(8,128)(2,1)S(1)} %get-tuple-element.77), channel_id=1, source_target_pairs={{0,4},{4,0},{8,12},{12,8},{16,20},{20,16},{24,28},{28,24},{1,5},{5... | collective-permute-start | bytes 602120 | tf_op jit(solution)/shard_map/ppermute | solution.py:16
  11.1 9.1 %collective-permute-start.8 = (bf16[784,128]{1,0:T(8,128)(2,1)S(1)}, bf16[784,128]{1,0:T(8,128)(2,1)S(1)}, u32[]{:S(2)}, u32[]{:S(2)}) collective-permute-start(bf16[784,128]{1,0:T(8,128)(2,1)S(1)} %get-tuple-element.78), channel_id=1, source_target_pairs={{0,8},{4,12},{8,0},{12,4},{16,24},{20,28},{24,16},{28,20},{1,9},{5... | collective-permute-start | bytes 602120 | tf_op jit(solution)/shard_map/ppermute | solution.py:16
  12.7 10.3 %collective-permute-start.9 = (bf16[784,128]{1,0:T(8,128)(2,1)S(1)}, bf16[784,128]{1,0:T(8,128)(2,1)S(1)}, u32[]{:S(2)}, u32[]{:S(2)}) collective-permute-start(bf16[784,128]{1,0:T(8,128)(2,1)S(1)} %get-tuple-element.79), channel_id=1, source_target_pairs={{0,12},{4,8},{8,4},{12,0},{16,28},{20,24},{24,20},{28,16},{1,13},{... | collective-permute-start | bytes 602120 | tf_op jit(solution)/shard_map/ppermute | solution.py:16
  16.7 10.4 %collective-permute-start.4 = (bf16[192,512]{1,0:T(8,128)(2,1)S(1)}, bf16[192,512]{1,0:T(8,128)(2,1)S(1)}, u32[]{:S(2)}, u32[]{:S(2)}) collective-permute-start(bf16[192,512]{1,0:T(8,128)(2,1)S(1)} %get-tuple-element.72), channel_id=1, source_target_pairs={{0,4},{4,0},{8,12},{12,8},{16,20},{20,16},{24,28},{28,24},{1,5},{5... | collective-permute-start | bytes 589832 | tf_op jit(solution)/shard_map/ppermute | solution.py:16
  18.5 9.0 %collective-permute-start.5 = (bf16[192,512]{1,0:T(8,128)(2,1)S(1)}, bf16[192,512]{1,0:T(8,128)(2,1)S(1)}, u32[]{:S(2)}, u32[]{:S(2)}) collective-permute-start(bf16[192,512]{1,0:T(8,128)(2,1)S(1)} %get-tuple-element.73), channel_id=1, source_target_pairs={{0,8},{4,12},{8,0},{12,4},{16,24},{20,28},{24,16},{28,20},{1,9},{5... | collective-permute-start | bytes 589832 | tf_op jit(solution)/shard_map/ppermute | solution.py:16
  20.1 10.3 %collective-permute-start.6 = (bf16[192,512]{1,0:T(8,128)(2,1)S(1)}, bf16[192,512]{1,0:T(8,128)(2,1)S(1)}, u32[]{:S(2)}, u32[]{:S(2)}) collective-permute-start(bf16[192,512]{1,0:T(8,128)(2,1)S(1)} %get-tuple-element.74), channel_id=1, source_target_pairs={{0,12},{4,8},{8,4},{12,0},{16,28},{20,24},{24,20},{28,16},{1,13},{... | collective-permute-start | bytes 589832 | tf_op jit(solution)/shard_map/ppermute | solution.py:16
  30.7 8.9 %collective-permute-start.12 = (bf16[784,128]{1,0:T(8,128)(2,1)S(1)}, bf16[784,128]{1,0:T(8,128)(2,1)S(1)}, u32[]{:S(2)}, u32[]{:S(2)}) collective-permute-start(bf16[784,128]{1,0:T(8,128)(2,1)S(1)} %shard_map.90.refs_0_.p0), channel_id=1, source_target_pairs={{0,12},{4,8},{8,4},{12,0},{16,28},{20,24},{24,20},{28,16},{1,13},{... | collective-permute-start | bytes 602120 | tf_op jit(solution)/shard_map/ppermute | solution.py:16
  33.4 8.6 %collective-permute-start.11 = (bf16[784,128]{1,0:T(8,128)(2,1)S(1)}, bf16[784,128]{1,0:T(8,128)(2,1)S(1)}, u32[]{:S(2)}, u32[]{:S(2)}) collective-permute-start(bf16[784,128]{1,0:T(8,128)(2,1)S(1)} %shard_map.90.refs_0_.p0), channel_id=1, source_target_pairs={{0,8},{4,12},{8,0},{12,4},{16,24},{20,28},{24,16},{28,20},{1,9},{5... | collective-permute-start | bytes 602120 | tf_op jit(solution)/shard_map/ppermute | solution.py:16
  33.9 9.0 %collective-permute-start.10 = (bf16[784,128]{1,0:T(8,128)(2,1)S(1)}, bf16[784,128]{1,0:T(8,128)(2,1)S(1)}, u32[]{:S(2)}, u32[]{:S(2)}) collective-permute-start(bf16[784,128]{1,0:T(8,128)(2,1)S(1)} %shard_map.90.refs_0_.p0), channel_id=1, source_target_pairs={{0,4},{4,0},{8,12},{12,8},{16,20},{20,16},{24,28},{28,24},{1,5},{5... | collective-permute-start | bytes 602120 | tf_op jit(solution)/shard_map/ppermute | solution.py:16
  43.4 1.5 %collective-permute-start.13 = (bf16[208,512]{1,0:T(8,128)(2,1)S(1)}, bf16[208,512]{1,0:T(8,128)(2,1)S(1)}, u32[]{:S(2)}, u32[]{:S(2)}) collective-permute-start(bf16[208,512]{1,0:T(8,128)(2,1)S(1)} %get-tuple-element.83), channel_id=1, source_target_pairs={{0,1},{1,0},{2,3},{3,2},{4,5},{5,4},{6,7},{7,6},{8,9},{9,8},{10,11... | collective-permute-start | bytes 638984 | tf_op jit(solution)/shard_map/ppermute | solution.py:16
  45.0 5.1 %collective-permute-start.14 = (bf16[208,256]{1,0:T(8,128)(2,1)S(1)}, bf16[208,256]{1,0:T(8,128)(2,1)S(1)}, u32[]{:S(2)}, u32[]{:S(2)}) collective-permute-start(bf16[208,256]{1,0:T(8,128)(2,1)S(1)} %get-tuple-element.87), channel_id=1, source_target_pairs={{0,2},{1,3},{2,0},{3,1},{4,6},{5,7},{6,4},{7,5},{8,10},{9,11},{10,... | collective-permute-start | bytes 319496 | tf_op jit(solution)/shard_map/ppermute | solution.py:16
  50.3 10.4 %collective-permute-start.15 = (bf16[192,256]{1,0:T(8,128)(2,1)S(1)}, bf16[192,256]{1,0:T(8,128)(2,1)S(1)}, u32[]{:S(2)}, u32[]{:S(2)}) collective-permute-start(bf16[192,256]{1,0:T(8,128)(2,1)S(1)} %shard_map.95), channel_id=1, source_target_pairs={{16,0},{20,4},{24,8},{28,12},{17,1},{21,5},{25,9},{29,13},{18,2},{... | collective-permute-start | bytes 294920 | tf_op jit(solution)/shard_map/ppermute | solution.py:633
  51.6 13.7 %collective-permute-start.21 = (bf16[192,512]{1,0:T(8,128)(2,1)S(1)}, bf16[192,512]{1,0:T(8,128)(2,1)S(1)}, u32[]{:S(2)}, u32[]{:S(2)}) collective-permute-start(bf16[192,512]{1,0:T(8,128)(2,1)S(1)} %get-tuple-element.93.h0), channel_id=1, source_target_pairs={{0,12},{4,8},{8,4},{12,0},{16,28},{20,24},{24,20},{28,16},{1,13},{... | collective-permute-start | bytes 589832 | tf_op jit(solution)/shard_map/ppermute | solution.py:16
  53.2 12.1 %collective-permute-start.20 = (bf16[192,512]{1,0:T(8,128)(2,1)S(1)}, bf16[192,512]{1,0:T(8,128)(2,1)S(1)}, u32[]{:S(2)}, u32[]{:S(2)}) collective-permute-start(bf16[192,512]{1,0:T(8,128)(2,1)S(1)} %get-tuple-element.93.h0), channel_id=1, source_target_pairs={{0,8},{4,12},{8,0},{12,4},{16,24},{20,28},{24,16},{28,20},{1,9},{5... | collective-permute-start | bytes 589832 | tf_op jit(solution)/shard_map/ppermute | solution.py:16
  53.7 11.7 %collective-permute-start.19 = (bf16[192,512]{1,0:T(8,128)(2,1)S(1)}, bf16[192,512]{1,0:T(8,128)(2,1)S(1)}, u32[]{:S(2)}, u32[]{:S(2)}) collective-permute-start(bf16[192,512]{1,0:T(8,128)(2,1)S(1)} %get-tuple-element.93.h0), channel_id=1, source_target_pairs={{0,4},{4,0},{8,12},{12,8},{16,20},{20,16},{24,28},{28,24},{1,5},{5... | collective-permute-start | bytes 589832 | tf_op jit(solution)/shard_map/ppermute | solution.py:16
  60.7 4.6 %collective-permute-start.16 = (bf16[192,256]{1,0:T(8,128)(2,1)S(1)}, bf16[192,256]{1,0:T(8,128)(2,1)S(1)}, u32[]{:S(2)}, u32[]{:S(2)}) collective-permute-start(bf16[192,256]{1,0:T(8,128)(2,1)S(1)} %collective-permute-done.15.refs_0_.refs_4_), channel_id=1, source_target_pairs={{0,2},{1,3},{2,0},{3,1},{4,6},{5,7},{6,4},{7,5},{8,10},{9,11},{10,... | collective-permute-start | bytes 294920 | tf_op jit(solution)/shard_map/ppermute | solution.py:16
  61.9 3.9 %collective-permute-start.18 = (bf16[192,256]{1,0:T(8,128)(2,1)S(1)}, bf16[192,256]{1,0:T(8,128)(2,1)S(1)}, u32[]{:S(2)}, u32[]{:S(2)}) collective-permute-start(bf16[192,256]{1,0:T(8,128)(2,1)S(1)} %collective-permute-done.15.refs_0_.refs_4_), channel_id=1, source_target_pairs={{0,1},{1,0},{2,3},{3,2},{4,5},{5,4},{6,7},{7,6},{8,9},{9,8},{10,11... | collective-permute-start | bytes 294920 | tf_op jit(solution)/shard_map/ppermute | solution.py:16
  65.3 1.4 %collective-permute-start.17 = (bf16[192,256]{1,0:T(8,128)(2,1)S(1)}, bf16[192,256]{1,0:T(8,128)(2,1)S(1)}, u32[]{:S(2)}, u32[]{:S(2)}) collective-permute-start(bf16[192,256]{1,0:T(8,128)(2,1)S(1)} %collective-permute-done.16.refs_1_.refs_6_), channel_id=1, source_target_pairs={{0,1},{1,0},{2,3},{3,2},{4,5},{5,4},{6,7},{7,6},{8,9},{9,8},{10,11... | collective-permute-start | bytes 294920 | tf_op jit(solution)/shard_map/ppermute | solution.py:16
  67.5 7.4 %collective-permute-start.22 = (bf16[192,512]{1,0:T(8,128)(2,1)S(1)}, bf16[192,512]{1,0:T(8,128)(2,1)S(1)}, u32[]{:S(2)}, u32[]{:S(2)}) collective-permute-start(bf16[192,512]{1,0:T(8,128)(2,1)S(1)} %get-tuple-element.99), channel_id=1, source_target_pairs={{0,4},{4,0},{8,12},{12,8},{16,20},{20,16},{24,28},{28,24},{1,5},{5... | collective-permute-start | bytes 589832 | tf_op jit(solution)/shard_map/ppermute | solution.py:16
  68.0 7.7 %collective-permute-start.23 = (bf16[192,512]{1,0:T(8,128)(2,1)S(1)}, bf16[192,512]{1,0:T(8,128)(2,1)S(1)}, u32[]{:S(2)}, u32[]{:S(2)}) collective-permute-start(bf16[192,512]{1,0:T(8,128)(2,1)S(1)} %get-tuple-element.100), channel_id=1, source_target_pairs={{0,8},{4,12},{8,0},{12,4},{16,24},{20,28},{24,16},{28,20},{1,9},{5... | collective-permute-start | bytes 589832 | tf_op jit(solution)/shard_map/ppermute | solution.py:16
  68.0 12.3 %collective-permute-start.24 = (bf16[192,512]{1,0:T(8,128)(2,1)S(1)}, bf16[192,512]{1,0:T(8,128)(2,1)S(1)}, u32[]{:S(2)}, u32[]{:S(2)}) collective-permute-start(bf16[192,512]{1,0:T(8,128)(2,1)S(1)} %get-tuple-element.101), channel_id=1, source_target_pairs={{0,12},{4,8},{8,4},{12,0},{16,28},{20,24},{24,20},{28,16},{1,13},{... | collective-permute-start | bytes 589832 | tf_op jit(solution)/shard_map/ppermute | solution.py:16
  80.5 8.9 %collective-permute-start.27 = (bf16[784,128]{1,0:T(8,128)(2,1)S(1)}, bf16[784,128]{1,0:T(8,128)(2,1)S(1)}, u32[]{:S(2)}, u32[]{:S(2)}) collective-permute-start(bf16[784,128]{1,0:T(8,128)(2,1)S(1)} %shard_map.100.refs_0_.p0), channel_id=1, source_target_pairs={{0,12},{4,8},{8,4},{12,0},{16,28},{20,24},{24,20},{28,16},{1,13},{... | collective-permute-start | bytes 602120 | tf_op jit(solution)/shard_map/ppermute | solution.py:16
  80.7 10.3 %collective-permute-start.26 = (bf16[784,128]{1,0:T(8,128)(2,1)S(1)}, bf16[784,128]{1,0:T(8,128)(2,1)S(1)}, u32[]{:S(2)}, u32[]{:S(2)}) collective-permute-start(bf16[784,128]{1,0:T(8,128)(2,1)S(1)} %shard_map.100.refs_0_.p0), channel_id=1, source_target_pairs={{0,8},{4,12},{8,0},{12,4},{16,24},{20,28},{24,16},{28,20},{1,9},{5... | collective-permute-start | bytes 602120 | tf_op jit(solution)/shard_map/ppermute | solution.py:16
  82.4 9.7 %collective-permute-start.25 = (bf16[784,128]{1,0:T(8,128)(2,1)S(1)}, bf16[784,128]{1,0:T(8,128)(2,1)S(1)}, u32[]{:S(2)}, u32[]{:S(2)}) collective-permute-start(bf16[784,128]{1,0:T(8,128)(2,1)S(1)} %shard_map.100.refs_0_.p0), channel_id=1, source_target_pairs={{0,4},{4,0},{8,12},{12,8},{16,20},{20,16},{24,28},{28,24},{1,5},{5... | collective-permute-start | bytes 602120 | tf_op jit(solution)/shard_map/ppermute | solution.py:16
  92.6 1.5 %collective-permute-start.28 = (bf16[208,512]{1,0:T(8,128)(2,1)S(1)}, bf16[208,512]{1,0:T(8,128)(2,1)S(1)}, u32[]{:S(2)}, u32[]{:S(2)}) collective-permute-start(bf16[208,512]{1,0:T(8,128)(2,1)S(1)} %get-tuple-element.103), channel_id=1, source_target_pairs={{0,1},{1,0},{2,3},{3,2},{4,5},{5,4},{6,7},{7,6},{8,9},{9,8},{10,11... | collective-permute-start | bytes 638984 | tf_op jit(solution)/shard_map/ppermute | solution.py:16
  94.2 5.1 %collective-permute-start.29 = (bf16[208,256]{1,0:T(8,128)(2,1)S(1)}, bf16[208,256]{1,0:T(8,128)(2,1)S(1)}, u32[]{:S(2)}, u32[]{:S(2)}) collective-permute-start(bf16[208,256]{1,0:T(8,128)(2,1)S(1)} %get-tuple-element.104), channel_id=1, source_target_pairs={{0,2},{1,3},{2,0},{3,1},{4,6},{5,7},{6,4},{7,5},{8,10},{9,11},{10,... | collective-permute-start | bytes 319496 | tf_op jit(solution)/shard_map/ppermute | solution.py:16

commit v3 on v2

--- a/solution.py
+++ b/solution.py
@@ -309,10 +309,37 @@
     return jnp.sum(wide * wide, axis=1, keepdims=True)
 
 
-def spread_in_first_kernel(x0, x1, gain, weight, total):
+def load_spread_kernel(x1, weight, x0, gain, weight_held, x0_held, gain_held, total, sems):
     mine, lane = place()
-    spread_in_part(x0, lane, gain, weight, mine, total, True)
-    spread_in_part(x1, lane ^ 1, gain, weight, mine, total, False)
+    share = x1.shape[1]
+    small = [pltpu.make_async_copy(source, held, sems.at[i]) for i, (source, held) in enumerate(((x0, x0_held), (gain, gain_held)))]
+    slices = [slot(lane ^ d, share) for d in range(4)]
+    large = [pltpu.make_async_copy(weight.at[at], weight_held.at[at], sems.at[2 + d]) for d, at in enumerate(slices)]
+    for copy in (*small, *large):
+        copy.start()
+    for copy in (*small, large[0]):
+        copy.wait()
+    spread_in_part(x0_held, lane, gain_held, weight_held, mine, total, True)
+    large[1].wait()
+    spread_in_part(x1, lane ^ 1, gain_held, weight_held, mine, total, False)
+    large[2].wait()
+    large[3].wait()
+
+
+def load_spread(x1, weight, x0, gain):
+    keep = pl.BlockSpec(memory_space=pltpu.VMEM)
+    rows, hidden = x0.shape[0], weight.shape[1]
+    outs = [(a.shape, a.dtype) for a in (weight, x0, gain)] + [((rows, hidden), F32)]
+    far = [pltpu.with_memory_space_constraint(a, pltpu.HBM) for a in (weight, x0, gain)]
+    return pl.pallas_call(
+        load_spread_kernel,
+        out_shape=tuple(resident(*out) for out in outs),
+        in_specs=[keep] + [pl.BlockSpec(memory_space=pl.ANY)] * 3,
+        out_specs=(keep,) * 4,
+        scratch_shapes=[pltpu.SemaphoreType.DMA((6,))],
+        compiler_params=pltpu.CompilerParams(vmem_limit_bytes=8 * 1024 * 1024),
+        cost_estimate=pl.CostEstimate(flops=rows * weight.size, bytes_accessed=4 * weight.size, transcendentals=0),
+    )(x1, *far)
 
 
 def spread_in_last_kernel(x0, x1, x2, x3, gain, weight, before, own, s1, s2, s3, x_full, squares, total):
@@ -543,13 +570,12 @@
     top = [s * 4 + d for s in range(sections) for d in range(4) if s // 4 == layers - 1]
     x2 = flip(x0, "dp", 2)
     x1 = flip(x0, "dp", 1)
-    weight_in, x0, gain = load(w_in[0], x0, gain)
-    x2, x1, weight_in = lax.optimization_barrier((x2, x1, weight_in))
+    weight_in, x0, gain, begun = load_spread(x1, w_in[0], x0, gain)
+    x2, weight_in = lax.optimization_barrier((x2, weight_in))
     sent = lax.ppermute(cot, ("section", "dp"), [((i // 4 ^ near) * 4 + i // 4 % 4, i) for i in top for near in (1, 0, 2) if i // 4 % 4 ^ i % 4 == (2, 1, 3)[near]])
     x3 = flip(x2, "dp", 1)
 
     packed = packed_shape(rows, piece)
-    (begun,) = local(spread_in_first_kernel, [resident((rows, hidden), F32)], x0, x1, gain, weight_in, flops=work)
     own, s1, s2, s3, x_full, squares = local(
         spread_in_last_kernel,
         [resident((rows, piece), F32)] + [resident(packed, BF16)] * 3

time: 100 us -> 100 us (level)
    pallas_call x0 -> x1, Pallas kernels: none -> 2.3 us  [load_spread(): pl.pallas_call(load_spread_kernel, out_shape=tuple((resident(*out) for ou...]
    pallas_call x2 -> x1, Pallas kernels: 4.49 us -> 2.27 us  [load(): pl.pallas_call(load_kernel, out_shape=tuple((resident(a.shape, a.dtype) f...]
    pallas_call x19 -> x18, Pallas kernels: 10.6 us -> 10.1 us  [local(): pl.pallas_call(body, out_shape=tuple(outs), in_specs=[spec] * len(args),...]
  transfers between devices with their start and end apart: 30 -> 30, of which waited for: 20 -> 20; matrix products, arithmetic and copies ran while one was open for 0% -> 0% of each run, Pallas kernels for 17% -> 16%
where the time goes in v3:
time: 100 us
  waiting for transfers between devices  48.9 us (49%)
  starting transfers between devices  30.6 us (31%)
  Pallas kernels  19.8 us (20%)
    ppermute x28, waiting for transfers between devices, flip(): return lax.ppermute(block, axis, [(i, i ^ bits) for i in range(count)])  43.2 us
    ppermute x28, starting transfers between devices, flip(): return lax.ppermute(block, axis, [(i, i ^ bits) for i in range(count)])  28.7 us
    pallas_call x18, Pallas kernels, local(): pl.pallas_call(body, out_shape=tuple(outs), in_specs=[spec] * len(args),...  10.1 us
    ppermute x1, waiting for transfers between devices, shards_of_four(): lax.ppermute(finished[0], 'section', [(i, i - 4) for i in range(4, sectio...  5.65 us
    pallas_call x2, Pallas kernels, gradient(): pl.pallas_call(body, out_shape=jax.ShapeDtypeStruct(shape, BF16), in_spec...  5.13 us
    pallas_call x1, Pallas kernels, load_spread(): pl.pallas_call(load_spread_kernel, out_shape=tuple((resident(*out) for ou...  2.3 us
    pallas_call x1, Pallas kernels, load(): pl.pallas_call(load_kernel, out_shape=tuple((resident(a.shape, a.dtype) f...  2.27 us
  transfers between devices with their start and end apart: 30, of which 20 were waited for; matrix products, arithmetic and copies ran while one was open for 0% of the time, Pallas kernels for 16%

profile of v3, /device:TPU:0, one launch (start us, length us, event | category | flops | bytes accessed | tf_op | source)
XLA Modules:
  0.0 100.1 jit_solution(685662564940206892)
XLA Ops:
  0.6 0.5 collective-permute-start
  1.1 2.6 %collective-permute-start.1 = (bf16[192,256]{1,0:T(8,128)(2,1)}, bf16[192,256]{1,0:T(8,128)(2,1)S(1)}, u32[]{:S(2)}, u32[]{:S(2)}) collective-permute-start(bf16[192,256]{1,0:T(8,128)(2,1)} %bitcast.14), channel_id=1, source_target_pairs={{0,2},{1,3},{2,0},{3,1},{4,6},{5,7},{6,4},{7,5},{8,10},{9,11},{10,... | collective-permute-start | bytes 294920 | tf_op jit(solution)/shard_map/ppermute | solution.py:16
  3.7 0.7 collective-permute-start.3
  4.4 2.3 %shard_map.84 = (bf16[1024,2048]{1,0:T(8,128)(2,1)S(1)}, bf16[192,256]{1,0:T(8,128)(2,1)S(1)}, f32[1,1024]{1,0:T(1,128)S(1)}, f32[192,2048]{1,0:T(8,128)S(1)}) custom-call(bf16[192,256]{1,0:T(8,128)(2,1)S(1)} %collective-permute-done.x1, bf16[1024,2048]{1,0:T(8,128)(2,1)} %bitcast.7, bf16[192,256]{1,0:T(8,128)(2,1)} %bitcast.15, f32[1,1024]{1,0:T(1,128)} %gain.1), custom_call_target="tpu_custom_call" | custom-call | flops 402653184 | bytes 8388608 | tf_op jit(solution)/shard_map/pallas_call | solution.py:334
  6.7 0.6 collective-permute-done.1.x2
  7.3 1.3 %collective-permute-done.2.x3 = bf16[192,256]{1,0:T(8,128)(2,1)S(1)} collective-permute-done((bf16[192,256]{1,0:T(8,128)(2,1)S(1)}, bf16[192,256]{1,0:T(8,128)(2,1)S(1)}, u32[]{:S(2)}, u32[]{:S(2)}) %collective-permute-start.2) | collective-permute-done | bytes 98336 | tf_op jit(solution)/shard_map/ppermute | solution.py:16
  8.6 0.6 shard_map.85
  9.2 1.9 %collective-permute-start.7 = (bf16[784,128]{1,0:T(8,128)(2,1)S(1)}, bf16[784,128]{1,0:T(8,128)(2,1)S(1)}, u32[]{:S(2)}, u32[]{:S(2)}) collective-permute-start(bf16[784,128]{1,0:T(8,128)(2,1)S(1)} %get-tuple-element.77), channel_id=1, source_target_pairs={{0,4},{4,0},{8,12},{12,8},{16,20},{20,16},{24,28},{28,24},{1,5},{5... | collective-permute-start | bytes 602120 | tf_op jit(solution)/shard_map/ppermute | solution.py:16
  11.1 1.6 %collective-permute-start.8 = (bf16[784,128]{1,0:T(8,128)(2,1)S(1)}, bf16[784,128]{1,0:T(8,128)(2,1)S(1)}, u32[]{:S(2)}, u32[]{:S(2)}) collective-permute-start(bf16[784,128]{1,0:T(8,128)(2,1)S(1)} %get-tuple-element.78), channel_id=1, source_target_pairs={{0,8},{4,12},{8,0},{12,4},{16,24},{20,28},{24,16},{28,20},{1,9},{5... | collective-permute-start | bytes 602120 | tf_op jit(solution)/shard_map/ppermute | solution.py:16
  12.7 0.1 collective-permute-start.9
  12.8 2.3 %shard_map.86 = (bf16[2048,1024]{1,0:T(8,128)(2,1)S(1)}, bf16[192,1024]{1,0:T(8,128)(2,1)S(1)}) custom-call(bf16[2048,1024]{1,0:T(8,128)(2,1)} %bitcast.8, bf16[192,1024]{1,0:T(8,128)(2,1)} %bitcast.12), custom_call_target="tpu_custom_call" | custom-call | bytes 9175040 | tf_op jit(solution)/shard_map/pallas_call | solution.py:270
  15.1 1.6 %shard_map.87 = (f32[192,512]{1,0:T(8,128)S(1)}, bf16[192,512]{1,0:T(8,128)(2,1)S(1)}, bf16[192,512]{1,0:T(8,128)(2,1)S(1)}, bf16[192,512]{1,0:T(8,128)(2,1)S(1)}, bf16[192,1024]{1,0:T(8,128)(2,1)S(1)}) custom-call(bf16[192,1024]{1,0:T(8,128)(2,1)S(1)} %get-tuple-element.69.cot, bf16[192,1024]{1,0:T(8,128)(2,1)S(1)} %collective-permute-done.3.sent, ...), custom_call_target="tpu_custom_call" | custom-call | flops 805306368 | bytes 4980736 | tf_op jit(solution)/shard_map/pallas_call | solution.py:196
  16.7 1.9 %collective-permute-start.4 = (bf16[192,512]{1,0:T(8,128)(2,1)S(1)}, bf16[192,512]{1,0:T(8,128)(2,1)S(1)}, u32[]{:S(2)}, u32[]{:S(2)}) collective-permute-start(bf16[192,512]{1,0:T(8,128)(2,1)S(1)} %get-tuple-element.72), channel_id=1, source_target_pairs={{0,4},{4,0},{8,12},{12,8},{16,20},{20,16},{24,28},{28,24},{1,5},{5... | collective-permute-start | bytes 589832 | tf_op jit(solution)/shard_map/ppermute | solution.py:16
  18.5 1.6 %collective-permute-start.5 = (bf16[192,512]{1,0:T(8,128)(2,1)S(1)}, bf16[192,512]{1,0:T(8,128)(2,1)S(1)}, u32[]{:S(2)}, u32[]{:S(2)}) collective-permute-start(bf16[192,512]{1,0:T(8,128)(2,1)S(1)} %get-tuple-element.73), channel_id=1, source_target_pairs={{0,8},{4,12},{8,0},{12,4},{16,24},{20,28},{24,16},{28,20},{1,9},{5... | collective-permute-start | bytes 589832 | tf_op jit(solution)/shard_map/ppermute | solution.py:16
  20.1 0.1 collective-permute-start.6
  20.2 2.8 %collective-permute-done.9.g3 = bf16[784,128]{1,0:T(8,128)(2,1)S(1)} collective-permute-done((bf16[784,128]{1,0:T(8,128)(2,1)S(1)}, bf16[784,128]{1,0:T(8,128)(2,1)S(1)}, u32[]{:S(2)}, u32[]{:S(2)}) %collective-permute-start.9) | collective-permute-done | bytes 200736 | tf_op jit(solution)/shard_map/ppermute | solution.py:16
  23.0 0.5 shard_map.88
  23.5 3.6 %collective-permute-done.4.g1 = bf16[192,512]{1,0:T(8,128)(2,1)S(1)} collective-permute-done((bf16[192,512]{1,0:T(8,128)(2,1)S(1)}, bf16[192,512]{1,0:T(8,128)(2,1)S(1)}, u32[]{:S(2)}, u32[]{:S(2)}) %collective-permute-start.4) | collective-permute-done | bytes 196640 | tf_op jit(solution)/shard_map/ppermute | solution.py:16
  27.1 0.4 collective-permute-done.5.g2
  27.5 2.9 %collective-permute-done.6.g3 = bf16[192,512]{1,0:T(8,128)(2,1)S(1)} collective-permute-done((bf16[192,512]{1,0:T(8,128)(2,1)S(1)}, bf16[192,512]{1,0:T(8,128)(2,1)S(1)}, u32[]{:S(2)}, u32[]{:S(2)}) %collective-permute-start.6) | collective-permute-done | bytes 196640 | tf_op jit(solution)/shard_map/ppermute | solution.py:16
  30.4 0.2 shard_map.89.refs_0_.p0
  30.7 2.7 %collective-permute-start.12 = (bf16[784,128]{1,0:T(8,128)(2,1)S(1)}, bf16[784,128]{1,0:T(8,128)(2,1)S(1)}, u32[]{:S(2)}, u32[]{:S(2)}) collective-permute-start(bf16[784,128]{1,0:T(8,128)(2,1)S(1)} %shard_map.89.refs_0_.p0), channel_id=1, source_target_pairs={{0,12},{4,8},{8,4},{12,0},{16,28},{20,24},{24,20},{28,16},{1,13},{... | collective-permute-start | bytes 602120 | tf_op jit(solution)/shard_map/ppermute | solution.py:16
  33.4 0.4 collective-permute-start.11
  33.9 0.4 collective-permute-start.10
  34.2 0.5 shard_map.90.refs_3_
  34.7 4.8 %collective-permute-done.12.refs_0_.p3 = bf16[784,128]{1,0:T(8,128)(2,1)S(1)} collective-permute-done((bf16[784,128]{1,0:T(8,128)(2,1)S(1)}, bf16[784,128]{1,0:T(8,128)(2,1)S(1)}, u32[]{:S(2)}, u32[]{:S(2)}) %collective-permute-start.12) | collective-permute-done | bytes 200736 | tf_op jit(solution)/shard_map/ppermute | solution.py:16
  39.5 2.5 %collective-permute-done.11.refs_1_.p2 = bf16[784,128]{1,0:T(8,128)(2,1)S(1)} collective-permute-done((bf16[784,128]{1,0:T(8,128)(2,1)S(1)}, bf16[784,128]{1,0:T(8,128)(2,1)S(1)}, u32[]{:S(2)}, u32[]{:S(2)}) %collective-permute-start.11) | collective-permute-done | bytes 200736 | tf_op jit(solution)/shard_map/ppermute | solution.py:16
  42.0 0.8 shard_map.91.earlier
  42.9 0.5 shard_map.92
  43.5 1.5 %collective-permute-done.13.got = bf16[208,512]{1,0:T(8,128)(2,1)S(1)} collective-permute-done((bf16[208,512]{1,0:T(8,128)(2,1)S(1)}, bf16[208,512]{1,0:T(8,128)(2,1)S(1)}, u32[]{:S(2)}, u32[]{:S(2)}) %collective-permute-start.13) | collective-permute-done | bytes 213024 | tf_op jit(solution)/shard_map/ppermute | solution.py:16
  45.0 1.6 %collective-permute-start.14 = (bf16[208,256]{1,0:T(8,128)(2,1)S(1)}, bf16[208,256]{1,0:T(8,128)(2,1)S(1)}, u32[]{:S(2)}, u32[]{:S(2)}) collective-permute-start(bf16[208,256]{1,0:T(8,128)(2,1)S(1)} %get-tuple-element.87), channel_id=1, source_target_pairs={{0,2},{1,3},{2,0},{3,1},{4,6},{5,7},{6,4},{7,5},{8,10},{9,11},{10,... | collective-permute-start | bytes 319496 | tf_op jit(solution)/shard_map/ppermute | solution.py:16
  46.6 3.5 %collective-permute-done.14.got = bf16[208,256]{1,0:T(8,128)(2,1)S(1)} collective-permute-done((bf16[208,256]{1,0:T(8,128)(2,1)S(1)}, bf16[208,256]{1,0:T(8,128)(2,1)S(1)}, u32[]{:S(2)}, u32[]{:S(2)}) %collective-permute-start.14) | collective-permute-done | bytes 106528 | tf_op jit(solution)/shard_map/ppermute | solution.py:16
  50.1 0.2 shard_map.94
  50.3 1.3 %collective-permute-start.15 = (bf16[192,256]{1,0:T(8,128)(2,1)S(1)}, bf16[192,256]{1,0:T(8,128)(2,1)S(1)}, u32[]{:S(2)}, u32[]{:S(2)}) collective-permute-start(bf16[192,256]{1,0:T(8,128)(2,1)S(1)} %shard_map.94), channel_id=1, source_target_pairs={{16,0},{20,4},{24,8},{28,12},{17,1},{21,5},{25,9},{29,13},{18,2},{... | collective-permute-start | bytes 294920 | tf_op jit(solution)/shard_map/ppermute | solution.py:659
  51.6 1.7 %collective-permute-start.21 = (bf16[192,512]{1,0:T(8,128)(2,1)S(1)}, bf16[192,512]{1,0:T(8,128)(2,1)S(1)}, u32[]{:S(2)}, u32[]{:S(2)}) collective-permute-start(bf16[192,512]{1,0:T(8,128)(2,1)S(1)} %get-tuple-element.93.h0), channel_id=1, source_target_pairs={{0,12},{4,8},{8,4},{12,0},{16,28},{20,24},{24,20},{28,16},{1,13},{... | collective-permute-start | bytes 589832 | tf_op jit(solution)/shard_map/ppermute | solution.py:16
  53.2 0.4 collective-permute-start.20
  53.7 1.5 %collective-permute-start.19 = (bf16[192,512]{1,0:T(8,128)(2,1)S(1)}, bf16[192,512]{1,0:T(8,128)(2,1)S(1)}, u32[]{:S(2)}, u32[]{:S(2)}) collective-permute-start(bf16[192,512]{1,0:T(8,128)(2,1)S(1)} %get-tuple-element.93.h0), channel_id=1, source_target_pairs={{0,4},{4,0},{8,12},{12,8},{16,20},{20,16},{24,28},{28,24},{1,5},{5... | collective-permute-start | bytes 589832 | tf_op jit(solution)/shard_map/ppermute | solution.py:16
  55.1 5.6 %collective-permute-done.15.refs_0_.refs_4_ = bf16[192,256]{1,0:T(8,128)(2,1)S(1)} collective-permute-done((bf16[192,256]{1,0:T(8,128)(2,1)S(1)}, bf16[192,256]{1,0:T(8,128)(2,1)S(1)}, u32[]{:S(2)}, u32[]{:S(2)}) %collective-permute-start.15) | collective-permute-done | bytes 98336 | tf_op jit(solution)/shard_map/ppermute | solution.py:659
  60.8 1.2 %collective-permute-start.16 = (bf16[192,256]{1,0:T(8,128)(2,1)S(1)}, bf16[192,256]{1,0:T(8,128)(2,1)S(1)}, u32[]{:S(2)}, u32[]{:S(2)}) collective-permute-start(bf16[192,256]{1,0:T(8,128)(2,1)S(1)} %collective-permute-done.15.refs_0_.refs_4_), channel_id=1, source_target_pairs={{0,2},{1,3},{2,0},{3,1},{4,6},{5,7},{6,4},{7,5},{8,10},{9,11},{10,... | collective-permute-start | bytes 294920 | tf_op jit(solution)/shard_map/ppermute | solution.py:16
  62.0 3.4 %collective-permute-done.16.refs_1_.refs_6_ = bf16[192,256]{1,0:T(8,128)(2,1)S(1)} collective-permute-done((bf16[192,256]{1,0:T(8,128)(2,1)S(1)}, bf16[192,256]{1,0:T(8,128)(2,1)S(1)}, u32[]{:S(2)}, u32[]{:S(2)}) %collective-permute-start.16) | collective-permute-done | bytes 98336 | tf_op jit(solution)/shard_map/ppermute | solution.py:16
  65.4 0.5 shard_map.95.refs_4_
  66.0 0.9 shard_map.96.refs_3_
  66.8 0.7 shard_map.97
  67.6 0.5 collective-permute-start.22
  68.1 3.1 %collective-permute-start.24 = (bf16[192,512]{1,0:T(8,128)(2,1)S(1)}, bf16[192,512]{1,0:T(8,128)(2,1)S(1)}, u32[]{:S(2)}, u32[]{:S(2)}) collective-permute-start(bf16[192,512]{1,0:T(8,128)(2,1)S(1)} %get-tuple-element.101), channel_id=1, source_target_pairs={{0,12},{4,8},{8,4},{12,0},{16,28},{20,24},{24,20},{28,16},{1,13},{... | collective-permute-start | bytes 589832 | tf_op jit(solution)/shard_map/ppermute | solution.py:16
  71.2 2.5 %shard_map.98 = bf16[2048,1024]{1,0:T(8,128)(2,1)} custom-call(bf16[192,512]{1,0:T(8,128)(2,1)S(1)} %get-tuple-element.93.h0, bf16[192,512]{1,0:T(8,128)(2,1)S(1)} %collective-permute-done.19.h1, bf16[192,512]{1,0:T(8,128)(2,1)S(1)} %collective-permute-done.20.h2, bf16[192,512]{1,0:T(8,128)(2,1)S(1)} %collective-permute-done.21.h3, ...), custom_call_target="tpu_custom_call" | custom-call | flops 805306368 | bytes 4194304 | tf_op jit(solution)/shard_map/pallas_call | solution.py:543
  73.7 1.3 %collective-permute-done.22.g1 = bf16[192,512]{1,0:T(8,128)(2,1)S(1)} collective-permute-done((bf16[192,512]{1,0:T(8,128)(2,1)S(1)}, bf16[192,512]{1,0:T(8,128)(2,1)S(1)}, u32[]{:S(2)}, u32[]{:S(2)}) %collective-permute-start.22) | collective-permute-done | bytes 196640 | tf_op jit(solution)/shard_map/ppermute | solution.py:16
  75.0 0.8 collective-permute-done.23.g2
  75.8 4.6 %collective-permute-done.24.g3 = bf16[192,512]{1,0:T(8,128)(2,1)S(1)} collective-permute-done((bf16[192,512]{1,0:T(8,128)(2,1)S(1)}, bf16[192,512]{1,0:T(8,128)(2,1)S(1)}, u32[]{:S(2)}, u32[]{:S(2)}) %collective-permute-start.24) | collective-permute-done | bytes 196640 | tf_op jit(solution)/shard_map/ppermute | solution.py:16
  80.4 0.2 shard_map.99.refs_0_.p0
  80.6 0.2 collective-permute-start.27
  80.8 1.7 %collective-permute-start.26 = (bf16[784,128]{1,0:T(8,128)(2,1)S(1)}, bf16[784,128]{1,0:T(8,128)(2,1)S(1)}, u32[]{:S(2)}, u32[]{:S(2)}) collective-permute-start(bf16[784,128]{1,0:T(8,128)(2,1)S(1)} %shard_map.99.refs_0_.p0), channel_id=1, source_target_pairs={{0,8},{4,12},{8,0},{12,4},{16,24},{20,28},{24,16},{28,20},{1,9},{5... | collective-permute-start | bytes 602120 | tf_op jit(solution)/shard_map/ppermute | solution.py:16
  82.5 1.6 %collective-permute-start.25 = (bf16[784,128]{1,0:T(8,128)(2,1)S(1)}, bf16[784,128]{1,0:T(8,128)(2,1)S(1)}, u32[]{:S(2)}, u32[]{:S(2)}) collective-permute-start(bf16[784,128]{1,0:T(8,128)(2,1)S(1)} %shard_map.99.refs_0_.p0), channel_id=1, source_target_pairs={{0,4},{4,0},{8,12},{12,8},{16,20},{20,16},{24,28},{28,24},{1,5},{5... | collective-permute-start | bytes 602120 | tf_op jit(solution)/shard_map/ppermute | solution.py:16
  84.1 0.5 shard_map.100.refs_3_
  84.7 4.9 %collective-permute-done.27.refs_0_.p3 = bf16[784,128]{1,0:T(8,128)(2,1)S(1)} collective-permute-done((bf16[784,128]{1,0:T(8,128)(2,1)S(1)}, bf16[784,128]{1,0:T(8,128)(2,1)S(1)}, u32[]{:S(2)}, u32[]{:S(2)}) %collective-permute-start.27) | collective-permute-done | bytes 200736 | tf_op jit(solution)/shard_map/ppermute | solution.py:16
  89.5 1.6 %collective-permute-done.26.refs_1_.p2 = bf16[784,128]{1,0:T(8,128)(2,1)S(1)} collective-permute-done((bf16[784,128]{1,0:T(8,128)(2,1)S(1)}, bf16[784,128]{1,0:T(8,128)(2,1)S(1)}, u32[]{:S(2)}, u32[]{:S(2)}) %collective-permute-start.26) | collective-permute-done | bytes 200736 | tf_op jit(solution)/shard_map/ppermute | solution.py:16
  91.1 0.8 shard_map.101.earlier
  91.9 0.2 collective-permute-done.25.p1
  92.1 0.5 shard_map.102
  92.7 1.5 %collective-permute-done.28.got = bf16[208,512]{1,0:T(8,128)(2,1)S(1)} collective-permute-done((bf16[208,512]{1,0:T(8,128)(2,1)S(1)}, bf16[208,512]{1,0:T(8,128)(2,1)S(1)}, u32[]{:S(2)}, u32[]{:S(2)}) %collective-permute-start.28) | collective-permute-done | bytes 213024 | tf_op jit(solution)/shard_map/ppermute | solution.py:16
  94.2 1.3 %collective-permute-start.29 = (bf16[208,256]{1,0:T(8,128)(2,1)S(1)}, bf16[208,256]{1,0:T(8,128)(2,1)S(1)}, u32[]{:S(2)}, u32[]{:S(2)}) collective-permute-start(bf16[208,256]{1,0:T(8,128)(2,1)S(1)} %get-tuple-element.104), channel_id=1, source_target_pairs={{0,2},{1,3},{2,0},{3,1},{4,6},{5,7},{6,4},{7,5},{8,10},{9,11},{10,... | collective-permute-start | bytes 319496 | tf_op jit(solution)/shard_map/ppermute | solution.py:16
  95.6 2.6 %shard_map.104 = bf16[1024,2048]{1,0:T(8,128)(2,1)} custom-call(bf16[784,128]{1,0:T(8,128)(2,1)S(1)} %shard_map.99.refs_0_.p0, bf16[784,128]{1,0:T(8,128)(2,1)S(1)} %collective-permute-done.25.p1, bf16[784,128]{1,0:T(8,128)(2,1)S(1)} %collective-permute-done.26.refs_1_.p2, bf16[784,128]{1,0:T(8,128)(2,1)S(1)} %collective-permute-done.27.refs_0_.p3, ...), custom_call_target="tpu_custom_call" | custom-call | flops 805306368 | bytes 4194304 | tf_op jit(solution)/shard_map/pallas_call | solution.py:543
  98.2 1.1 %collective-permute-done.29.got = bf16[208,256]{1,0:T(8,128)(2,1)S(1)} collective-permute-done((bf16[208,256]{1,0:T(8,128)(2,1)S(1)}, bf16[208,256]{1,0:T(8,128)(2,1)S(1)}, u32[]{:S(2)}, u32[]{:S(2)}) %collective-permute-start.29) | collective-permute-done | bytes 106528 | tf_op jit(solution)/shard_map/ppermute | solution.py:16
  99.3 0.8 shard_map.105
  (18 shorter events, 0.3 us)
Async XLA Ops:
  0.6 3.8 %collective-permute-start = (bf16[192,256]{1,0:T(8,128)(2,1)}, bf16[192,256]{1,0:T(8,128)(2,1)S(1)}, u32[]{:S(2)}, u32[]{:S(2)}) collective-permute-start(bf16[192,256]{1,0:T(8,128)(2,1)} %bitcast.13), channel_id=1, source_target_pairs={{0,1},{1,0},{2,3},{3,2},{4,5},{5,4},{6,7},{7,6},{8,9},{9,8},{10,11... | collective-permute-start | bytes 294920 | tf_op jit(solution)/shard_map/ppermute | solution.py:16
  1.1 6.2 %collective-permute-start.1 = (bf16[192,256]{1,0:T(8,128)(2,1)}, bf16[192,256]{1,0:T(8,128)(2,1)S(1)}, u32[]{:S(2)}, u32[]{:S(2)}) collective-permute-start(bf16[192,256]{1,0:T(8,128)(2,1)} %bitcast.14), channel_id=1, source_target_pairs={{0,2},{1,3},{2,0},{3,1},{4,6},{5,7},{6,4},{7,5},{8,10},{9,11},{10,... | collective-permute-start | bytes 294920 | tf_op jit(solution)/shard_map/ppermute | solution.py:16
  3.7 11.4 %collective-permute-start.3 = (bf16[192,1024]{1,0:T(8,128)(2,1)}, bf16[192,1024]{1,0:T(8,128)(2,1)S(1)}, u32[]{:S(2)}, u32[]{:S(2)}) collective-permute-start(bf16[192,1024]{1,0:T(8,128)(2,1)} %bitcast.11), channel_id=1, source_target_pairs={{20,17},{16,18},{24,19},{17,20},{29,22},{21,23},{26,24},{18,25},{3... | collective-permute-start | bytes 1179656 | tf_op jit(solution)/shard_map/ppermute | solution.py:575
  7.3 1.3 %collective-permute-start.2 = (bf16[192,256]{1,0:T(8,128)(2,1)S(1)}, bf16[192,256]{1,0:T(8,128)(2,1)S(1)}, u32[]{:S(2)}, u32[]{:S(2)}) collective-permute-start(bf16[192,256]{1,0:T(8,128)(2,1)S(1)} %collective-permute-done.1.x2), channel_id=1, source_target_pairs={{0,1},{1,0},{2,3},{3,2},{4,5},{5,4},{6,7},{7,6},{8,9},{9,8},{10,11... | collective-permute-start | bytes 294920 | tf_op jit(solution)/shard_map/ppermute | solution.py:16
  9.2 10.8 %collective-permute-start.7 = (bf16[784,128]{1,0:T(8,128)(2,1)S(1)}, bf16[784,128]{1,0:T(8,128)(2,1)S(1)}, u32[]{:S(2)}, u32[]{:S(2)}) collective-permute-start(bf16[784,128]{1,0:T(8,128)(2,1)S(1)} %get-tuple-element.77), channel_id=1, source_target_pairs={{0,4},{4,0},{8,12},{12,8},{16,20},{20,16},{24,28},{28,24},{1,5},{5... | collective-permute-start | bytes 602120 | tf_op jit(solution)/shard_map/ppermute | solution.py:16
  11.1 9.1 %collective-permute-start.8 = (bf16[784,128]{1,0:T(8,128)(2,1)S(1)}, bf16[784,128]{1,0:T(8,128)(2,1)S(1)}, u32[]{:S(2)}, u32[]{:S(2)}) collective-permute-start(bf16[784,128]{1,0:T(8,128)(2,1)S(1)} %get-tuple-element.78), channel_id=1, source_target_pairs={{0,8},{4,12},{8,0},{12,4},{16,24},{20,28},{24,16},{28,20},{1,9},{5... | collective-permute-start | bytes 602120 | tf_op jit(solution)/shard_map/ppermute | solution.py:16
  12.7 10.3 %collective-permute-start.9 = (bf16[784,128]{1,0:T(8,128)(2,1)S(1)}, bf16[784,128]{1,0:T(8,128)(2,1)S(1)}, u32[]{:S(2)}, u32[]{:S(2)}) collective-permute-start(bf16[784,128]{1,0:T(8,128)(2,1)S(1)} %get-tuple-element.79), channel_id=1, source_target_pairs={{0,12},{4,8},{8,4},{12,0},{16,28},{20,24},{24,20},{28,16},{1,13},{... | collective-permute-start | bytes 602120 | tf_op jit(solution)/shard_map/ppermute | solution.py:16
  16.7 10.4 %collective-permute-start.4 = (bf16[192,512]{1,0:T(8,128)(2,1)S(1)}, bf16[192,512]{1,0:T(8,128)(2,1)S(1)}, u32[]{:S(2)}, u32[]{:S(2)}) collective-permute-start(bf16[192,512]{1,0:T(8,128)(2,1)S(1)} %get-tuple-element.72), channel_id=1, source_target_pairs={{0,4},{4,0},{8,12},{12,8},{16,20},{20,16},{24,28},{28,24},{1,5},{5... | collective-permute-start | bytes 589832 | tf_op jit(solution)/shard_map/ppermute | solution.py:16
  18.5 9.0 %collective-permute-start.5 = (bf16[192,512]{1,0:T(8,128)(2,1)S(1)}, bf16[192,512]{1,0:T(8,128)(2,1)S(1)}, u32[]{:S(2)}, u32[]{:S(2)}) collective-permute-start(bf16[192,512]{1,0:T(8,128)(2,1)S(1)} %get-tuple-element.73), channel_id=1, source_target_pairs={{0,8},{4,12},{8,0},{12,4},{16,24},{20,28},{24,16},{28,20},{1,9},{5... | collective-permute-start | bytes 589832 | tf_op jit(solution)/shard_map/ppermute | solution.py:16
  20.1 10.3 %collective-permute-start.6 = (bf16[192,512]{1,0:T(8,128)(2,1)S(1)}, bf16[192,512]{1,0:T(8,128)(2,1)S(1)}, u32[]{:S(2)}, u32[]{:S(2)}) collective-permute-start(bf16[192,512]{1,0:T(8,128)(2,1)S(1)} %get-tuple-element.74), channel_id=1, source_target_pairs={{0,12},{4,8},{8,4},{12,0},{16,28},{20,24},{24,20},{28,16},{1,13},{... | collective-permute-start | bytes 589832 | tf_op jit(solution)/shard_map/ppermute | solution.py:16
  30.7 8.9 %collective-permute-start.12 = (bf16[784,128]{1,0:T(8,128)(2,1)S(1)}, bf16[784,128]{1,0:T(8,128)(2,1)S(1)}, u32[]{:S(2)}, u32[]{:S(2)}) collective-permute-start(bf16[784,128]{1,0:T(8,128)(2,1)S(1)} %shard_map.89.refs_0_.p0), channel_id=1, source_target_pairs={{0,12},{4,8},{8,4},{12,0},{16,28},{20,24},{24,20},{28,16},{1,13},{... | collective-permute-start | bytes 602120 | tf_op jit(solution)/shard_map/ppermute | solution.py:16
  33.4 8.6 %collective-permute-start.11 = (bf16[784,128]{1,0:T(8,128)(2,1)S(1)}, bf16[784,128]{1,0:T(8,128)(2,1)S(1)}, u32[]{:S(2)}, u32[]{:S(2)}) collective-permute-start(bf16[784,128]{1,0:T(8,128)(2,1)S(1)} %shard_map.89.refs_0_.p0), channel_id=1, source_target_pairs={{0,8},{4,12},{8,0},{12,4},{16,24},{20,28},{24,16},{28,20},{1,9},{5... | collective-permute-start | bytes 602120 | tf_op jit(solution)/shard_map/ppermute | solution.py:16
  33.9 9.0 %collective-permute-start.10 = (bf16[784,128]{1,0:T(8,128)(2,1)S(1)}, bf16[784,128]{1,0:T(8,128)(2,1)S(1)}, u32[]{:S(2)}, u32[]{:S(2)}) collective-permute-start(bf16[784,128]{1,0:T(8,128)(2,1)S(1)} %shard_map.89.refs_0_.p0), channel_id=1, source_target_pairs={{0,4},{4,0},{8,12},{12,8},{16,20},{20,16},{24,28},{28,24},{1,5},{5... | collective-permute-start | bytes 602120 | tf_op jit(solution)/shard_map/ppermute | solution.py:16
  43.4 1.5 %collective-permute-start.13 = (bf16[208,512]{1,0:T(8,128)(2,1)S(1)}, bf16[208,512]{1,0:T(8,128)(2,1)S(1)}, u32[]{:S(2)}, u32[]{:S(2)}) collective-permute-start(bf16[208,512]{1,0:T(8,128)(2,1)S(1)} %get-tuple-element.83), channel_id=1, source_target_pairs={{0,1},{1,0},{2,3},{3,2},{4,5},{5,4},{6,7},{7,6},{8,9},{9,8},{10,11... | collective-permute-start | bytes 638984 | tf_op jit(solution)/shard_map/ppermute | solution.py:16
  45.0 5.1 %collective-permute-start.14 = (bf16[208,256]{1,0:T(8,128)(2,1)S(1)}, bf16[208,256]{1,0:T(8,128)(2,1)S(1)}, u32[]{:S(2)}, u32[]{:S(2)}) collective-permute-start(bf16[208,256]{1,0:T(8,128)(2,1)S(1)} %get-tuple-element.87), channel_id=1, source_target_pairs={{0,2},{1,3},{2,0},{3,1},{4,6},{5,7},{6,4},{7,5},{8,10},{9,11},{10,... | collective-permute-start | bytes 319496 | tf_op jit(solution)/shard_map/ppermute | solution.py:16
  50.3 10.5 %collective-permute-start.15 = (bf16[192,256]{1,0:T(8,128)(2,1)S(1)}, bf16[192,256]{1,0:T(8,128)(2,1)S(1)}, u32[]{:S(2)}, u32[]{:S(2)}) collective-permute-start(bf16[192,256]{1,0:T(8,128)(2,1)S(1)} %shard_map.94), channel_id=1, source_target_pairs={{16,0},{20,4},{24,8},{28,12},{17,1},{21,5},{25,9},{29,13},{18,2},{... | collective-permute-start | bytes 294920 | tf_op jit(solution)/shard_map/ppermute | solution.py:659
  51.6 13.8 %collective-permute-start.21 = (bf16[192,512]{1,0:T(8,128)(2,1)S(1)}, bf16[192,512]{1,0:T(8,128)(2,1)S(1)}, u32[]{:S(2)}, u32[]{:S(2)}) collective-permute-start(bf16[192,512]{1,0:T(8,128)(2,1)S(1)} %get-tuple-element.93.h0), channel_id=1, source_target_pairs={{0,12},{4,8},{8,4},{12,0},{16,28},{20,24},{24,20},{28,16},{1,13},{... | collective-permute-start | bytes 589832 | tf_op jit(solution)/shard_map/ppermute | solution.py:16
  53.2 12.2 %collective-permute-start.20 = (bf16[192,512]{1,0:T(8,128)(2,1)S(1)}, bf16[192,512]{1,0:T(8,128)(2,1)S(1)}, u32[]{:S(2)}, u32[]{:S(2)}) collective-permute-start(bf16[192,512]{1,0:T(8,128)(2,1)S(1)} %get-tuple-element.93.h0), channel_id=1, source_target_pairs={{0,8},{4,12},{8,0},{12,4},{16,24},{20,28},{24,16},{28,20},{1,9},{5... | collective-permute-start | bytes 589832 | tf_op jit(solution)/shard_map/ppermute | solution.py:16
  53.7 11.8 %collective-permute-start.19 = (bf16[192,512]{1,0:T(8,128)(2,1)S(1)}, bf16[192,512]{1,0:T(8,128)(2,1)S(1)}, u32[]{:S(2)}, u32[]{:S(2)}) collective-permute-start(bf16[192,512]{1,0:T(8,128)(2,1)S(1)} %get-tuple-element.93.h0), channel_id=1, source_target_pairs={{0,4},{4,0},{8,12},{12,8},{16,20},{20,16},{24,28},{28,24},{1,5},{5... | collective-permute-start | bytes 589832 | tf_op jit(solution)/shard_map/ppermute | solution.py:16
  60.8 4.6 %collective-permute-start.16 = (bf16[192,256]{1,0:T(8,128)(2,1)S(1)}, bf16[192,256]{1,0:T(8,128)(2,1)S(1)}, u32[]{:S(2)}, u32[]{:S(2)}) collective-permute-start(bf16[192,256]{1,0:T(8,128)(2,1)S(1)} %collective-permute-done.15.refs_0_.refs_4_), channel_id=1, source_target_pairs={{0,2},{1,3},{2,0},{3,1},{4,6},{5,7},{6,4},{7,5},{8,10},{9,11},{10,... | collective-permute-start | bytes 294920 | tf_op jit(solution)/shard_map/ppermute | solution.py:16
  62.0 4.0 %collective-permute-start.18 = (bf16[192,256]{1,0:T(8,128)(2,1)S(1)}, bf16[192,256]{1,0:T(8,128)(2,1)S(1)}, u32[]{:S(2)}, u32[]{:S(2)}) collective-permute-start(bf16[192,256]{1,0:T(8,128)(2,1)S(1)} %collective-permute-done.15.refs_0_.refs_4_), channel_id=1, source_target_pairs={{0,1},{1,0},{2,3},{3,2},{4,5},{5,4},{6,7},{7,6},{8,9},{9,8},{10,11... | collective-permute-start | bytes 294920 | tf_op jit(solution)/shard_map/ppermute | solution.py:16
  65.4 1.4 %collective-permute-start.17 = (bf16[192,256]{1,0:T(8,128)(2,1)S(1)}, bf16[192,256]{1,0:T(8,128)(2,1)S(1)}, u32[]{:S(2)}, u32[]{:S(2)}) collective-permute-start(bf16[192,256]{1,0:T(8,128)(2,1)S(1)} %collective-permute-done.16.refs_1_.refs_6_), channel_id=1, source_target_pairs={{0,1},{1,0},{2,3},{3,2},{4,5},{5,4},{6,7},{7,6},{8,9},{9,8},{10,11... | collective-permute-start | bytes 294920 | tf_op jit(solution)/shard_map/ppermute | solution.py:16
  67.6 7.4 %collective-permute-start.22 = (bf16[192,512]{1,0:T(8,128)(2,1)S(1)}, bf16[192,512]{1,0:T(8,128)(2,1)S(1)}, u32[]{:S(2)}, u32[]{:S(2)}) collective-permute-start(bf16[192,512]{1,0:T(8,128)(2,1)S(1)} %get-tuple-element.99), channel_id=1, source_target_pairs={{0,4},{4,0},{8,12},{12,8},{16,20},{20,16},{24,28},{28,24},{1,5},{5... | collective-permute-start | bytes 589832 | tf_op jit(solution)/shard_map/ppermute | solution.py:16
  68.1 7.7 %collective-permute-start.23 = (bf16[192,512]{1,0:T(8,128)(2,1)S(1)}, bf16[192,512]{1,0:T(8,128)(2,1)S(1)}, u32[]{:S(2)}, u32[]{:S(2)}) collective-permute-start(bf16[192,512]{1,0:T(8,128)(2,1)S(1)} %get-tuple-element.100), channel_id=1, source_target_pairs={{0,8},{4,12},{8,0},{12,4},{16,24},{20,28},{24,16},{28,20},{1,9},{5... | collective-permute-start | bytes 589832 | tf_op jit(solution)/shard_map/ppermute | solution.py:16
  68.1 12.3 %collective-permute-start.24 = (bf16[192,512]{1,0:T(8,128)(2,1)S(1)}, bf16[192,512]{1,0:T(8,128)(2,1)S(1)}, u32[]{:S(2)}, u32[]{:S(2)}) collective-permute-start(bf16[192,512]{1,0:T(8,128)(2,1)S(1)} %get-tuple-element.101), channel_id=1, source_target_pairs={{0,12},{4,8},{8,4},{12,0},{16,28},{20,24},{24,20},{28,16},{1,13},{... | collective-permute-start | bytes 589832 | tf_op jit(solution)/shard_map/ppermute | solution.py:16
  80.6 8.9 %collective-permute-start.27 = (bf16[784,128]{1,0:T(8,128)(2,1)S(1)}, bf16[784,128]{1,0:T(8,128)(2,1)S(1)}, u32[]{:S(2)}, u32[]{:S(2)}) collective-permute-start(bf16[784,128]{1,0:T(8,128)(2,1)S(1)} %shard_map.99.refs_0_.p0), channel_id=1, source_target_pairs={{0,12},{4,8},{8,4},{12,0},{16,28},{20,24},{24,20},{28,16},{1,13},{... | collective-permute-start | bytes 602120 | tf_op jit(solution)/shard_map/ppermute | solution.py:16
  80.8 10.3 %collective-permute-start.26 = (bf16[784,128]{1,0:T(8,128)(2,1)S(1)}, bf16[784,128]{1,0:T(8,128)(2,1)S(1)}, u32[]{:S(2)}, u32[]{:S(2)}) collective-permute-start(bf16[784,128]{1,0:T(8,128)(2,1)S(1)} %shard_map.99.refs_0_.p0), channel_id=1, source_target_pairs={{0,8},{4,12},{8,0},{12,4},{16,24},{20,28},{24,16},{28,20},{1,9},{5... | collective-permute-start | bytes 602120 | tf_op jit(solution)/shard_map/ppermute | solution.py:16
  82.5 9.6 %collective-permute-start.25 = (bf16[784,128]{1,0:T(8,128)(2,1)S(1)}, bf16[784,128]{1,0:T(8,128)(2,1)S(1)}, u32[]{:S(2)}, u32[]{:S(2)}) collective-permute-start(bf16[784,128]{1,0:T(8,128)(2,1)S(1)} %shard_map.99.refs_0_.p0), channel_id=1, source_target_pairs={{0,4},{4,0},{8,12},{12,8},{16,20},{20,16},{24,28},{28,24},{1,5},{5... | collective-permute-start | bytes 602120 | tf_op jit(solution)/shard_map/ppermute | solution.py:16
  92.7 1.5 %collective-permute-start.28 = (bf16[208,512]{1,0:T(8,128)(2,1)S(1)}, bf16[208,512]{1,0:T(8,128)(2,1)S(1)}, u32[]{:S(2)}, u32[]{:S(2)}) collective-permute-start(bf16[208,512]{1,0:T(8,128)(2,1)S(1)} %get-tuple-element.103), channel_id=1, source_target_pairs={{0,1},{1,0},{2,3},{3,2},{4,5},{5,4},{6,7},{7,6},{8,9},{9,8},{10,11... | collective-permute-start | bytes 638984 | tf_op jit(solution)/shard_map/ppermute | solution.py:16
  94.2 5.1 %collective-permute-start.29 = (bf16[208,256]{1,0:T(8,128)(2,1)S(1)}, bf16[208,256]{1,0:T(8,128)(2,1)S(1)}, u32[]{:S(2)}, u32[]{:S(2)}) collective-permute-start(bf16[208,256]{1,0:T(8,128)(2,1)S(1)} %get-tuple-element.104), channel_id=1, source_target_pairs={{0,2},{1,3},{2,0},{3,1},{4,6},{5,7},{6,4},{7,5},{8,10},{9,11},{10,... | collective-permute-start | bytes 319496 | tf_op jit(solution)/shard_map/ppermute | solution.py:16
